TPU v7x, 32 devices: a whole 2x2x4 slice. The times are simulated.
32 devices in a mesh: atoms: 16 (over z, x, core), beads: 2 (over y).
Axes of the slice: x: 2, y: 2, z: 4, core: 2. Of those that a mesh axis runs over, the one named last changes fastest.
Arguments:
- positions: float32 [8, 3, 2048], P('beads', None, 'atoms'), may hold values from 0 to 1
- velocities: float32 [8, 3, 2048], P('beads', None, 'atoms'), may hold values from -3 to 3
- charges_in: float32 [8, 2048], P('beads', 'atoms'), may hold values from -3 to 3
- species: int32 [2048], P('atoms'), may hold values from 0 to 7
- neighbors: int32 [8, 2048], P(None, 'atoms'), may hold values from -32 to 32
- k_index: int32 [3, 2048], replicated, may hold values from -8 to 8
- kernel: float32 [2048], replicated, may hold values from 0.1 to 1
- chi_table: float32 [8], replicated, may hold values from -2 to 2
- hard_table: float32 [8], replicated, may hold values from 1 to 4
- bond_table: float32 [8], replicated, may hold values from 0.2 to 0.8
- mass_table: float32 [8], replicated, may hold values from 1 to 8
Outputs:
- new_positions: float32 [8, 3, 2048], P('beads', None, 'atoms')
- new_velocities: float32 [8, 3, 2048], P('beads', None, 'atoms')
- charges: float32 [8, 2048], P('beads', 'atoms')
Inputs may be any that keep to these rules, and one draw needn't show every extreme that they name: species index the tables. `neighbors`: neighbour offsets count in atom order, cyclically over 2048 atoms.
All inputs are finite; a program needn't handle non-finite values.
Results may differ from a plain program's by a relative error of at most 0.00021.
Values sent between devices are 32-bit elements; how exact they have to be, the bound alone decides.
No kernel may reach another device: no remote copies, remote signals or barrier semaphores. Data moves between devices by JAX's collectives and lax.ppermute only.
A program may use at most 64 MiB of HBM per device.

v0:
```python
import math

import jax
import jax.numpy as jnp
from jax import lax
from jax.sharding import PartitionSpec as P

KVEC = 2048
QITERS = 2
RIM = 32
SPECIES = 8


two_pi = 2.0 * math.pi
ewald_gain = 4.0
mixing = 0.5
spring_rate = 0.5
time_step = 0.05
HIGH = lax.Precision.HIGHEST


def extended(block, sides, width):
    for axis, dim in sides:
        count = lax.axis_size(axis)
        forward = [(i, i + 1) for i in range(count - 1)]
        forward.append((count - 1, 0))
        backward = [(target, source) for source, target in forward]
        low = lax.ppermute(
            lax.slice_in_dim(block, block.shape[dim] - width, None, axis=dim), axis, forward
        )
        high = lax.ppermute(lax.slice_in_dim(block, 0, width, axis=dim), axis, backward)
        block = jnp.concatenate([low, block, high], axis=dim)
    return block


def phase_tables(positions, nblock):
    angle = two_pi * (
        positions[:, 0, :, None] * nblock[0]
        + positions[:, 1, :, None] * nblock[1]
        + positions[:, 2, :, None] * nblock[2]
    )
    return (jnp.cos(angle), jnp.sin(angle))


def unblock(stacked):
    blocks, beads_here, parts, width = stacked.shape
    return stacked.transpose(1, 2, 0, 3).reshape(beads_here, parts, blocks * width)


def to_blocks(pair, blocks):
    beads_here, parts, total = pair.shape
    return pair.reshape(beads_here, parts, blocks, total // blocks).transpose(2, 0, 1, 3)


def local_factors(positions, charge, wave_blocks):

    def local_visit(unused, nblock):
        cosine, sine_part = phase_tables(positions, nblock)
        real_part = jnp.einsum("ba,bak->bk", charge, cosine, precision=HIGH)
        imag_part = jnp.einsum("ba,bak->bk", charge, sine_part, precision=HIGH)
        pair = jnp.stack([real_part, imag_part], 1)
        return (unused, pair)

    unused, stacked = lax.scan(local_visit, None, wave_blocks)
    return unblock(stacked)


def potential_sum(positions, pair, wave_blocks, kernel_blocks):
    coeff_blocks = to_blocks(pair, wave_blocks.shape[0]) * kernel_blocks[:, None, None, :]

    def potential_visit(accum, inputs):
        nblock, cblock = inputs
        cosine, sine_part = phase_tables(positions, nblock)
        accum = accum + jnp.einsum("bak,bk->ba", cosine, cblock[:, 0], precision=HIGH)
        return (accum + jnp.einsum("bak,bk->ba", sine_part, cblock[:, 1], precision=HIGH), None)

    start = jnp.zeros((positions.shape[0], positions.shape[2]), jnp.float32)
    result, unused = lax.scan(potential_visit, start, (wave_blocks, coeff_blocks))
    return result


def force_sum(positions, pair, wave_blocks, kernel_blocks):
    coeff_blocks = to_blocks(pair, wave_blocks.shape[0]) * kernel_blocks[:, None, None, :]

    def force_visit(accum, inputs):
        nblock, cblock = inputs
        cosine, sine_part = phase_tables(positions, nblock)
        mixed = sine_part * cblock[:, 0][:, None, :] - cosine * cblock[:, 1][:, None, :]
        return (accum + jnp.einsum("bak,dk->bda", mixed, nblock, precision=HIGH), None)

    result, unused = lax.scan(
        force_visit, jnp.zeros(positions.shape, jnp.float32), (wave_blocks, coeff_blocks)
    )
    return result


def summed_factors(positions, charge, wave_blocks):
    return lax.psum(local_factors(positions, charge, wave_blocks), "atoms")


def body(
    positions,
    velocities,
    charges_in,
    species,
    neighbors,
    k_index,
    kernel,
    chi_table,
    hard_table,
    bond_table,
    mass_table,
):
    atom_here = positions.shape[2]
    atom_count = atom_here * lax.axis_size("atoms")
    ewald_scale = ewald_gain / math.sqrt(KVEC * atom_count)
    width = min(256, KVEC)
    blocks = KVEC // width
    wave = k_index.astype(jnp.float32)
    wave_blocks = wave.reshape(3, blocks, width).transpose(1, 0, 2)
    kernel_blocks = kernel.reshape(blocks, width)
    onehot = (species[None, :] == jnp.arange(SPECIES, dtype=jnp.int32)[:, None]).astype(jnp.float32)

    def lookup(table):
        return jnp.sum(table[:, None] * onehot, 0)

    electroneg = lookup(chi_table)
    hardness = lookup(hard_table)
    bond_term = lookup(bond_table)
    atom_mass = lookup(mass_table)
    neighbour_index = jnp.arange(atom_here, dtype=jnp.int32)[None, :] + RIM + neighbors
    charge = charges_in
    for rounds in range(QITERS):
        pair = summed_factors(positions, charge, wave_blocks)
        potential = ewald_scale * potential_sum(positions, pair, wave_blocks, kernel_blocks)
        weighted = bond_term[None, :] * charge
        padded = extended(weighted, (("atoms", 1),), RIM)
        neighbour_sum = jnp.sum(padded[:, neighbour_index], 1)
        relaxed = (1.0 - mixing) * charge + mixing * (
            -(electroneg + potential + bond_term * neighbour_sum) / hardness
        )
        charge_sum = lax.psum(jnp.sum(relaxed, 1), "atoms")
        charge = relaxed - (charge_sum / atom_count)[:, None]
    pair = summed_factors(positions, charge, wave_blocks)
    ewald_force = (
        two_pi
        * ewald_scale
        * charge[:, None, :]
        * force_sum(positions, pair, wave_blocks, kernel_blocks)
    )
    padded_beads = extended(positions, (("beads", 0),), 1)
    laplace = 2.0 * positions - padded_beads[:-2] - padded_beads[2:]
    acceleration = ewald_force / atom_mass[None, None, :] - spring_rate * laplace
    new_velocities = velocities + time_step * acceleration
    new_positions = positions + time_step * new_velocities
    return (new_positions, new_velocities, charge)


def solution(mesh):
    return jax.shard_map(
        body,
        mesh=mesh,
        in_specs=(
            P("beads", None, "atoms"),
            P("beads", None, "atoms"),
            P("beads", "atoms"),
            P("atoms"),
            P(None, "atoms"),
            P(),
            P(),
            P(),
            P(),
            P(),
            P(),
        ),
        out_specs=(P("beads", None, "atoms"), P("beads", None, "atoms"), P("beads", "atoms")),
        check_vma=False,
    )
```

profile of v0, /device:TPU:0, one launch (start us, length us, event | category | flops | bytes accessed | tf_op | source)
XLA Modules:
  0.0 570.7 jit_solution(8976064320558124092)
XLA Ops:
  8.6 5.0 collective-permute-start.1
  15.1 40.7 %while.63 = (s32[]{:T(128)}, f32[8,4,2,256]{3,1,2,0:T(4,128)S(1)}, f32[4,3,128]{2,0,1:T(4,128)S(1)}, f32[8,3,256]{2,1,0:T(4,128)S(1)}, f32[4,128]{1,0:T(4,128)S(1)}, /*index=5*/s32[]{:T(128)}, s32[]{:T(128)}, s32[]{}, s32[]{}) while((s32[]{:T(128)}, f32[8,4,2,256]{3,1,2,0:T(4,128)S(1)}, f32[4,3,128]{2,0,1:T(4,128)S(1)}, ...), condition=%wide.region_2.0_spmd, body=%wide.region_1.0_spmd.sunk | while | flops 4720644 | bytes 114821 | solution.py:64
  15.1 2.5 fusion.185
  17.6 2.5 fusion.184
  20.2 2.5 fusion.185
  22.7 2.5 fusion.184
  25.3 2.5 fusion.185
  27.8 2.5 fusion.184
  30.4 2.5 fusion.185
  32.9 2.5 fusion.184
  35.5 2.5 fusion.185
  37.9 2.5 fusion.184
  40.5 2.5 fusion.185
  43.0 2.5 fusion.184
  45.6 2.5 fusion.185
  48.1 2.5 fusion.184
  53.2 2.5 fusion.184
  57.4 2.8 gather_fusion
  60.4 79.7 %all-reduce.4.cloned.1.call-done = f32[4,2,8,256]{3,0,1,2:T(4,128)} async-done(((f32[4,2,8,256]{3,0,1,2:T(4,128)}), f32[4,2,8,256]{3,0,1,2:T(4,128)}) %all-reduce.4.cloned.1.call-update) | async-done | bytes 65552 | tf_op jit(solution)/shard_map/psum | solution.py:98
  140.9 39.9 %while.66 = (s32[]{:T(128)}, f32[4,128]{1,0:T(4,128)S(1)}, f32[4,3,128]{2,0,1:T(4,128)S(1)}, f32[8,3,256]{2,1,0:T(4,128)S(1)}, f32[8,4,2,256]{3,1,2,0:T(4,128)S(1)}, /*index=5*/s32[]{:T(128)}, s32[]{:T(128)}, s32[]{}, s32[]{}) while((s32[]{:T(128)}, f32[4,128]{1,0:T(4,128)S(1)}, f32[4,3,128]{2,0,1:T(4,128)S(1)}, ...), condition=%wide.region_5.6_spmd.clone, body=%wide.region_4.5_spmd.clone.sunk | while | flops 4720133 | bytes 90255 | solution.py:78
  180.9 31.8 %psum.36 = f32[4]{0:T(128)S(1)} all-reduce(f32[4]{0:T(128)S(1)} %get-tuple-element.386), channel_id=1, replica_groups=mesh['atoms'=16,'beads'=2] {'atoms'}, use_global_device_ids=true, to_apply=%region_10.11 | all-reduce | flops 4 | bytes 32 | tf_op jit(solution)/shard_map/psum | solution.py:142
  212.9 4.4 collective-permute-start.3
  217.3 40.7 %while.64 = (s32[]{:T(128)}, f32[8,4,2,256]{3,1,2,0:T(4,128)S(1)}, f32[4,3,128]{2,0,1:T(4,128)S(1)}, f32[8,3,256]{2,1,0:T(4,128)S(1)}, f32[4,128]{1,0:T(4,128)S(1)}, /*index=5*/s32[]{:T(128)}, s32[]{:T(128)}, s32[]{}, s32[]{}) while((s32[]{:T(128)}, f32[8,4,2,256]{3,1,2,0:T(4,128)S(1)}, f32[4,3,128]{2,0,1:T(4,128)S(1)}, ...), condition=%wide.region_12.13_spmd, body=%wide.region_11.12_spmd.sunk | while | flops 4720644 | bytes 114821 | solution.py:64
  219.8 2.5 fusion.190
  224.9 2.5 fusion.190
  230.0 2.5 fusion.190
  235.1 2.5 fusion.190
  240.2 2.5 fusion.190
  245.3 2.5 fusion.190
  247.9 2.5 fusion.191
  250.4 2.5 fusion.190
  253.0 2.5 fusion.191
  255.5 2.5 fusion.190
  259.2 2.8 gather_fusion.1
  262.1 78.5 %all-reduce.6.cloned.1.call-done = f32[4,2,8,256]{3,0,1,2:T(4,128)} async-done(((f32[4,2,8,256]{3,0,1,2:T(4,128)}), f32[4,2,8,256]{3,0,1,2:T(4,128)}) %all-reduce.6.cloned.1.call-update) | async-done | bytes 65552 | tf_op jit(solution)/shard_map/psum | solution.py:98
  341.4 39.9 %while.67 = (s32[]{:T(128)}, f32[4,128]{1,0:T(4,128)S(1)}, f32[4,3,128]{2,0,1:T(4,128)S(1)}, f32[8,3,256]{2,1,0:T(4,128)S(1)}, f32[8,4,2,256]{3,1,2,0:T(4,128)S(1)}, /*index=5*/s32[]{:T(128)}, s32[]{:T(128)}, s32[]{}, s32[]{}) while((s32[]{:T(128)}, f32[4,128]{1,0:T(4,128)S(1)}, f32[4,3,128]{2,0,1:T(4,128)S(1)}, ...), condition=%wide.region_15.16_spmd.clone, body=%wide.region_14.15_spmd.clone.sunk | while | flops 4720133 | bytes 90255 | solution.py:78
  381.5 31.8 %psum.38 = f32[4]{0:T(128)S(1)} all-reduce(f32[4]{0:T(128)S(1)} %get-tuple-element.382), channel_id=1, replica_groups=mesh['atoms'=16,'beads'=2] {'atoms'}, use_global_device_ids=true, to_apply=%region_18.19 | all-reduce | flops 4 | bytes 32 | tf_op jit(solution)/shard_map/psum | solution.py:142
  413.3 40.8 %while.65 = (s32[]{:T(128)}, f32[8,4,2,256]{3,1,2,0:T(4,128)S(1)}, f32[4,3,128]{2,0,1:T(4,128)S(1)}, f32[8,3,256]{2,1,0:T(4,128)S(1)}, f32[4,128]{1,0:T(4,128)S(1)}, /*index=5*/s32[]{:T(128)}, s32[]{:T(128)}, s32[]{}, s32[]{}) while((s32[]{:T(128)}, f32[8,4,2,256]{3,1,2,0:T(4,128)S(1)}, f32[4,3,128]{2,0,1:T(4,128)S(1)}, ...), condition=%wide.region_20.21_spmd, body=%wide.region_19.20_spmd.sunk | while | flops 4720644 | bytes 114821 | solution.py:64
  413.4 2.5 fusion.197
  415.9 2.5 fusion.196
  418.5 2.5 fusion.197
  421.0 2.5 fusion.196
  423.6 2.5 fusion.197
  426.1 2.5 fusion.196
  428.7 2.5 fusion.197
  431.2 2.5 fusion.196
  433.8 2.5 fusion.197
  436.3 2.5 fusion.196
  438.9 2.5 fusion.197
  441.4 2.5 fusion.196
  444.0 2.5 fusion.197
  446.5 2.5 fusion.196
  449.1 2.5 fusion.197
  451.6 2.5 fusion.196
  456.9 79.8 %all-reduce.8.cloned.1.call-done = f32[4,2,8,256]{3,0,1,2:T(4,128)} async-done(((f32[4,2,8,256]{3,0,1,2:T(4,128)}), f32[4,2,8,256]{3,0,1,2:T(4,128)}) %all-reduce.8.cloned.1.call-update) | async-done | bytes 65552 | tf_op jit(solution)/shard_map/psum | solution.py:98
  537.5 25.9 %while.68 = (s32[]{:T(128)}, f32[4,3,128]{2,1,0:T(4,128)S(1)}, f32[8,3,256]{2,1,0:T(4,128)S(1)}, f32[4,3,128]{2,0,1:T(4,128)S(1)}, f32[8,4,2,256]{3,1,2,0:T(4,128)S(1)}, /*index=5*/s32[]{:T(128)}, s32[]{:T(128)}, s32[]{}, s32[]{}) while((s32[]{:T(128)}, f32[4,3,128]{2,1,0:T(4,128)S(1)}, f32[8,3,256]{2,1,0:T(4,128)S(1)}, ...), condition=%wide.region_23.24_spmd.clone, body=%wide.region_22.23_spmd.clone.sunk | while | flops 5901317 | bytes 87187 | solution.py:91
  537.6 3.1 fusion.210
  540.9 3.1 fusion.210
  544.1 3.1 fusion.210
  547.4 3.1 fusion.210
  550.6 3.1 fusion.210
  553.8 3.1 fusion.210
  557.1 3.1 fusion.210
  560.3 3.1 fusion.210
  (410 shorter events, 110.7 us)
Async XLA Ops:
  7.2 132.9 %all-reduce.4.cloned.1.call-start = ((), (), s32[]{:S(2)}) async-start(), calls=%async_computation | async-start | bytes 131072 | tf_op jit(solution)/shard_map/psum | solution.py:98
  7.2 0.8 copy-start.4
  8.1 49.1 %collective-permute-start = (f32[4,32]{1,0:T(4,128)S(1)}, f32[4,32]{1,0:T(4,128)S(1)}, u32[]{:S(2)}, u32[]{:S(2)}) collective-permute-start(f32[4,32]{1,0:T(4,128)S(1)} %get-tuple-element.430), channel_id=1, source_target_pairs={{0,2},{2,4},{4,6},{6,8},{8,10},{10,12},{12,14},{14,16},{16,18},{18... | collective-permute-start | bytes 1544 | tf_op jit(solution)/shard_map/ppermute | solution.py:28
  8.6 48.7 %collective-permute-start.1 = (f32[4,32]{1,0:T(4,128)S(1)}, f32[4,32]{1,0:T(4,128)S(1)}, u32[]{:S(2)}, u32[]{:S(2)}) collective-permute-start(f32[4,32]{1,0:T(4,128)S(1)} %get-tuple-element.431), channel_id=1, source_target_pairs={{2,0},{4,2},{6,4},{8,6},{10,8},{12,10},{14,12},{16,14},{18,16},{20... | collective-permute-start | bytes 1544 | tf_op jit(solution)/shard_map/ppermute | solution.py:31
  14.4 0.7 copy-start
  55.8 0.6 copy-start.2
  55.8 0.7 copy-start.7
  56.4 284.1 %all-reduce.6.cloned.1.call-start = ((), (), s32[]{:S(2)}) async-start(), calls=%async_computation.1 | async-start | bytes 131072 | tf_op jit(solution)/shard_map/psum | solution.py:98
  56.5 0.7 copy-start.5
  212.8 46.1 %collective-permute-start.2 = (f32[4,32]{1,0:T(4,128)S(1)}, f32[4,32]{1,0:T(4,128)S(1)}, u32[]{:S(2)}, u32[]{:S(2)}) collective-permute-start(f32[4,32]{1,0:T(4,128)S(1)} %get-tuple-element.428), channel_id=1, source_target_pairs={{0,2},{2,4},{4,6},{6,8},{8,10},{10,12},{12,14},{14,16},{16,18},{18... | collective-permute-start | bytes 1544 | tf_op jit(solution)/shard_map/ppermute | solution.py:28
  212.9 46.1 %collective-permute-start.3 = (f32[4,32]{1,0:T(4,128)S(1)}, f32[4,32]{1,0:T(4,128)S(1)}, u32[]{:S(2)}, u32[]{:S(2)}) collective-permute-start(f32[4,32]{1,0:T(4,128)S(1)} %get-tuple-element.429), channel_id=1, source_target_pairs={{2,0},{4,2},{6,4},{8,6},{10,8},{12,10},{14,12},{16,14},{18,16},{20... | collective-permute-start | bytes 1544 | tf_op jit(solution)/shard_map/ppermute | solution.py:31
  258.1 0.6 copy-start.3
  258.7 278.0 %all-reduce.8.cloned.1.call-start = ((), (), s32[]{:S(2)}) async-start(), calls=%async_computation.2 | async-start | bytes 131072 | tf_op jit(solution)/shard_map/psum | solution.py:98
  454.1 0.6 copy-start.8
  454.2 0.6 copy-start.1
  454.8 108.7 %collective-permute-start.4 = (f32[1,3,128]{2,0,1:T(1,128)S(1)}, f32[1,3,128]{2,0,1:T(1,128)S(1)}, u32[]{:S(2)}, u32[]{:S(2)}) collective-permute-start(f32[1,3,128]{2,0,1:T(1,128)S(1)} %get-tuple-element.426), channel_id=1, source_target_pairs={{0,1},{1,0},{2,3},{3,2},{4,5},{5,4},{6,7},{7,6},{8,9},{9,8},{10,11... | collective-permute-start | bytes 4616 | tf_op jit(solution)/shard_map/ppermute | solution.py:28
  456.4 107.2 %collective-permute-start.5 = (f32[1,3,128]{2,0,1:T(1,128)S(1)}, f32[1,3,128]{2,0,1:T(1,128)S(1)}, u32[]{:S(2)}, u32[]{:S(2)}) collective-permute-start(f32[1,3,128]{2,0,1:T(1,128)S(1)} %get-tuple-element.427), channel_id=1, source_target_pairs={{1,0},{0,1},{3,2},{2,3},{5,4},{4,5},{7,6},{6,7},{9,8},{8,9},{11,10... | collective-permute-start | bytes 4616 | tf_op jit(solution)/shard_map/ppermute | solution.py:31
  537.5 26.0 %copy-start.6 = (f32[4,3,128]{2,0,1:T(4,128)S(1)}, f32[4,3,128]{2,0,1:T(4,128)}, u32[]{:S(2)}) copy-start(f32[4,3,128]{2,0,1:T(4,128)} %param.24) | copy-start | bytes 18436
Sparse Core Ops, SparseCore 0:
  56.6 83.4 all-reduce.3
  258.8 81.7 all-reduce.5
  454.9 81.6 all-reduce.7
where the time goes:
time: 572 us; the launch traced here: 571 us
  waiting for transfers between devices  238 us (42%)
  matrix products  223 us (39%)
  blocking collectives  63.5 us (11%)
  between operations  14.1 us (2%)
  starting transfers between devices  12.3 us (2%)
  local copies, waits for them, and re-layouts  11.7 us (2%)
  other arithmetic  6.01 us (1%)
    psum x3, waiting for transfers between devices, summed_factors(): return lax.psum(local_factors(positions, charge, wave_blocks), 'atoms')  238 us
    psum x2, blocking collectives, body(): charge_sum = lax.psum(jnp.sum(relaxed, 1), 'atoms')  63.5 us
    dot_general x24, matrix products, local_visit(): imag_part = jnp.einsum('ba,bak->bk', charge, sine_part, precision=HIGH)  59.9 us
    dot_general x24, matrix products, local_visit(): real_part = jnp.einsum('ba,bak->bk', charge, cosine, precision=HIGH)  59.6 us
    dot_general x16, matrix products, potential_visit(): jnp.einsum('bak,bk->ba', sine_part, cblock[:, 1], precision=HIGH)  39.5 us
    dot_general x16, matrix products, potential_visit(): jnp.einsum('bak,bk->ba', cosine, cblock[:, 0], precision=HIGH)  38.8 us
    dot_general x8, matrix products, force_visit(): jnp.einsum('bak,dk->bda', mixed, nblock, precision=HIGH)  25.1 us
  transfers between devices with their start and end apart: 9, of which 3 were waited for; matrix products, arithmetic and copies ran while one was open for 20% of the time, Pallas kernels for 0%

commit v1 on v0

v1 whole, which is shorter than its diff:
```python
import functools
import math

import jax
import jax.numpy as jnp
from jax import lax
from jax.experimental import pallas as pl
from jax.experimental.pallas import tpu as pltpu
from jax.sharding import PartitionSpec as P

KVEC = 2048
QITERS = 2
SPECIES = 8
KMAX = 8
MODES = 160

two_pi = 2.0 * math.pi
ewald_gain = 4.0
mixing = 0.5
spring_rate = 0.5
time_step = 0.05

COS = (
    0.9999999998855522,
    -19.739208743453656,
    64.93938907588092,
    -85.45665831455305,
    60.242131335932854,
    -26.404668174676782,
    7.800131403864327,
    -1.4531122801527303,
)
SIN = (
    6.2831853025115,
    -41.34170040531697,
    81.60513138577565,
    -76.70301535354703,
    42.02592698387527,
    -14.89984666196953,
    3.2381375032044204,
)

F32 = jnp.float32
BF16 = jnp.bfloat16
NT = (((1,), (1,)), ((), ()))
NN = (((1,), (0,)), ((), ()))


def horner(coeffs, x):
    value = jnp.full_like(x, coeffs[-1])
    for coeff in coeffs[-2::-1]:
        value = value * x + coeff
    return value


def turns(multiple, x):
    t = multiple * x
    t = t - jnp.floor(t + 0.5)
    square = t * t
    return horner(COS, square), t * horner(SIN, square)


def halves(x):
    high = x.astype(BF16)
    return high, (x - high.astype(F32)).astype(BF16)


def rows_of(one, two, rest):
    high, low = halves(jnp.concatenate([one, two], 0))
    rest_high = rest.astype(BF16).astype(F32)
    both = jnp.concatenate([rest_high, rest - rest_high], 0).astype(BF16)
    return jnp.concatenate([high, both, low], 0)


def product(left, high, low, dims):
    main = lax.dot_general(left, high, dims, preferred_element_type=F32)
    one = main[0:8] + main[32:40]
    two = main[8:16] + main[40:48]
    rest = main[16:24] + main[24:32]
    if low is not None:
        minor = lax.dot_general(left[0:32], low, dims, preferred_element_type=F32)
        one = one + minor[0:8]
        two = two + minor[8:16]
        rest = rest + minor[16:24]
    return one, two, rest


def pack_kernel(ranks, pos, charge, species, neighbors, out, edges):
    beads, _, width = pos.shape
    spec = species[...].astype(F32)
    near = neighbors[...].astype(F32)
    pad = jnp.zeros((3, width), F32)
    blocks = [
        jnp.concatenate([pos[b], charge[b : b + 1, :], spec, pad], 0) for b in range(beads)
    ]
    for rank in range(ranks):
        out[rank, 0:8, :] = near
        out[rank, 8:16, :] = blocks[rank % beads]
    edges[0] = pos[0]
    edges[1] = pos[beads - 1]


def weight_kernel(k_index, kernel, out):
    count = k_index.shape[1]
    k = k_index[...]
    first, second, third = k[0:1], k[1:2], k[2:3]
    flip = (first < 0) | ((first == 0) & (second < 0))
    sign = jnp.where(flip, -1, 1)
    p, q, r = sign * first, sign * second, sign * third
    wide = 16 * (p - 1)
    with_p = jnp.where(q > 0, wide + q - 1, jnp.where(q < 0, wide + 7 - q, 135 + p))
    without_p = jnp.where(q > 0, 127 + q, 144)
    mode = jnp.where(p > 0, with_p, without_p)
    at = lax.broadcasted_iota(jnp.int32, (MODES, count), 0)
    chosen = jnp.where(at == mode, 1.0, 0.0).astype(BF16)
    row = lax.broadcasted_iota(jnp.int32, (8, count), 0)
    weight = kernel[...]
    here = row + 1 == jnp.abs(r)
    even = jnp.where(here, weight, 0.0)
    odd = jnp.where(here, jnp.where(r < 0, -weight, weight), 0.0)
    zero = jnp.where((row == 0) & (r == 0), weight, 0.0)
    even, odd, zero = product(rows_of(even, odd, zero), chosen, None, NT)
    out[0:8, :] = even
    out[8:16, :] = odd
    out[16:24, :] = zero


def bead_kernel(
    scale,
    inverse_atoms,
    beads,
    rank_ref,
    got,
    weights,
    chi_table,
    hard_table,
    bond_table,
    out,
    cos_high,
    cos_low,
    sin_high,
    sin_low,
    left,
    z_cos,
    z_sin,
    charges,
):
    ranks, _, width = got.shape
    lane = lax.broadcasted_iota(jnp.int32, (8, width), 1)
    row = lax.broadcasted_iota(jnp.int32, (8, width), 0)
    multiple = (row + 1).astype(F32)
    single = jnp.where(row == 0, 1.0, 0.0)
    blank = jnp.zeros((8, width), F32)

    def at(j):
        return slice(j * width, (j + 1) * width)

    def everywhere(x):
        return jnp.broadcast_to(x, (8, width))

    def column_sum(x):
        return everywhere(jnp.sum(x, axis=0, keepdims=True))

    chi, hard, bond, charge = [], [], [], []
    for j in range(ranks):
        cx, sx = turns(multiple, got[j, 8:9, :])
        cy, sy = turns(multiple, got[j, 9:10, :])
        cz, sz = turns(multiple, got[j, 10:11, :])
        z_cos[:, at(j)] = cz
        z_sin[:, at(j)] = sz

        def keep(rows, cosine, sine):
            high, low = halves(cosine)
            cos_high[rows, at(j)] = high
            cos_low[rows, at(j)] = low
            high, low = halves(sine)
            sin_high[rows, at(j)] = high
            sin_low[rows, at(j)] = low

        for p in range(8):
            cp, sp = everywhere(cx[p : p + 1]), everywhere(sx[p : p + 1])
            cc, ss, sc, cs = cp * cy, sp * sy, sp * cy, cp * sy
            keep(
                slice(16 * p, 16 * p + 16),
                jnp.concatenate([cc - ss, cc + ss], 0),
                jnp.concatenate([sc + cs, sc - cs], 0),
            )
        keep(slice(128, 144), jnp.concatenate([cy, cx], 0), jnp.concatenate([sy, sx], 0))
        keep(
            slice(144, 160),
            jnp.concatenate([single, blank], 0),
            jnp.concatenate([blank, blank], 0),
        )
        species = everywhere(got[j, 12:13, :])
        c, h, b = blank, blank, blank
        for kind in range(SPECIES):
            this = species == float(kind)
            c = jnp.where(this, chi_table[kind], c)
            h = jnp.where(this, hard_table[kind], h)
            b = jnp.where(this, bond_table[kind], b)
        chi.append(c)
        hard.append(mixing / h)
        bond.append(b)
        charge.append(everywhere(got[j, 11:12, :]))

    even, odd, zero = weights[0:8, :], weights[8:16, :], weights[16:24, :]

    def coefficients(charge):
        for j in range(ranks):
            left[:, at(j)] = rows_of(
                charge[j] * z_cos[:, at(j)], charge[j] * z_sin[:, at(j)], charge[j] * single
            )
        t_cc, t_cs, t_c0 = product(left[...], cos_high[...], cos_low[...], NT)
        t_sc, t_ss, t_s0 = product(left[...], sin_high[...], sin_low[...], NT)
        v_cos = (even * t_cc - odd * t_ss, even * t_cs + odd * t_sc, zero * t_c0)
        v_sin = (even * t_sc + odd * t_cs, even * t_ss - odd * t_cc, zero * t_s0)
        return v_cos, v_sin

    for rounds in range(QITERS):
        v_cos, v_sin = coefficients(charge)
        from_cos = product(rows_of(*v_cos), cos_high[...], cos_low[...], NN)
        from_sin = product(rows_of(*v_sin), sin_high[...], sin_low[...], NN)
        u_c, u_s, u_0 = (a + b for a, b in zip(from_cos, from_sin))
        weighted = [b * q for b, q in zip(bond, charge)]
        relaxed = []
        total = blank
        for j in range(ranks):
            potential = scale * column_sum(
                z_cos[:, at(j)] * u_c[:, at(j)] + z_sin[:, at(j)] * u_s[:, at(j)] + u_0[:, at(j)]
            )
            before = weighted[(j - 1) % ranks]
            after = weighted[(j + 1) % ranks]
            lower = jnp.where(lane < 3 * width // 4, weighted[j], before)
            upper = jnp.where(lane >= width // 4, weighted[j], after)
            place = (lane + got[j, 0:8, :].astype(jnp.int32)) & (width - 1)
            near = jnp.where(
                lane < width // 2,
                jnp.take_along_axis(lower, place, axis=1),
                jnp.take_along_axis(upper, place, axis=1),
            )
            new = (1.0 - mixing) * charge[j] - hard[j] * (
                chi[j] + potential + bond[j] * column_sum(near)
            )
            relaxed.append(new)
            total = total + new
        mean = jnp.sum(total, axis=1, keepdims=True) * inverse_atoms
        charge = [new - mean for new in relaxed]

    for j in range(ranks):
        charges[:, at(j)] = charge[j]
    (v_cc, v_cs, v_c0), (v_sc, v_ss, v_s0) = coefficients(charge)
    mode = lax.broadcasted_iota(jnp.int32, (8, MODES), 1)
    inner = mode & 15
    wave_x = jnp.where(
        mode < 128, (mode >> 4) + 1, jnp.where((mode >= 136) & (mode < 144), mode - 135, 0)
    ).astype(F32)
    wave_y = jnp.where(
        mode < 128,
        jnp.where(inner < 8, inner + 1, 7 - inner),
        jnp.where(mode < 136, mode - 127, 0),
    ).astype(F32)
    span = beads * width
    base = pl.multiple_of((rank_ref[0] // beads) * span, span)
    own = pl.ds(base, span)
    ch, cl, sh, sl = (ref[:, own] for ref in (cos_high, cos_low, sin_high, sin_low))
    zc, zs, q = z_cos[:, own], z_sin[:, own], charges[:, own]

    def field(for_cos, for_sin):
        a = product(rows_of(*for_cos), ch, cl, NN)
        b = product(rows_of(*for_sin), sh, sl, NN)
        return (one + two for one, two in zip(a, b))

    def force(wave):
        u_c, u_s, u_0 = field(
            (-wave * v_sc, -wave * v_ss, -wave * v_s0), (wave * v_cc, wave * v_cs, wave * v_c0)
        )
        return zc * u_c + zs * u_s + u_0

    along_x = force(wave_x)
    along_y = force(wave_y)
    u_c, u_s, _ = field((v_cc, v_cs, v_c0), (v_sc, v_ss, v_s0))
    wide_multiple = jnp.broadcast_to(multiple[:, 0:1], (8, span))
    along_z = wide_multiple * (zs * u_c - zc * u_s)
    factor = (two_pi * scale) * q
    for t in range(beads):
        cut = at(t)
        fx, fy, fz = (
            factor[:, cut] * column_sum(f[:, cut]) for f in (along_x, along_y, along_z)
        )
        out[t] = jnp.where(row == 0, fx, jnp.where(row == 1, fy, jnp.where(row == 2, fz, q[:, cut])))


def move_kernel(low_at, high_at, pos, vel, got, low, high, species, mass_table, pos_out, vel_out, charge_out):
    beads, dims, width = pos.shape
    kinds = jnp.broadcast_to(species[...], (dims, width))
    mass = jnp.zeros((dims, width), F32)
    for kind in range(SPECIES):
        mass = jnp.where(kinds == kind, mass_table[kind], mass)
    for b in range(beads):
        here = pos[b]
        before = pos[b - 1] if b > 0 else low[low_at]
        after = pos[b + 1] if b < beads - 1 else high[high_at]
        laplace = 2.0 * here - before - after
        fresh = vel[b] + time_step * (got[b, 0:3, :] / mass - spring_rate * laplace)
        vel_out[b] = fresh
        pos_out[b] = here + time_step * fresh
        charge_out[b : b + 1, :] = got[b, 3:4, :]


VMEM = pl.BlockSpec(memory_space=pltpu.VMEM)
SMEM = pl.BlockSpec(memory_space=pltpu.SMEM)


def body(
    positions,
    velocities,
    charges_in,
    species,
    neighbors,
    k_index,
    kernel,
    chi_table,
    hard_table,
    bond_table,
    mass_table,
):
    beads, dims, width = positions.shape
    ranks = lax.axis_size("atoms")
    chain = lax.axis_size("beads")
    atoms = ranks * width
    scale = ewald_gain / math.sqrt(KVEC * atoms)
    kinds = species[None, :]
    shape = jax.ShapeDtypeStruct

    packed, edges = pl.pallas_call(
        functools.partial(pack_kernel, ranks),
        out_shape=(shape((ranks, 16, width), F32), shape((2, dims, width), F32)),
        in_specs=[VMEM] * 4,
        out_specs=(VMEM, VMEM),
        name="pack",
    )(positions, charges_in, kinds, neighbors)
    if chain == 2:
        low = high = lax.ppermute(edges, "beads", [(0, 1), (1, 0)])
        low_at, high_at = 1, 0
    else:
        forward = [(i, (i + 1) % chain) for i in range(chain)]
        low = lax.ppermute(edges[1:2], "beads", forward)
        high = lax.ppermute(edges[0:1], "beads", [(b, a) for a, b in forward])
        low_at, high_at = 0, 0
    got = lax.all_to_all(packed, "atoms", 0, 0, tiled=True)

    weights = pl.pallas_call(
        weight_kernel,
        out_shape=shape((24, MODES), F32),
        in_specs=[VMEM] * 2,
        out_specs=VMEM,
        name="weights",
        cost_estimate=pl.CostEstimate(flops=10**9, bytes_accessed=10**5, transcendentals=0),
    )(k_index, kernel[None, :])

    rank = lax.axis_index("atoms").astype(jnp.int32)[None]
    result = pl.pallas_call(
        functools.partial(bead_kernel, scale, 1.0 / atoms, beads),
        out_shape=shape((beads, 8, width), F32),
        in_specs=[SMEM, VMEM, VMEM, SMEM, SMEM, SMEM],
        out_specs=VMEM,
        scratch_shapes=[
            pltpu.VMEM((MODES, atoms), BF16),
            pltpu.VMEM((MODES, atoms), BF16),
            pltpu.VMEM((MODES, atoms), BF16),
            pltpu.VMEM((MODES, atoms), BF16),
            pltpu.VMEM((48, atoms), BF16),
            pltpu.VMEM((8, atoms), F32),
            pltpu.VMEM((8, atoms), F32),
            pltpu.VMEM((8, atoms), F32),
        ],
        compiler_params=pltpu.CompilerParams(vmem_limit_bytes=32 * 1024 * 1024),
        name="bead",
    )(rank, got, weights, chi_table, hard_table, bond_table)

    groups = [list(range(g, g + beads)) for g in range(0, ranks, beads)]
    home = lax.all_to_all(result, "atoms", 0, 0, axis_index_groups=groups, tiled=True)

    return pl.pallas_call(
        functools.partial(move_kernel, low_at, high_at),
        out_shape=(
            shape(positions.shape, F32),
            shape(positions.shape, F32),
            shape(charges_in.shape, F32),
        ),
        in_specs=[VMEM] * 6 + [SMEM],
        out_specs=(VMEM, VMEM, VMEM),
        name="move",
    )(positions, velocities, home, low, high, kinds, mass_table)


def solution(mesh):
    return jax.shard_map(
        body,
        mesh=mesh,
        in_specs=(
            P("beads", None, "atoms"),
            P("beads", None, "atoms"),
            P("beads", "atoms"),
            P("atoms"),
            P(None, "atoms"),
            P(),
            P(),
            P(),
            P(),
            P(),
            P(),
        ),
        out_specs=(P("beads", None, "atoms"), P("beads", None, "atoms"), P("beads", "atoms")),
        check_vma=False,
    )
```

time: 572 us -> 37.7 us (0.07)
  waiting for transfers between devices: 238 us -> 7.84 us
  matrix products: 223 us -> 0 us
  blocking collectives: 63.5 us -> 0 us
  between operations: 14.1 us -> 0.68 us
  Pallas kernels: 0 us -> 10.7 us
  local copies, waits for them, and re-layouts: 11.7 us -> 5.6 us
  other arithmetic: 6.01 us -> 0 us
    psum x3 -> x0, waiting for transfers between devices: 238 us -> none  [summed_factors(): return lax.psum(local_factors(positions, charge, wave_blocks), 'atoms')]
    dot_general x88 -> x0, matrix products: 223 us -> none  [the longest x24 59.9 us: local_visit(): imag_part = jnp.einsum('ba,bak->bk', charge, sine_part, precision=HIGH)]
    psum x2 -> x0, blocking collectives: 63.5 us -> none  [body(): charge_sum = lax.psum(jnp.sum(relaxed, 1), 'atoms')]
    all_to_all x0 -> x2, starting transfers between devices: none -> 10.7 us  [the longest x1 7.36 us: body(): got = lax.all_to_all(packed, 'atoms', 0, 0, tiled=True)]
    pallas_call x0 -> x4, Pallas kernels: none -> 10.7 us  [the longest x1 6.13 us: body(): pl.pallas_call(functools.partial(bead_kernel, scale, 1.0 / atoms, beads),...]
    ppermute x6 -> x1, starting transfers between devices: 12 us -> 1.58 us  [body(): low = high = lax.ppermute(edges, 'beads', [(0, 1), (1, 0)])]
    all_to_all x0 -> x2, waiting for transfers between devices: none -> 6.35 us  [the longest x1 6.22 us: body(): got = lax.all_to_all(packed, 'atoms', 0, 0, tiled=True)]
  transfers between devices with their start and end apart: 9 -> 3, of which waited for: 3 -> 3; matrix products, arithmetic and copies ran while one was open for 20% -> 2% of each run, Pallas kernels for 0% -> 5%
where the time goes in v1:
time: 37.7 us; the launch traced here: 37.1 us
  starting transfers between devices  12.3 us (33%)
  Pallas kernels  10.7 us (28%)
  waiting for transfers between devices  7.84 us (21%)
  local copies, waits for them, and re-layouts  5.6 us (15%)
  between operations  0.68 us (2%)
    all_to_all x1, starting transfers between devices, body(): got = lax.all_to_all(packed, 'atoms', 0, 0, tiled=True)  7.36 us
    all_to_all x1, waiting for transfers between devices, body(): got = lax.all_to_all(packed, 'atoms', 0, 0, tiled=True)  6.22 us
    pallas_call x1, Pallas kernels, body(): pl.pallas_call(functools.partial(bead_kernel, scale, 1.0 / atoms, beads),...  6.13 us
    unnamed x20, local copies, waits for them, and re-layouts  3.7 us
    all_to_all x1, starting transfers between devices, body(): lax.all_to_all(result, 'atoms', 0, 0, axis_index_groups=groups, tiled=True)  3.37 us
    pallas_call x2, local copies, waits for them, and re-layouts, body(): pl.pallas_call(functools.partial(move_kernel, low_at, high_at), out_shape...  1.9 us
    pallas_call x1, Pallas kernels, body(): pl.pallas_call(weight_kernel, out_shape=shape((24, MODES), F32), in_specs...  1.71 us
    ppermute x1, starting transfers between devices, body(): low = high = lax.ppermute(edges, 'beads', [(0, 1), (1, 0)])  1.58 us
  transfers between devices with their start and end apart: 3, of which 3 were waited for; matrix products, arithmetic and copies ran while one was open for 2% of the time, Pallas kernels for 5%

profile of v1, /device:TPU:0, one launch (start us, length us, event | category | flops | bytes accessed | tf_op | source)
XLA Modules:
  0.0 37.1 jit_solution(11273604810783981804)
XLA Ops:
  0.6 1.3 %copy.15.pos = f32[4,3,128]{2,1,0:T(4,128)} copy(f32[4,3,128]{2,0,1:T(4,128)} %param.11) | data formatting | bytes 12288 | tf_op args[0]
  1.9 1.4 %pack.1 = (f32[16,16,128]{2,1,0:T(8,128)}, f32[2,3,128]{2,1,0:T(4,128)}) custom-call(f32[4,3,128]{2,1,0:T(4,128)} %copy.15.pos, f32[4,128]{1,0:T(4,128)} %charge.1, s32[1,128]{1,0:T(1,128)} %bitcast.3, s32[8,128]{1,0:T(8,128)} %neighbors.1), custom_call_target="tpu_custom_call" | custom-call | tf_op jit(solution)/shard_map/pack/pallas_call | solution.py:335
  3.3 7.4 %all-to-all-start = ((f32[16,16,128]{2,1,0:T(8,128)}), f32[16,16,128]{2,1,0:T(8,128)S(1)}, u32[]{:S(2)}, u32[]{:S(2)}) async-start(f32[16,16,128]{2,1,0:T(8,128)} %get-tuple-element.5), calls=%async_computation | async-start | bytes 262144 | tf_op jit(solution)/shard_map/all_to_all | solution.py:350
  10.7 1.7 %weights.1 = f32[24,160]{1,0:T(8,128)} custom-call(s32[3,2048]{1,0:T(4,128)} %k_index.1, f32[1,2048]{1,0:T(1,128)} %bitcast.5), custom_call_target="tpu_custom_call" | custom-call | flops 1000000000 | bytes 100000 | tf_op jit(solution)/shard_map/weights/pallas_call | solution.py:352
  12.4 0.0 copy-start.1
  12.4 0.0 copy-start.2
  12.4 0.0 copy-start.3
  12.4 6.2 %all-to-all-done.got = f32[16,16,128]{2,1,0:T(8,128)S(1)} async-done(((f32[16,16,128]{2,1,0:T(8,128)}), f32[16,16,128]{2,1,0:T(8,128)S(1)}, u32[]{:S(2)}, u32[]{:S(2)}) %all-to-all-start) | async-done | bytes 131104 | tf_op jit(solution)/shard_map/all_to_all | solution.py:350
  18.6 0.0 copy-done.1
  18.6 0.0 copy-done.2
  18.6 0.0 copy-done.3
  18.6 0.0 copy-start
  18.7 0.7 %copy-done = f32[24,160]{1,0:T(8,128)S(1)} copy-done((f32[24,160]{1,0:T(8,128)S(1)}, f32[24,160]{1,0:T(8,128)}, u32[]{:S(2)}) %copy-start) | copy-done | bytes 15384
  19.4 0.0 copy-start.7
  19.4 6.1 %bead.1 = f32[4,8,128]{2,1,0:T(8,128)} custom-call(s32[1]{0:T(128)} %bitcast.rank_ref, f32[16,16,128]{2,1,0:T(8,128)S(1)} %all-to-all-done.got, f32[24,160]{1,0:T(8,128)S(1)} %copy-done, f32[8]{0:T(128)S(1)} %copy-done.1, f32[8]{0:T(128)S(1)} %copy-done.2, f32[8]{0:T(128)S(1)} %copy-done.3), custom_call_target="tpu_custom_call" | custom-call | tf_op jit(solution)/shard_map/bead/pallas_call | solution.py:362
  25.5 0.0 copy-start.8
  25.5 3.4 %all-to-all-start.1 = ((f32[4,8,128]{2,1,0:T(8,128)}), f32[4,8,128]{2,1,0:T(8,128)S(1)}, u32[]{:S(2)}, u32[]{:S(2)}) async-start(f32[4,8,128]{2,1,0:T(8,128)} %bead.1), calls=%async_computation.1 | async-start | bytes 32768 | tf_op jit(solution)/shard_map/all_to_all | solution.py:382
  28.9 0.0 copy-done.8
  28.9 1.6 %collective-permute-start = (f32[2,3,128]{2,1,0:T(4,128)S(1)}, f32[2,3,128]{2,1,0:T(4,128)S(1)}, u32[]{:S(2)}, u32[]{:S(2)}) collective-permute-start(f32[2,3,128]{2,1,0:T(4,128)S(1)} %copy-done.8), channel_id=1, source_target_pairs={{0,1},{1,0},{2,3},{3,2},{4,5},{5,4},{6,7},{7,6},{8,9},{9,8},{10,11... | collective-permute-start | bytes 9224 | tf_op jit(solution)/shard_map/ppermute | solution.py:343
  30.5 0.0 copy-done.7
  30.5 0.6 %copy.16.vel = f32[4,3,128]{2,1,0:T(4,128)} copy(f32[4,3,128]{2,0,1:T(4,128)S(1)} %copy-done.7) | data formatting | bytes 12288 | tf_op args[1]
  31.1 1.5 %collective-permute-done.low.high = f32[2,3,128]{2,1,0:T(4,128)S(1)} collective-permute-done((f32[2,3,128]{2,1,0:T(4,128)S(1)}, f32[2,3,128]{2,1,0:T(4,128)S(1)}, u32[]{:S(2)}, u32[]{:S(2)}) %collective-permute-start) | collective-permute-done | bytes 3104 | tf_op jit(solution)/shard_map/ppermute | solution.py:343
  32.6 0.0 copy-start.5
  32.6 0.1 all-to-all-done.1.got
  32.7 0.5 %copy-done.5 = f32[2,3,128]{2,1,0:T(4,128)} copy-done((f32[2,3,128]{2,1,0:T(4,128)}, f32[2,3,128]{2,1,0:T(4,128)S(1)}, u32[]{:S(2)}) %copy-start.5) | copy-done | bytes 3096
  33.2 0.0 copy-start.4
  33.2 0.6 %copy-done.4 = f32[4,8,128]{2,1,0:T(8,128)} copy-done((f32[4,8,128]{2,1,0:T(8,128)}, f32[4,8,128]{2,1,0:T(8,128)S(1)}, u32[]{:S(2)}) %copy-start.4) | copy-done | bytes 16408
  33.8 1.4 %move.1 = (f32[4,3,128]{2,1,0:T(4,128)}, f32[4,3,128]{2,1,0:T(4,128)}, f32[4,128]{1,0:T(4,128)}) custom-call(f32[4,3,128]{2,1,0:T(4,128)} %copy.15.pos, f32[4,3,128]{2,1,0:T(4,128)} %copy.16.vel, f32[4,8,128]{2,1,0:T(8,128)} %copy-done.4, f32[2,3,128]{2,1,0:T(4,128)} %copy-done.5, f32[2,3,128]{2,1,0:T(4,128)} %copy-done.5, s32[1,128]{1,0:T(1,128)} %bitcast.4, ...), custom_call_target="tpu_custom_call" | custom-call | tf_op jit(solution)/shard_map/move/pallas_call | solution.py:384
  35.2 0.0 copy-start.6
  35.2 1.3 %copy.17 = f32[4,3,128]{2,0,1:T(4,128)} copy(f32[4,3,128]{2,1,0:T(4,128)} %get-tuple-element.7) | data formatting | bytes 12288 | tf_op jit(solution)/shard_map/move/pallas_call | solution.py:384
  36.5 0.0 copy-done.6
  36.5 0.6 %copy.18 = f32[4,3,128]{2,0,1:T(4,128)} copy(f32[4,3,128]{2,1,0:T(4,128)S(1)} %copy-done.6) | data formatting | bytes 12288 | tf_op jit(solution)/shard_map/move/pallas_call | solution.py:384
Async XLA Ops:
  3.3 15.3 %all-to-all-start = ((f32[16,16,128]{2,1,0:T(8,128)}), f32[16,16,128]{2,1,0:T(8,128)S(1)}, u32[]{:S(2)}, u32[]{:S(2)}) async-start(f32[16,16,128]{2,1,0:T(8,128)} %get-tuple-element.5), calls=%async_computation | async-start | bytes 262144 | tf_op jit(solution)/shard_map/all_to_all | solution.py:350
  12.4 6.2 %copy-start.1 = (f32[8]{0:T(128)S(1)}, f32[8]{0:T(128)}, u32[]{:S(2)}) copy-start(f32[8]{0:T(128)} %chi_table.1) | copy-start | bytes 100
  12.4 6.2 %copy-start.2 = (f32[8]{0:T(128)S(1)}, f32[8]{0:T(128)}, u32[]{:S(2)}) copy-start(f32[8]{0:T(128)} %hard_table.1) | copy-start | bytes 100
  12.4 6.2 %copy-start.3 = (f32[8]{0:T(128)S(1)}, f32[8]{0:T(128)}, u32[]{:S(2)}) copy-start(f32[8]{0:T(128)} %bond_table.1) | copy-start | bytes 100
  18.6 0.7 %copy-start = (f32[24,160]{1,0:T(8,128)S(1)}, f32[24,160]{1,0:T(8,128)}, u32[]{:S(2)}) copy-start(f32[24,160]{1,0:T(8,128)} %weights.1) | copy-start | bytes 46084
  19.4 11.1 %copy-start.7 = (f32[4,3,128]{2,0,1:T(4,128)S(1)}, f32[4,3,128]{2,0,1:T(4,128)}, u32[]{:S(2)}) copy-start(f32[4,3,128]{2,0,1:T(4,128)} %param.12) | copy-start | bytes 18436
  25.5 3.4 %copy-start.8 = (f32[2,3,128]{2,1,0:T(4,128)S(1)}, f32[2,3,128]{2,1,0:T(4,128)}, u32[]{:S(2)}) copy-start(f32[2,3,128]{2,1,0:T(4,128)} %get-tuple-element.6) | copy-start | bytes 9220
  25.5 7.2 %all-to-all-start.1 = ((f32[4,8,128]{2,1,0:T(8,128)}), f32[4,8,128]{2,1,0:T(8,128)S(1)}, u32[]{:S(2)}, u32[]{:S(2)}) async-start(f32[4,8,128]{2,1,0:T(8,128)} %bead.1), calls=%async_computation.1 | async-start | bytes 32768 | tf_op jit(solution)/shard_map/all_to_all | solution.py:382
  28.9 3.7 %collective-permute-start = (f32[2,3,128]{2,1,0:T(4,128)S(1)}, f32[2,3,128]{2,1,0:T(4,128)S(1)}, u32[]{:S(2)}, u32[]{:S(2)}) collective-permute-start(f32[2,3,128]{2,1,0:T(4,128)S(1)} %copy-done.8), channel_id=1, source_target_pairs={{0,1},{1,0},{2,3},{3,2},{4,5},{5,4},{6,7},{7,6},{8,9},{9,8},{10,11... | collective-permute-start | bytes 9224 | tf_op jit(solution)/shard_map/ppermute | solution.py:343
  32.6 0.6 %copy-start.5 = (f32[2,3,128]{2,1,0:T(4,128)}, f32[2,3,128]{2,1,0:T(4,128)S(1)}, u32[]{:S(2)}) copy-start(f32[2,3,128]{2,1,0:T(4,128)S(1)} %collective-permute-done.low.high) | copy-start | bytes 9220
  33.2 0.6 %copy-start.4 = (f32[4,8,128]{2,1,0:T(8,128)}, f32[4,8,128]{2,1,0:T(8,128)S(1)}, u32[]{:S(2)}) copy-start(f32[4,8,128]{2,1,0:T(8,128)S(1)} %all-to-all-done.1.got) | copy-start | bytes 49156
  35.2 1.3 %copy-start.6 = (f32[4,3,128]{2,1,0:T(4,128)S(1)}, f32[4,3,128]{2,1,0:T(4,128)}, u32[]{:S(2)}) copy-start(f32[4,3,128]{2,1,0:T(4,128)} %get-tuple-element.8) | copy-start | bytes 18436

commit v2 on v1

--- a/solution.py
+++ b/solution.py
@@ -85,22 +85,32 @@
     return one, two, rest
 
 
-def pack_kernel(ranks, pos, charge, species, neighbors, out, edges):
-    beads, _, width = pos.shape
+def partner(me, t, count):
+    if count & (count - 1) == 0:
+        return me ^ abs(t)
+    return (me + t + count) % count
+
+
+def pack_kernel(ranks, pos, charge, species, neighbors, out):
+    dims, beads, width = pos.shape
     spec = species[...].astype(F32)
     near = neighbors[...].astype(F32)
     pad = jnp.zeros((3, width), F32)
     blocks = [
-        jnp.concatenate([pos[b], charge[b : b + 1, :], spec, pad], 0) for b in range(beads)
+        jnp.concatenate([pos[d, b : b + 1, :] for d in range(dims)] + [charge[b : b + 1, :], spec, pad], 0)
+        for b in range(beads)
     ]
     for rank in range(ranks):
         out[rank, 0:8, :] = near
         out[rank, 8:16, :] = blocks[rank % beads]
-    edges[0] = pos[0]
-    edges[1] = pos[beads - 1]
-
-
-def weight_kernel(k_index, kernel, out):
+
+
+def weight_kernel(k_index, kernel, pos, after, out, edges):
+    del after
+    dims, beads, _ = pos.shape
+    for d in range(dims):
+        edges[d : d + 1, :] = pos[d, 0:1, :]
+        edges[dims + d : dims + d + 1, :] = pos[d, beads - 1 : beads, :]
     count = k_index.shape[1]
     k = k_index[...]
     first, second, third = k[0:1], k[1:2], k[2:3]
@@ -131,20 +141,29 @@
     beads,
     rank_ref,
     got,
-    weights,
+    weights_hbm,
+    edges,
     chi_table,
     hard_table,
     bond_table,
-    out,
-    cos_high,
-    cos_low,
-    sin_high,
-    sin_low,
-    left,
-    z_cos,
-    z_sin,
-    charges,
+    *refs,
 ):
+    outs = refs[:beads]
+    (
+        cos_high,
+        cos_low,
+        sin_high,
+        sin_low,
+        left,
+        z_cos,
+        z_sin,
+        charges,
+        weights,
+        mine,
+        arrived,
+    ) = refs[beads:]
+    bring = pltpu.make_async_copy(weights_hbm, weights, arrived)
+    bring.start()
     ranks, _, width = got.shape
     lane = lax.broadcasted_iota(jnp.int32, (8, width), 1)
     row = lax.broadcasted_iota(jnp.int32, (8, width), 0)
@@ -203,6 +222,7 @@
         bond.append(b)
         charge.append(everywhere(got[j, 11:12, :]))
 
+    bring.wait()
     even, odd, zero = weights[0:8, :], weights[8:16, :], weights[16:24, :]
 
     def coefficients(charge):
@@ -287,28 +307,42 @@
         fx, fy, fz = (
             factor[:, cut] * column_sum(f[:, cut]) for f in (along_x, along_y, along_z)
         )
-        out[t] = jnp.where(row == 0, fx, jnp.where(row == 1, fy, jnp.where(row == 2, fz, q[:, cut])))
-
-
-def move_kernel(low_at, high_at, pos, vel, got, low, high, species, mass_table, pos_out, vel_out, charge_out):
-    beads, dims, width = pos.shape
-    kinds = jnp.broadcast_to(species[...], (dims, width))
-    mass = jnp.zeros((dims, width), F32)
+        mine[:, cut] = jnp.where(
+            row == 0, fx, jnp.where(row == 1, fy, jnp.where(row == 2, fz, q[:, cut]))
+        )
+    me = rank_ref[0] % beads
+    for t in range(beads):
+        there = pl.multiple_of(partner(me, t, beads) * width, width)
+        outs[t][...] = mine[0:4, pl.ds(there, width)]
+
+
+def move_kernel(low_at, high_at, rank_ref, pos, vel, low, high, species, mass_table, *refs):
+    dims, beads, width = pos.shape
+    got, (pos_out, vel_out, charge_out, home) = refs[:beads], refs[beads:]
+    me = rank_ref[0] % beads
+    for t in range(beads):
+        bead = partner(me, -t, beads)
+        for d in range(dims + 1):
+            home[pl.ds(d * beads + bead, 1), :] = got[t][d : d + 1, :]
+    kinds = jnp.broadcast_to(species[...], (beads, width))
+    mass = jnp.zeros((beads, width), F32)
     for kind in range(SPECIES):
         mass = jnp.where(kinds == kind, mass_table[kind], mass)
-    for b in range(beads):
-        here = pos[b]
-        before = pos[b - 1] if b > 0 else low[low_at]
-        after = pos[b + 1] if b < beads - 1 else high[high_at]
+    for d in range(dims):
+        here = pos[d]
+        before = jnp.concatenate([low[low_at + d : low_at + d + 1, :], here[: beads - 1]], 0)
+        after = jnp.concatenate([here[1:], high[high_at + d : high_at + d + 1, :]], 0)
         laplace = 2.0 * here - before - after
-        fresh = vel[b] + time_step * (got[b, 0:3, :] / mass - spring_rate * laplace)
-        vel_out[b] = fresh
-        pos_out[b] = here + time_step * fresh
-        charge_out[b : b + 1, :] = got[b, 3:4, :]
+        force = home[d * beads : (d + 1) * beads, :]
+        fresh = vel[d] + time_step * (force / mass - spring_rate * laplace)
+        vel_out[d] = fresh
+        pos_out[d] = here + time_step * fresh
+    charge_out[...] = home[dims * beads : (dims + 1) * beads, :]
 
 
 VMEM = pl.BlockSpec(memory_space=pltpu.VMEM)
 SMEM = pl.BlockSpec(memory_space=pltpu.SMEM)
+ANY = pl.BlockSpec(memory_space=pl.ANY)
 
 
 def body(
@@ -332,38 +366,41 @@
     kinds = species[None, :]
     shape = jax.ShapeDtypeStruct
 
-    packed, edges = pl.pallas_call(
+    places = positions.transpose(1, 0, 2)
+    speeds = velocities.transpose(1, 0, 2)
+
+    packed = pl.pallas_call(
         functools.partial(pack_kernel, ranks),
-        out_shape=(shape((ranks, 16, width), F32), shape((2, dims, width), F32)),
+        out_shape=shape((ranks, 16, width), F32),
         in_specs=[VMEM] * 4,
+        out_specs=VMEM,
+        name="pack",
+    )(places, charges_in, kinds, neighbors)
+    got = lax.all_to_all(packed, "atoms", 0, 0, tiled=True)
+
+    weights, edges = pl.pallas_call(
+        weight_kernel,
+        out_shape=(shape((24, MODES), F32), shape((2 * dims, width), F32)),
+        in_specs=[VMEM] * 3 + [ANY],
         out_specs=(VMEM, VMEM),
-        name="pack",
-    )(positions, charges_in, kinds, neighbors)
+        name="weights",
+        cost_estimate=pl.CostEstimate(flops=10**9, bytes_accessed=10**5, transcendentals=0),
+    )(k_index, kernel[None, :], places, packed)
     if chain == 2:
         low = high = lax.ppermute(edges, "beads", [(0, 1), (1, 0)])
-        low_at, high_at = 1, 0
+        low_at, high_at = dims, 0
     else:
         forward = [(i, (i + 1) % chain) for i in range(chain)]
-        low = lax.ppermute(edges[1:2], "beads", forward)
-        high = lax.ppermute(edges[0:1], "beads", [(b, a) for a, b in forward])
+        low = lax.ppermute(edges[dims:], "beads", forward)
+        high = lax.ppermute(edges[:dims], "beads", [(b, a) for a, b in forward])
         low_at, high_at = 0, 0
-    got = lax.all_to_all(packed, "atoms", 0, 0, tiled=True)
-
-    weights = pl.pallas_call(
-        weight_kernel,
-        out_shape=shape((24, MODES), F32),
-        in_specs=[VMEM] * 2,
-        out_specs=VMEM,
-        name="weights",
-        cost_estimate=pl.CostEstimate(flops=10**9, bytes_accessed=10**5, transcendentals=0),
-    )(k_index, kernel[None, :])
 
     rank = lax.axis_index("atoms").astype(jnp.int32)[None]
-    result = pl.pallas_call(
+    results = pl.pallas_call(
         functools.partial(bead_kernel, scale, 1.0 / atoms, beads),
-        out_shape=shape((beads, 8, width), F32),
-        in_specs=[SMEM, VMEM, VMEM, SMEM, SMEM, SMEM],
-        out_specs=VMEM,
+        out_shape=[shape((4, width), F32)] * beads,
+        in_specs=[SMEM, VMEM, ANY, ANY, SMEM, SMEM, SMEM],
+        out_specs=[VMEM] * beads,
         scratch_shapes=[
             pltpu.VMEM((MODES, atoms), BF16),
             pltpu.VMEM((MODES, atoms), BF16),
@@ -373,25 +410,32 @@
             pltpu.VMEM((8, atoms), F32),
             pltpu.VMEM((8, atoms), F32),
             pltpu.VMEM((8, atoms), F32),
+            pltpu.VMEM((24, MODES), F32),
+            pltpu.VMEM((8, beads * width), F32),
+            pltpu.SemaphoreType.DMA,
         ],
         compiler_params=pltpu.CompilerParams(vmem_limit_bytes=32 * 1024 * 1024),
         name="bead",
-    )(rank, got, weights, chi_table, hard_table, bond_table)
-
-    groups = [list(range(g, g + beads)) for g in range(0, ranks, beads)]
-    home = lax.all_to_all(result, "atoms", 0, 0, axis_index_groups=groups, tiled=True)
-
-    return pl.pallas_call(
+    )(rank, got, weights, low, chi_table, hard_table, bond_table)
+
+    home = [results[0]]
+    for t in range(1, beads):
+        pairs = [(r, r // beads * beads + partner(r % beads, t, beads)) for r in range(ranks)]
+        home.append(lax.ppermute(results[t], "atoms", pairs))
+
+    new_places, new_speeds, charge = pl.pallas_call(
         functools.partial(move_kernel, low_at, high_at),
         out_shape=(
-            shape(positions.shape, F32),
-            shape(positions.shape, F32),
+            shape(places.shape, F32),
+            shape(places.shape, F32),
             shape(charges_in.shape, F32),
         ),
-        in_specs=[VMEM] * 6 + [SMEM],
+        in_specs=[SMEM] + [VMEM] * 5 + [SMEM] + [VMEM] * beads,
         out_specs=(VMEM, VMEM, VMEM),
+        scratch_shapes=[pltpu.VMEM(((dims + 1) * beads, width), F32)],
         name="move",
-    )(positions, velocities, home, low, high, kinds, mass_table)
+    )(rank, places, speeds, low, high, kinds, mass_table, *home)
+    return new_places.transpose(1, 0, 2), new_speeds.transpose(1, 0, 2), charge
 
 
 def solution(mesh):

time: 37.7 us -> 30.9 us (0.82)
  local copies, waits for them, and re-layouts: 5.6 us -> 2.44 us
  starting transfers between devices: 12.3 us -> 10.4 us
  waiting for transfers between devices: 7.84 us -> 6.47 us
    all_to_all x1, waiting for transfers between devices: 6.22 us -> 2.39 us  [body(): got = lax.all_to_all(packed, 'atoms', 0, 0, tiled=True)]
    all_to_all x1 -> x0, starting transfers between devices: 3.37 us -> none  [body(): lax.all_to_all(result, 'atoms', 0, 0, axis_index_groups=groups, tiled=True)]
    pallas_call x2 -> x0, local copies, waits for them, and re-layouts: 1.9 us -> none  [body(): pl.pallas_call(functools.partial(move_kernel, low_at, high_at), out_shape...]
    ppermute x0 -> x3, waiting for transfers between devices: none -> 1.79 us  [body(): home.append(lax.ppermute(results[t], 'atoms', pairs))]
    ppermute x0 -> x3, starting transfers between devices: none -> 1.5 us  [body(): home.append(lax.ppermute(results[t], 'atoms', pairs))]
    unnamed x20 -> x18, local copies, waits for them, and re-layouts: 3.7 us -> 2.44 us
    ppermute x1, waiting for transfers between devices: 1.49 us -> 2.3 us  [body(): low = high = lax.ppermute(edges, 'beads', [(0, 1), (1, 0)])]
  transfers between devices with their start and end apart: 3 -> 5, of which waited for: 3 -> 3; matrix products, arithmetic and copies ran while one was open for 2% -> 0% of each run, Pallas kernels for 5% -> 6%
where the time goes in v2:
time: 30.9 us; the launch traced here: 30.5 us
  Pallas kernels  10.5 us (34%)
  starting transfers between devices  10.4 us (34%)
  waiting for transfers between devices  6.47 us (21%)
  local copies, waits for them, and re-layouts  2.44 us (8%)
  between operations  0.69 us (2%)
    all_to_all x1, starting transfers between devices, body(): got = lax.all_to_all(packed, 'atoms', 0, 0, tiled=True)  7.36 us
    pallas_call x1, Pallas kernels, body(): pl.pallas_call(functools.partial(bead_kernel, scale, 1.0 / atoms, beads),...  5.98 us
    unnamed x18, local copies, waits for them, and re-layouts  2.44 us
    all_to_all x1, waiting for transfers between devices, body(): got = lax.all_to_all(packed, 'atoms', 0, 0, tiled=True)  2.39 us
    ppermute x1, waiting for transfers between devices, body(): low = high = lax.ppermute(edges, 'beads', [(0, 1), (1, 0)])  2.3 us
    ppermute x3, waiting for transfers between devices, body(): home.append(lax.ppermute(results[t], 'atoms', pairs))  1.79 us
    pallas_call x1, Pallas kernels, body(): pl.pallas_call(weight_kernel, out_shape=(shape((24, MODES), F32), shape((...  1.73 us
    ppermute x1, starting transfers between devices, body(): low = high = lax.ppermute(edges, 'beads', [(0, 1), (1, 0)])  1.52 us
  transfers between devices with their start and end apart: 5, of which 3 were waited for; matrix products, arithmetic and copies ran while one was open for 0% of the time, Pallas kernels for 6%

profile of v2, /device:TPU:0, one launch (start us, length us, event | category | flops | bytes accessed | tf_op | source)
XLA Modules:
  0.0 30.5 jit_solution(730980116047135013)
XLA Ops:
  0.6 1.4 %pack.1.after = f32[16,16,128]{2,1,0:T(8,128)} custom-call(f32[3,4,128]{2,1,0:T(4,128)} %bitcast.7, f32[4,128]{1,0:T(4,128)} %charge.1, s32[1,128]{1,0:T(1,128)} %bitcast.11, s32[8,128]{1,0:T(8,128)} %neighbors.1), custom_call_target="tpu_custom_call" | custom-call | tf_op jit(solution)/shard_map/pack/pallas_call | solution.py:372
  2.0 7.4 %all-to-all-start = ((f32[16,16,128]{2,1,0:T(8,128)}), f32[16,16,128]{2,1,0:T(8,128)S(1)}, u32[]{:S(2)}, u32[]{:S(2)}) async-start(f32[16,16,128]{2,1,0:T(8,128)} %pack.1.after), calls=%async_computation | async-start | bytes 262144 | tf_op jit(solution)/shard_map/all_to_all | solution.py:379
  9.4 1.7 %weights.1 = (f32[24,160]{1,0:T(8,128)}, f32[6,128]{1,0:T(8,128)}) custom-call(s32[3,2048]{1,0:T(4,128)} %k_index.1, f32[1,2048]{1,0:T(1,128)} %bitcast.13, f32[3,4,128]{2,1,0:T(4,128)} %bitcast.8, f32[16,16,128]{2,1,0:T(8,128)} %pack.1.after), custom_call_target="tpu_custom_call" | custom-call | flops 1000000000 | bytes 100000 | tf_op jit(solution)/shard_map/weights/pallas_call | solution.py:381
  11.1 1.5 %collective-permute-start = (f32[6,128]{1,0:T(8,128)}, f32[6,128]{1,0:T(8,128)S(1)}, u32[]{:S(2)}, u32[]{:S(2)}) collective-permute-start(f32[6,128]{1,0:T(8,128)} %get-tuple-element.12), channel_id=1, source_target_pairs={{0,1},{1,0},{2,3},{3,2},{4,5},{5,4},{6,7},{7,6},{8,9},{9,8},{10,11... | collective-permute-start | bytes 9224 | tf_op jit(solution)/shard_map/ppermute | solution.py:390
  12.6 2.3 %collective-permute-done.edges.low.high = f32[6,128]{1,0:T(8,128)S(1)} collective-permute-done((f32[6,128]{1,0:T(8,128)}, f32[6,128]{1,0:T(8,128)S(1)}, u32[]{:S(2)}, u32[]{:S(2)}) %collective-permute-start) | collective-permute-done | bytes 3104 | tf_op jit(solution)/shard_map/ppermute | solution.py:390
  14.9 0.0 copy-start
  14.9 2.4 %all-to-all-done.got = f32[16,16,128]{2,1,0:T(8,128)S(1)} async-done(((f32[16,16,128]{2,1,0:T(8,128)}), f32[16,16,128]{2,1,0:T(8,128)S(1)}, u32[]{:S(2)}, u32[]{:S(2)}) %all-to-all-start) | async-done | bytes 131104 | tf_op jit(solution)/shard_map/all_to_all | solution.py:379
  17.3 0.0 copy-start.3
  17.3 0.0 copy-start.4
  17.3 0.0 copy-start.5
  17.3 0.6 %copy-done.3 = f32[8]{0:T(128)S(1)} copy-done((f32[8]{0:T(128)S(1)}, f32[8]{0:T(128)}, u32[]{:S(2)}) %copy-start.3) | copy-done | bytes 56
  18.0 0.0 copy-done.4
  18.0 0.0 copy-done.5
  18.0 0.0 copy-start.1
  18.0 0.7 %copy-done.1 = f32[24,160]{1,0:T(8,128)S(1)} copy-done((f32[24,160]{1,0:T(8,128)S(1)}, f32[24,160]{1,0:T(8,128)}, u32[]{:S(2)}) %copy-start.1) | copy-done | bytes 15384
  18.8 6.0 %bead.1 = (f32[4,128]{1,0:T(4,128)S(1)}, f32[4,128]{1,0:T(4,128)S(1)}, f32[4,128]{1,0:T(4,128)S(1)}, f32[4,128]{1,0:T(4,128)S(1)}) custom-call(s32[1]{0:T(128)} %bitcast.rank_ref, f32[16,16,128]{2,1,0:T(8,128)S(1)} %all-to-all-done.got, f32[24,160]{1,0:T(8,128)S(1)} %copy-done.1, f32[6,128]{1,0:T(8,128)S(1)} %collective-permute-done.edges.low.high, ...), custom_call_target="tpu_custom_call" | custom-call | tf_op jit(solution)/shard_map/bead/pallas_call | solution.py:399
  24.8 0.0 copy-done
  24.8 0.0 copy-start.2
  24.8 0.1 collective-permute-start.1
  24.8 0.1 collective-permute-start.2
  24.9 0.4 %copy-done.2 = f32[4,128]{1,0:T(4,128)} copy-done((f32[4,128]{1,0:T(4,128)}, f32[4,128]{1,0:T(4,128)S(1)}, u32[]{:S(2)}) %copy-start.2) | copy-done | bytes 2072
  25.4 1.4 %collective-permute-start.3 = (f32[4,128]{1,0:T(4,128)S(1)}, f32[4,128]{1,0:T(4,128)S(1)}, u32[]{:S(2)}, u32[]{:S(2)}) collective-permute-start(f32[4,128]{1,0:T(4,128)S(1)} %get-tuple-element.17), channel_id=1, source_target_pairs={{0,6},{2,4},{4,2},{6,0},{8,14},{10,12},{12,10},{14,8},{16,22},{18,... | collective-permute-start | bytes 6152 | tf_op jit(solution)/shard_map/ppermute | solution.py:424
  26.7 0.0 collective-permute-done.1.refs_1_
  26.7 0.0 copy-start.6
  26.7 1.8 %collective-permute-done.2.refs_2_ = f32[4,128]{1,0:T(4,128)S(1)} collective-permute-done((f32[4,128]{1,0:T(4,128)S(1)}, f32[4,128]{1,0:T(4,128)S(1)}, u32[]{:S(2)}, u32[]{:S(2)}) %collective-permute-start.2) | collective-permute-done | bytes 2080 | tf_op jit(solution)/shard_map/ppermute | solution.py:424
  28.5 0.0 copy-start.7
  28.5 0.0 collective-permute-done.3.refs_3_
  28.5 0.0 copy-start.8
  28.5 0.0 copy-done.6
  28.5 0.6 %copy-done.7 = f32[4,128]{1,0:T(4,128)} copy-done((f32[4,128]{1,0:T(4,128)}, f32[4,128]{1,0:T(4,128)S(1)}, u32[]{:S(2)}) %copy-start.7) | copy-done | bytes 2072
  29.1 0.0 copy-done.8
  29.1 1.4 %move.1 = (f32[3,4,128]{2,1,0:T(4,128)}, f32[3,4,128]{2,1,0:T(4,128)}, f32[4,128]{1,0:T(4,128)}) custom-call(s32[1]{0:T(128)} %bitcast.rank_ref, f32[3,4,128]{2,1,0:T(4,128)} %bitcast.9, f32[3,4,128]{2,1,0:T(4,128)} %bitcast.10, f32[6,128]{1,0:T(8,128)} %copy-done, f32[6,128]{1,0:T(8,128)} %copy-done, s32[1,128]{1,0:T(1,128)} %bitcast.12, f32[8]{0:T(128)} %mass_table.1, ...), custom_call_target="tpu_custom_call" | custom-call | tf_op jit(solution)/shard_map/move/pallas_call | solution.py:426
Async XLA Ops:
  2.0 15.3 %all-to-all-start = ((f32[16,16,128]{2,1,0:T(8,128)}), f32[16,16,128]{2,1,0:T(8,128)S(1)}, u32[]{:S(2)}, u32[]{:S(2)}) async-start(f32[16,16,128]{2,1,0:T(8,128)} %pack.1.after), calls=%async_computation | async-start | bytes 262144 | tf_op jit(solution)/shard_map/all_to_all | solution.py:379
  11.1 3.8 %collective-permute-start = (f32[6,128]{1,0:T(8,128)}, f32[6,128]{1,0:T(8,128)S(1)}, u32[]{:S(2)}, u32[]{:S(2)}) collective-permute-start(f32[6,128]{1,0:T(8,128)} %get-tuple-element.12), channel_id=1, source_target_pairs={{0,1},{1,0},{2,3},{3,2},{4,5},{5,4},{6,7},{7,6},{8,9},{9,8},{10,11... | collective-permute-start | bytes 9224 | tf_op jit(solution)/shard_map/ppermute | solution.py:390
  14.9 9.8 %copy-start = (f32[6,128]{1,0:T(8,128)}, f32[6,128]{1,0:T(8,128)S(1)}, u32[]{:S(2)}) copy-start(f32[6,128]{1,0:T(8,128)S(1)} %collective-permute-done.edges.low.high) | copy-start | bytes 9220
  17.3 0.7 %copy-start.3 = (f32[8]{0:T(128)S(1)}, f32[8]{0:T(128)}, u32[]{:S(2)}) copy-start(f32[8]{0:T(128)} %chi_table.1) | copy-start | bytes 100
  17.3 0.7 %copy-start.4 = (f32[8]{0:T(128)S(1)}, f32[8]{0:T(128)}, u32[]{:S(2)}) copy-start(f32[8]{0:T(128)} %hard_table.1) | copy-start | bytes 100
  17.3 0.7 %copy-start.5 = (f32[8]{0:T(128)S(1)}, f32[8]{0:T(128)}, u32[]{:S(2)}) copy-start(f32[8]{0:T(128)} %bond_table.1) | copy-start | bytes 100
  18.0 0.7 %copy-start.1 = (f32[24,160]{1,0:T(8,128)S(1)}, f32[24,160]{1,0:T(8,128)}, u32[]{:S(2)}) copy-start(f32[24,160]{1,0:T(8,128)} %get-tuple-element.13.weights_hbm) | copy-start | bytes 46084
  24.8 0.6 %copy-start.2 = (f32[4,128]{1,0:T(4,128)}, f32[4,128]{1,0:T(4,128)S(1)}, u32[]{:S(2)}) copy-start(f32[4,128]{1,0:T(4,128)S(1)} %get-tuple-element.14.refs_0_) | copy-start | bytes 6148
  24.8 1.9 %collective-permute-start.1 = (f32[4,128]{1,0:T(4,128)S(1)}, f32[4,128]{1,0:T(4,128)S(1)}, u32[]{:S(2)}, u32[]{:S(2)}) collective-permute-start(f32[4,128]{1,0:T(4,128)S(1)} %get-tuple-element.15), channel_id=1, source_target_pairs={{0,2},{2,0},{4,6},{6,4},{8,10},{10,8},{12,14},{14,12},{16,18},{18,... | collective-permute-start | bytes 6152 | tf_op jit(solution)/shard_map/ppermute | solution.py:424
  24.8 3.7 %collective-permute-start.2 = (f32[4,128]{1,0:T(4,128)S(1)}, f32[4,128]{1,0:T(4,128)S(1)}, u32[]{:S(2)}, u32[]{:S(2)}) collective-permute-start(f32[4,128]{1,0:T(4,128)S(1)} %get-tuple-element.16), channel_id=1, source_target_pairs={{0,4},{2,6},{4,0},{6,2},{8,12},{10,14},{12,8},{14,10},{16,20},{18,... | collective-permute-start | bytes 6152 | tf_op jit(solution)/shard_map/ppermute | solution.py:424
  25.4 3.2 %collective-permute-start.3 = (f32[4,128]{1,0:T(4,128)S(1)}, f32[4,128]{1,0:T(4,128)S(1)}, u32[]{:S(2)}, u32[]{:S(2)}) collective-permute-start(f32[4,128]{1,0:T(4,128)S(1)} %get-tuple-element.17), channel_id=1, source_target_pairs={{0,6},{2,4},{4,2},{6,0},{8,14},{10,12},{12,10},{14,8},{16,22},{18,... | collective-permute-start | bytes 6152 | tf_op jit(solution)/shard_map/ppermute | solution.py:424
  26.7 1.8 %copy-start.6 = (f32[4,128]{1,0:T(4,128)}, f32[4,128]{1,0:T(4,128)S(1)}, u32[]{:S(2)}) copy-start(f32[4,128]{1,0:T(4,128)S(1)} %collective-permute-done.1.refs_1_) | copy-start | bytes 6148
  28.5 0.6 %copy-start.7 = (f32[4,128]{1,0:T(4,128)}, f32[4,128]{1,0:T(4,128)S(1)}, u32[]{:S(2)}) copy-start(f32[4,128]{1,0:T(4,128)S(1)} %collective-permute-done.2.refs_2_) | copy-start | bytes 6148
  28.5 0.6 %copy-start.8 = (f32[4,128]{1,0:T(4,128)}, f32[4,128]{1,0:T(4,128)S(1)}, u32[]{:S(2)}) copy-start(f32[4,128]{1,0:T(4,128)S(1)} %collective-permute-done.3.refs_3_) | copy-start | bytes 6148

commit v3 on v2

--- a/solution.py
+++ b/solution.py
@@ -91,18 +91,25 @@
     return (me + t + count) % count
 
 
-def pack_kernel(ranks, pos, charge, species, neighbors, out):
+def lookup(tables, kinds):
+    found = [jnp.zeros(kinds.shape, F32) for _ in tables]
+    for kind in range(SPECIES):
+        here = kinds == kind
+        found = [jnp.where(here, table[kind], x) for table, x in zip(tables, found)]
+    return found
+
+
+def pack_kernel(ranks, pos, charge, species, neighbors, chi_table, hard_table, bond_table, out):
     dims, beads, width = pos.shape
-    spec = species[...].astype(F32)
     near = neighbors[...].astype(F32)
-    pad = jnp.zeros((3, width), F32)
-    blocks = [
-        jnp.concatenate([pos[d, b : b + 1, :] for d in range(dims)] + [charge[b : b + 1, :], spec, pad], 0)
-        for b in range(beads)
-    ]
-    for rank in range(ranks):
-        out[rank, 0:8, :] = near
-        out[rank, 8:16, :] = blocks[rank % beads]
+    chi, hard, bond = lookup((chi_table, hard_table, bond_table), species[...])
+    shared = [chi, mixing / hard, bond, jnp.zeros((1, width), F32)]
+    for b in range(beads):
+        own = [pos[d, b : b + 1, :] for d in range(dims)] + [charge[b : b + 1, :]]
+        block = jnp.concatenate(own + shared, 0)
+        for rank in range(b, ranks, beads):
+            out[rank, 0:8, :] = near
+            out[rank, 8:16, :] = block
 
 
 def weight_kernel(k_index, kernel, pos, after, out, edges):
@@ -142,10 +149,6 @@
     rank_ref,
     got,
     weights_hbm,
-    edges,
-    chi_table,
-    hard_table,
-    bond_table,
     *refs,
 ):
     outs = refs[:beads]
@@ -210,17 +213,10 @@
             jnp.concatenate([single, blank], 0),
             jnp.concatenate([blank, blank], 0),
         )
-        species = everywhere(got[j, 12:13, :])
-        c, h, b = blank, blank, blank
-        for kind in range(SPECIES):
-            this = species == float(kind)
-            c = jnp.where(this, chi_table[kind], c)
-            h = jnp.where(this, hard_table[kind], h)
-            b = jnp.where(this, bond_table[kind], b)
-        chi.append(c)
-        hard.append(mixing / h)
-        bond.append(b)
         charge.append(everywhere(got[j, 11:12, :]))
+        chi.append(everywhere(got[j, 12:13, :]))
+        hard.append(everywhere(got[j, 13:14, :]))
+        bond.append(everywhere(got[j, 14:15, :]))
 
     bring.wait()
     even, odd, zero = weights[0:8, :], weights[8:16, :], weights[16:24, :]
@@ -324,10 +320,7 @@
         bead = partner(me, -t, beads)
         for d in range(dims + 1):
             home[pl.ds(d * beads + bead, 1), :] = got[t][d : d + 1, :]
-    kinds = jnp.broadcast_to(species[...], (beads, width))
-    mass = jnp.zeros((beads, width), F32)
-    for kind in range(SPECIES):
-        mass = jnp.where(kinds == kind, mass_table[kind], mass)
+    (mass,) = lookup((mass_table,), jnp.broadcast_to(species[...], (beads, width)))
     for d in range(dims):
         here = pos[d]
         before = jnp.concatenate([low[low_at + d : low_at + d + 1, :], here[: beads - 1]], 0)
@@ -343,6 +336,10 @@
 VMEM = pl.BlockSpec(memory_space=pltpu.VMEM)
 SMEM = pl.BlockSpec(memory_space=pltpu.SMEM)
 ANY = pl.BlockSpec(memory_space=pl.ANY)
+
+
+def params(mebibytes):
+    return pltpu.CompilerParams(vmem_limit_bytes=mebibytes << 20)
 
 
 def body(
@@ -372,10 +369,11 @@
     packed = pl.pallas_call(
         functools.partial(pack_kernel, ranks),
         out_shape=shape((ranks, 16, width), F32),
-        in_specs=[VMEM] * 4,
+        in_specs=[VMEM] * 4 + [SMEM] * 3,
         out_specs=VMEM,
+        compiler_params=params(4),
         name="pack",
-    )(places, charges_in, kinds, neighbors)
+    )(places, charges_in, kinds, neighbors, chi_table, hard_table, bond_table)
     got = lax.all_to_all(packed, "atoms", 0, 0, tiled=True)
 
     weights, edges = pl.pallas_call(
@@ -383,6 +381,7 @@
         out_shape=(shape((24, MODES), F32), shape((2 * dims, width), F32)),
         in_specs=[VMEM] * 3 + [ANY],
         out_specs=(VMEM, VMEM),
+        compiler_params=params(8),
         name="weights",
         cost_estimate=pl.CostEstimate(flops=10**9, bytes_accessed=10**5, transcendentals=0),
     )(k_index, kernel[None, :], places, packed)
@@ -399,7 +398,7 @@
     results = pl.pallas_call(
         functools.partial(bead_kernel, scale, 1.0 / atoms, beads),
         out_shape=[shape((4, width), F32)] * beads,
-        in_specs=[SMEM, VMEM, ANY, ANY, SMEM, SMEM, SMEM],
+        in_specs=[SMEM, VMEM, ANY],
         out_specs=[VMEM] * beads,
         scratch_shapes=[
             pltpu.VMEM((MODES, atoms), BF16),
@@ -414,9 +413,10 @@
             pltpu.VMEM((8, beads * width), F32),
             pltpu.SemaphoreType.DMA,
         ],
-        compiler_params=pltpu.CompilerParams(vmem_limit_bytes=32 * 1024 * 1024),
+        compiler_params=params(24),
         name="bead",
-    )(rank, got, weights, low, chi_table, hard_table, bond_table)
+        cost_estimate=pl.CostEstimate(flops=10**10, bytes_accessed=10**6, transcendentals=0),
+    )(rank, got, weights)
 
     home = [results[0]]
     for t in range(1, beads):
@@ -433,6 +433,7 @@
         in_specs=[SMEM] + [VMEM] * 5 + [SMEM] + [VMEM] * beads,
         out_specs=(VMEM, VMEM, VMEM),
         scratch_shapes=[pltpu.VMEM(((dims + 1) * beads, width), F32)],
+        compiler_params=params(4),
         name="move",
     )(rank, places, speeds, low, high, kinds, mass_table, *home)
     return new_places.transpose(1, 0, 2), new_speeds.transpose(1, 0, 2), charge

time: 30.9 us -> 31.3 us (1.013)
  Pallas kernels: 10.5 us -> 8.06 us
  waiting for transfers between devices: 6.47 us -> 7.76 us
  local copies, waits for them, and re-layouts: 2.44 us -> 3.37 us
  starting transfers between devices: 10.4 us -> 11 us
    all_to_all x1, waiting for transfers between devices: 2.39 us -> 5.98 us  [body(): got = lax.all_to_all(packed, 'atoms', 0, 0, tiled=True)]
    ppermute x1, waiting for transfers between devices: 2.3 us -> 0.01 us  [body(): low = high = lax.ppermute(edges, 'beads', [(0, 1), (1, 0)])]
    pallas_call x1, Pallas kernels: 1.73 us -> 0.34 us  [body(): pl.pallas_call(weight_kernel, out_shape=(shape((24, MODES), F32), shape((...]
    unnamed x18 -> x24, local copies, waits for them, and re-layouts: 2.44 us -> 3.37 us
    pallas_call x1, Pallas kernels: 5.98 us -> 5.34 us  [body(): pl.pallas_call(functools.partial(bead_kernel, scale, 1.0 / atoms, beads),...]
    ppermute x3, starting transfers between devices: 1.5 us -> 1.93 us  [body(): home.append(lax.ppermute(results[t], 'atoms', pairs))]
  transfers between devices with their start and end apart: 5 -> 5, of which waited for: 3 -> 2; matrix products, arithmetic and copies ran while one was open for 0% -> 0% of each run, Pallas kernels for 6% -> 18%
where the time goes in v3:
time: 31.3 us; the launch traced here: 30.9 us
  starting transfers between devices  11 us (35%)
  Pallas kernels  8.06 us (26%)
  waiting for transfers between devices  7.76 us (25%)
  local copies, waits for them, and re-layouts  3.37 us (11%)
  between operations  0.75 us (2%)
    all_to_all x1, starting transfers between devices, body(): got = lax.all_to_all(packed, 'atoms', 0, 0, tiled=True)  7.49 us
    all_to_all x1, waiting for transfers between devices, body(): got = lax.all_to_all(packed, 'atoms', 0, 0, tiled=True)  5.98 us
    pallas_call x1, Pallas kernels, body(): pl.pallas_call(functools.partial(bead_kernel, scale, 1.0 / atoms, beads),...  5.34 us
    unnamed x24, local copies, waits for them, and re-layouts  3.37 us
    ppermute x3, starting transfers between devices, body(): home.append(lax.ppermute(results[t], 'atoms', pairs))  1.93 us
    ppermute x3, waiting for transfers between devices, body(): home.append(lax.ppermute(results[t], 'atoms', pairs))  1.79 us
    ppermute x1, starting transfers between devices, body(): low = high = lax.ppermute(edges, 'beads', [(0, 1), (1, 0)])  1.58 us
    pallas_call x1, Pallas kernels, body(): pl.pallas_call(functools.partial(pack_kernel, ranks), out_shape=shape((ra...  1.22 us
  transfers between devices with their start and end apart: 5, of which 2 were waited for; matrix products, arithmetic and copies ran while one was open for 0% of the time, Pallas kernels for 18%

profile of v3, /device:TPU:0, one launch (start us, length us, event | category | flops | bytes accessed | tf_op | source)
XLA Modules:
  0.0 30.9 jit_solution(5780151767512549654)
XLA Ops:
  0.6 0.0 copy-start.4
  0.6 0.0 copy-start.5
  0.7 0.0 copy-start.6
  0.7 0.0 copy-start.7
  0.7 0.6 %copy-done.4 = f32[4,128]{1,0:T(4,128)S(1)} copy-done((f32[4,128]{1,0:T(4,128)S(1)}, f32[4,128]{1,0:T(4,128)}, u32[]{:S(2)}) %copy-start.4) | copy-done | bytes 2072
  1.3 0.0 copy-done.5
  1.3 0.0 copy-done.6
  1.3 0.0 copy-done.7
  1.3 0.0 copy-start
  1.3 0.7 %copy-done = f32[4,3,128]{2,0,1:T(4,128)S(1)} copy-done((f32[4,3,128]{2,0,1:T(4,128)S(1)}, f32[4,3,128]{2,0,1:T(4,128)}, u32[]{:S(2)}) %copy-start) | copy-done | bytes 6168
  2.0 0.0 copy-start.3
  2.0 0.7 %copy-done.3 = s32[8,128]{1,0:T(8,128)S(1)} copy-done((s32[8,128]{1,0:T(8,128)S(1)}, s32[8,128]{1,0:T(8,128)}, u32[]{:S(2)}) %copy-start.3) | copy-done | bytes 4120
  2.7 0.0 copy-start.8
  2.7 0.7 %copy-done.8 = f32[8]{0:T(128)S(1)} copy-done((f32[8]{0:T(128)S(1)}, f32[8]{0:T(128)}, u32[]{:S(2)}) %copy-start.8) | copy-done | bytes 56
  3.4 1.2 %pack.1.after = f32[16,16,128]{2,1,0:T(8,128)} custom-call(f32[3,4,128]{2,1,0:T(4,128)S(1)} %bitcast.7, f32[4,128]{1,0:T(4,128)S(1)} %copy-done.4, s32[1,128]{1,0:T(1,128)S(1)} %bitcast.11, s32[8,128]{1,0:T(8,128)S(1)} %copy-done.3, f32[8]{0:T(128)S(1)} %copy-done.6, f32[8]{0:T(128)S(1)} %copy-done.7, f32[8]{0:T(128)S(1)} %copy-done.8), custom_call_target="tpu_custom_call" | custom-call | tf_op jit(solution)/shard_map/pack/pallas_call | solution.py:369
  4.6 0.0 copy-start.1
  4.6 0.0 copy-start.10
  4.6 0.0 copy-start.11
  4.6 7.5 %all-to-all-start = ((f32[16,16,128]{2,1,0:T(8,128)}), f32[16,16,128]{2,1,0:T(8,128)S(1)}, u32[]{:S(2)}, u32[]{:S(2)}) async-start(f32[16,16,128]{2,1,0:T(8,128)} %pack.1.after), calls=%async_computation | async-start | bytes 262144 | tf_op jit(solution)/shard_map/all_to_all | solution.py:377
  12.1 0.0 copy-done.1
  12.1 0.0 copy-done.10
  12.1 0.0 copy-done.11
  12.1 0.3 %weights.1 = (f32[24,160]{1,0:T(8,128)S(1)}, f32[6,128]{1,0:T(8,128)S(1)}) custom-call(s32[3,2048]{1,0:T(4,128)S(1)} %copy-done.10, f32[1,2048]{1,0:T(1,128)S(1)} %bitcast.13, f32[3,4,128]{2,1,0:T(4,128)S(1)} %bitcast.8, f32[16,16,128]{2,1,0:T(8,128)} %pack.1.after), custom_call_target="tpu_custom_call" | custom-call | flops 1000000000 | bytes 100000 | tf_op jit(solution)/shard_map/weights/pallas_call | solution.py:379
  12.5 1.6 %collective-permute-start = (f32[6,128]{1,0:T(8,128)S(1)}, f32[6,128]{1,0:T(8,128)S(1)}, u32[]{:S(2)}, u32[]{:S(2)}) collective-permute-start(f32[6,128]{1,0:T(8,128)S(1)} %get-tuple-element.12), channel_id=1, source_target_pairs={{0,1},{1,0},{2,3},{3,2},{4,5},{5,4},{6,7},{7,6},{8,9},{9,8},{10,11... | collective-permute-start | bytes 9224 | tf_op jit(solution)/shard_map/ppermute | solution.py:389
  14.1 6.0 %all-to-all-done.got = f32[16,16,128]{2,1,0:T(8,128)S(1)} async-done(((f32[16,16,128]{2,1,0:T(8,128)}), f32[16,16,128]{2,1,0:T(8,128)S(1)}, u32[]{:S(2)}, u32[]{:S(2)}) %all-to-all-start) | async-done | bytes 131104 | tf_op jit(solution)/shard_map/all_to_all | solution.py:377
  20.0 5.3 %bead.1 = (f32[4,128]{1,0:T(4,128)S(1)}, f32[4,128]{1,0:T(4,128)S(1)}, f32[4,128]{1,0:T(4,128)S(1)}, f32[4,128]{1,0:T(4,128)S(1)}) custom-call(s32[1]{0:T(128)} %bitcast.rank_ref, f32[16,16,128]{2,1,0:T(8,128)S(1)} %all-to-all-done.got, f32[24,160]{1,0:T(8,128)S(1)} %get-tuple-element.13.weights_hbm), custom_call_target="tpu_custom_call" | custom-call | flops 10000000000 | bytes 1000000 | tf_op jit(solution)/shard_map/bead/pallas_call | solution.py:398
  25.4 0.0 copy-start.2
  25.4 0.1 collective-permute-start.1
  25.5 0.1 collective-permute-start.2
  25.6 1.8 %collective-permute-start.3 = (f32[4,128]{1,0:T(4,128)S(1)}, f32[4,128]{1,0:T(4,128)S(1)}, u32[]{:S(2)}, u32[]{:S(2)}) collective-permute-start(f32[4,128]{1,0:T(4,128)S(1)} %get-tuple-element.17), channel_id=1, source_target_pairs={{0,6},{2,4},{4,2},{6,0},{8,14},{10,12},{12,10},{14,8},{16,22},{18,... | collective-permute-start | bytes 6152 | tf_op jit(solution)/shard_map/ppermute | solution.py:424
  27.3 0.0 collective-permute-done.low.high
  27.3 0.0 collective-permute-done.1.refs_1_
  27.3 1.8 %collective-permute-done.2.refs_2_ = f32[4,128]{1,0:T(4,128)S(1)} collective-permute-done((f32[4,128]{1,0:T(4,128)S(1)}, f32[4,128]{1,0:T(4,128)S(1)}, u32[]{:S(2)}, u32[]{:S(2)}) %collective-permute-start.2) | collective-permute-done | bytes 2080 | tf_op jit(solution)/shard_map/ppermute | solution.py:424
  29.1 0.0 collective-permute-done.3.refs_3_
  29.1 0.0 copy-start.9
  29.1 0.0 copy-done.2
  29.1 0.6 %copy-done.9 = f32[8]{0:T(128)S(1)} copy-done((f32[8]{0:T(128)S(1)}, f32[8]{0:T(128)}, u32[]{:S(2)}) %copy-start.9) | copy-done | bytes 56
  29.8 1.2 %move.1 = (f32[3,4,128]{2,1,0:T(4,128)}, f32[3,4,128]{2,1,0:T(4,128)}, f32[4,128]{1,0:T(4,128)}) custom-call(s32[1]{0:T(128)} %bitcast.rank_ref, f32[3,4,128]{2,1,0:T(4,128)S(1)} %bitcast.9, f32[3,4,128]{2,1,0:T(4,128)S(1)} %bitcast.10, f32[6,128]{1,0:T(8,128)S(1)} %collective-permute-done.low.high, f32[6,128]{1,0:T(8,128)S(1)} %collective-permute-done.low.high, ...), custom_call_target="tpu_custom_call" | custom-call | tf_op jit(solution)/shard_map/move/pallas_call | solution.py:426
Async XLA Ops:
  0.6 0.7 %copy-start.4 = (f32[4,128]{1,0:T(4,128)S(1)}, f32[4,128]{1,0:T(4,128)}, u32[]{:S(2)}) copy-start(f32[4,128]{1,0:T(4,128)} %charge.1) | copy-start | bytes 6148
  0.6 0.7 %copy-start.5 = (s32[128]{0:T(128)S(1)}, s32[128]{0:T(128)}, u32[]{:S(2)}) copy-start(s32[128]{0:T(128)} %param.14) | copy-start | bytes 1540
  0.7 0.7 %copy-start.6 = (f32[8]{0:T(128)S(1)}, f32[8]{0:T(128)}, u32[]{:S(2)}) copy-start(f32[8]{0:T(128)} %chi_table.1) | copy-start | bytes 100
  0.7 0.7 %copy-start.7 = (f32[8]{0:T(128)S(1)}, f32[8]{0:T(128)}, u32[]{:S(2)}) copy-start(f32[8]{0:T(128)} %hard_table.1) | copy-start | bytes 100
  1.3 0.7 %copy-start = (f32[4,3,128]{2,0,1:T(4,128)S(1)}, f32[4,3,128]{2,0,1:T(4,128)}, u32[]{:S(2)}) copy-start(f32[4,3,128]{2,0,1:T(4,128)} %param.11) | copy-start | bytes 18436
  2.0 0.7 %copy-start.3 = (s32[8,128]{1,0:T(8,128)S(1)}, s32[8,128]{1,0:T(8,128)}, u32[]{:S(2)}) copy-start(s32[8,128]{1,0:T(8,128)} %neighbors.1) | copy-start | bytes 12292
  2.7 0.7 %copy-start.8 = (f32[8]{0:T(128)S(1)}, f32[8]{0:T(128)}, u32[]{:S(2)}) copy-start(f32[8]{0:T(128)} %bond_table.1) | copy-start | bytes 100
  4.6 7.5 %copy-start.1 = (f32[4,3,128]{2,0,1:T(4,128)S(1)}, f32[4,3,128]{2,0,1:T(4,128)}, u32[]{:S(2)}) copy-start(f32[4,3,128]{2,0,1:T(4,128)} %param.11) | copy-start | bytes 18436
  4.6 7.5 %copy-start.10 = (s32[3,2048]{1,0:T(4,128)S(1)}, s32[3,2048]{1,0:T(4,128)}, u32[]{:S(2)}) copy-start(s32[3,2048]{1,0:T(4,128)} %k_index.1) | copy-start | bytes 73732
  4.6 7.5 %copy-start.11 = (f32[2048]{0:T(1024)S(1)}, f32[2048]{0:T(1024)}, u32[]{:S(2)}) copy-start(f32[2048]{0:T(1024)} %param.17) | copy-start | bytes 24580
  4.6 15.4 %all-to-all-start = ((f32[16,16,128]{2,1,0:T(8,128)}), f32[16,16,128]{2,1,0:T(8,128)S(1)}, u32[]{:S(2)}, u32[]{:S(2)}) async-start(f32[16,16,128]{2,1,0:T(8,128)} %pack.1.after), calls=%async_computation | async-start | bytes 262144 | tf_op jit(solution)/shard_map/all_to_all | solution.py:377
  12.5 14.9 %collective-permute-start = (f32[6,128]{1,0:T(8,128)S(1)}, f32[6,128]{1,0:T(8,128)S(1)}, u32[]{:S(2)}, u32[]{:S(2)}) collective-permute-start(f32[6,128]{1,0:T(8,128)S(1)} %get-tuple-element.12), channel_id=1, source_target_pairs={{0,1},{1,0},{2,3},{3,2},{4,5},{5,4},{6,7},{7,6},{8,9},{9,8},{10,11... | collective-permute-start | bytes 9224 | tf_op jit(solution)/shard_map/ppermute | solution.py:389
  25.4 3.7 %copy-start.2 = (f32[4,3,128]{2,0,1:T(4,128)S(1)}, f32[4,3,128]{2,0,1:T(4,128)}, u32[]{:S(2)}) copy-start(f32[4,3,128]{2,0,1:T(4,128)} %param.12) | copy-start | bytes 18436
  25.4 1.9 %collective-permute-start.1 = (f32[4,128]{1,0:T(4,128)S(1)}, f32[4,128]{1,0:T(4,128)S(1)}, u32[]{:S(2)}, u32[]{:S(2)}) collective-permute-start(f32[4,128]{1,0:T(4,128)S(1)} %get-tuple-element.15), channel_id=1, source_target_pairs={{0,2},{2,0},{4,6},{6,4},{8,10},{10,8},{12,14},{14,12},{16,18},{18,... | collective-permute-start | bytes 6152 | tf_op jit(solution)/shard_map/ppermute | solution.py:424
  25.5 3.7 %collective-permute-start.2 = (f32[4,128]{1,0:T(4,128)S(1)}, f32[4,128]{1,0:T(4,128)S(1)}, u32[]{:S(2)}, u32[]{:S(2)}) collective-permute-start(f32[4,128]{1,0:T(4,128)S(1)} %get-tuple-element.16), channel_id=1, source_target_pairs={{0,4},{2,6},{4,0},{6,2},{8,12},{10,14},{12,8},{14,10},{16,20},{18,... | collective-permute-start | bytes 6152 | tf_op jit(solution)/shard_map/ppermute | solution.py:424
  25.6 3.6 %collective-permute-start.3 = (f32[4,128]{1,0:T(4,128)S(1)}, f32[4,128]{1,0:T(4,128)S(1)}, u32[]{:S(2)}, u32[]{:S(2)}) collective-permute-start(f32[4,128]{1,0:T(4,128)S(1)} %get-tuple-element.17), channel_id=1, source_target_pairs={{0,6},{2,4},{4,2},{6,0},{8,14},{10,12},{12,10},{14,8},{16,22},{18,... | collective-permute-start | bytes 6152 | tf_op jit(solution)/shard_map/ppermute | solution.py:424
  29.1 0.7 %copy-start.9 = (f32[8]{0:T(128)S(1)}, f32[8]{0:T(128)}, u32[]{:S(2)}) copy-start(f32[8]{0:T(128)} %mass_table.1) | copy-start | bytes 100

commit v4 on v3

--- a/solution.py
+++ b/solution.py
@@ -112,8 +112,10 @@
             out[rank, 8:16, :] = block
 
 
-def weight_kernel(k_index, kernel, pos, after, out, edges):
+def weight_kernel(k_index, kernel, pos, species, mass_table, after, out, edges, pull):
     del after
+    (mass,) = lookup((mass_table,), species[...])
+    pull[...] = time_step / mass
     dims, beads, _ = pos.shape
     for d in range(dims):
         edges[d : d + 1, :] = pos[d, 0:1, :]
@@ -312,7 +314,7 @@
         outs[t][...] = mine[0:4, pl.ds(there, width)]
 
 
-def move_kernel(low_at, high_at, rank_ref, pos, vel, low, high, species, mass_table, *refs):
+def move_kernel(low_at, high_at, rank_ref, pos, vel, low, high, pull, *refs):
     dims, beads, width = pos.shape
     got, (pos_out, vel_out, charge_out, home) = refs[:beads], refs[beads:]
     me = rank_ref[0] % beads
@@ -320,14 +322,14 @@
         bead = partner(me, -t, beads)
         for d in range(dims + 1):
             home[pl.ds(d * beads + bead, 1), :] = got[t][d : d + 1, :]
-    (mass,) = lookup((mass_table,), jnp.broadcast_to(species[...], (beads, width)))
+    gain = jnp.broadcast_to(pull[...], (beads, width))
     for d in range(dims):
         here = pos[d]
         before = jnp.concatenate([low[low_at + d : low_at + d + 1, :], here[: beads - 1]], 0)
         after = jnp.concatenate([here[1:], high[high_at + d : high_at + d + 1, :]], 0)
         laplace = 2.0 * here - before - after
         force = home[d * beads : (d + 1) * beads, :]
-        fresh = vel[d] + time_step * (force / mass - spring_rate * laplace)
+        fresh = vel[d] + (gain * force - (time_step * spring_rate) * laplace)
         vel_out[d] = fresh
         pos_out[d] = here + time_step * fresh
     charge_out[...] = home[dims * beads : (dims + 1) * beads, :]
@@ -371,20 +373,23 @@
         out_shape=shape((ranks, 16, width), F32),
         in_specs=[VMEM] * 4 + [SMEM] * 3,
         out_specs=VMEM,
-        compiler_params=params(4),
         name="pack",
     )(places, charges_in, kinds, neighbors, chi_table, hard_table, bond_table)
     got = lax.all_to_all(packed, "atoms", 0, 0, tiled=True)
 
-    weights, edges = pl.pallas_call(
+    weights, edges, pull = pl.pallas_call(
         weight_kernel,
-        out_shape=(shape((24, MODES), F32), shape((2 * dims, width), F32)),
-        in_specs=[VMEM] * 3 + [ANY],
-        out_specs=(VMEM, VMEM),
+        out_shape=(
+            shape((24, MODES), F32),
+            shape((2 * dims, width), F32),
+            shape((1, width), F32),
+        ),
+        in_specs=[VMEM] * 4 + [SMEM, ANY],
+        out_specs=(VMEM, VMEM, VMEM),
         compiler_params=params(8),
         name="weights",
         cost_estimate=pl.CostEstimate(flops=10**9, bytes_accessed=10**5, transcendentals=0),
-    )(k_index, kernel[None, :], places, packed)
+    )(k_index, kernel[None, :], places, kinds, mass_table, packed)
     if chain == 2:
         low = high = lax.ppermute(edges, "beads", [(0, 1), (1, 0)])
         low_at, high_at = dims, 0
@@ -430,12 +435,12 @@
             shape(places.shape, F32),
             shape(charges_in.shape, F32),
         ),
-        in_specs=[SMEM] + [VMEM] * 5 + [SMEM] + [VMEM] * beads,
+        in_specs=[SMEM] + [VMEM] * (5 + beads),
         out_specs=(VMEM, VMEM, VMEM),
         scratch_shapes=[pltpu.VMEM(((dims + 1) * beads, width), F32)],
         compiler_params=params(4),
         name="move",
-    )(rank, places, speeds, low, high, kinds, mass_table, *home)
+    )(rank, places, speeds, low, high, pull, *home)
     return new_places.transpose(1, 0, 2), new_speeds.transpose(1, 0, 2), charge
 
 

time: 31.3 us -> 27.6 us (0.88)
  local copies, waits for them, and re-layouts: 3.37 us -> 0.64 us
  waiting for transfers between devices: 7.76 us -> 6.57 us
    unnamed x24 -> x14, local copies, waits for them, and re-layouts: 3.37 us -> 0.64 us
    all_to_all x1, waiting for transfers between devices: 5.98 us -> 4.78 us  [body(): got = lax.all_to_all(packed, 'atoms', 0, 0, tiled=True)]
    pallas_call x1, Pallas kernels: 0.34 us -> 0.89 us  [body(): pl.pallas_call(weight_kernel, out_shape=(shape((24, MODES), F32), shape((...]
    pallas_call x1, Pallas kernels: 1.17 us -> 0.62 us  [body(): pl.pallas_call(functools.partial(move_kernel, low_at, high_at), out_shape...]
  transfers between devices with their start and end apart: 5 -> 5, of which waited for: 2 -> 2; matrix products, arithmetic and copies ran while one was open for 0% -> 0% of each run, Pallas kernels for 18% -> 23%
where the time goes in v4:
time: 27.6 us; the launch traced here: 27.3 us
  starting transfers between devices  11 us (40%)
  Pallas kernels  8.35 us (30%)
  waiting for transfers between devices  6.57 us (24%)
  between operations  0.74 us (3%)
  local copies, waits for them, and re-layouts  0.64 us (2%)
    all_to_all x1, starting transfers between devices, body(): got = lax.all_to_all(packed, 'atoms', 0, 0, tiled=True)  7.5 us
    pallas_call x1, Pallas kernels, body(): pl.pallas_call(functools.partial(bead_kernel, scale, 1.0 / atoms, beads),...  5.34 us
    all_to_all x1, waiting for transfers between devices, body(): got = lax.all_to_all(packed, 'atoms', 0, 0, tiled=True)  4.78 us
    ppermute x3, starting transfers between devices, body(): home.append(lax.ppermute(results[t], 'atoms', pairs))  1.93 us
    ppermute x3, waiting for transfers between devices, body(): home.append(lax.ppermute(results[t], 'atoms', pairs))  1.79 us
    ppermute x1, starting transfers between devices, body(): low = high = lax.ppermute(edges, 'beads', [(0, 1), (1, 0)])  1.58 us
    pallas_call x1, Pallas kernels, body(): pl.pallas_call(functools.partial(pack_kernel, ranks), out_shape=shape((ra...  1.5 us
    pallas_call x1, Pallas kernels, body(): pl.pallas_call(weight_kernel, out_shape=(shape((24, MODES), F32), shape((...  0.89 us
  transfers between devices with their start and end apart: 5, of which 2 were waited for; matrix products, arithmetic and copies ran while one was open for 0% of the time, Pallas kernels for 23%

profile of v4, /device:TPU:0, one launch (start us, length us, event | category | flops | bytes accessed | tf_op | source)
XLA Modules:
  0.0 27.3 jit_solution(9321994986530456204)
XLA Ops:
  0.6 1.5 %pack.1.after = f32[16,16,128]{2,1,0:T(8,128)} custom-call(f32[3,4,128]{2,1,0:T(4,128)} %bitcast.7, f32[4,128]{1,0:T(4,128)} %charge.1, s32[1,128]{1,0:T(1,128)} %bitcast.11, s32[8,128]{1,0:T(8,128)} %neighbors.1, f32[8]{0:T(128)} %chi_table.1, f32[8]{0:T(128)} %hard_table.1, f32[8]{0:T(128)} %bond_table.1), custom_call_target="tpu_custom_call" | custom-call | tf_op jit(solution)/shard_map/pack/pallas_call | solution.py:371
  2.1 0.0 copy-start
  2.1 0.0 copy-start.1
  2.1 0.0 copy-start.4
  2.1 0.0 copy-start.5
  2.2 7.5 %all-to-all-start = ((f32[16,16,128]{2,1,0:T(8,128)}), f32[16,16,128]{2,1,0:T(8,128)S(1)}, u32[]{:S(2)}, u32[]{:S(2)}) async-start(f32[16,16,128]{2,1,0:T(8,128)} %pack.1.after), calls=%async_computation | async-start | bytes 262144 | tf_op jit(solution)/shard_map/all_to_all | solution.py:378
  9.7 0.0 copy-start.3
  9.7 0.0 copy-start.6
  9.7 0.0 copy-done
  9.7 0.0 copy-done.1
  9.7 0.0 copy-done.4
  9.7 0.0 copy-done.5
  9.7 0.6 %copy-done.3 = s32[128]{0:T(128)S(1)} copy-done((s32[128]{0:T(128)S(1)}, s32[128]{0:T(128)}, u32[]{:S(2)}) %copy-start.3) | copy-done | bytes 536
  10.3 0.0 copy-done.6
  10.3 0.9 %weights.1 = (f32[24,160]{1,0:T(8,128)S(1)}, f32[6,128]{1,0:T(8,128)S(1)}, f32[1,128]{1,0:T(1,128)S(1)}) custom-call(s32[3,2048]{1,0:T(4,128)S(1)} %copy-done.4, f32[1,2048]{1,0:T(1,128)S(1)} %bitcast.13, f32[3,4,128]{2,1,0:T(4,128)S(1)} %bitcast.8, s32[1,128]{1,0:T(1,128)S(1)} %bitcast.12, f32[8]{0:T(128)S(1)} %copy-done.6, f32[16,16,128]{2,1,0:T(8,128)S(1)} %copy-done), custom_call_target="tpu_custom_call" | custom-call | flops 1000000000 | bytes 100000 | tf_op jit(solution)/shard_map/weights/pallas_call | solution.py:380
  11.2 1.6 %collective-permute-start = (f32[6,128]{1,0:T(8,128)S(1)}, f32[6,128]{1,0:T(8,128)S(1)}, u32[]{:S(2)}, u32[]{:S(2)}) collective-permute-start(f32[6,128]{1,0:T(8,128)S(1)} %get-tuple-element.13), channel_id=1, source_target_pairs={{0,1},{1,0},{2,3},{3,2},{4,5},{5,4},{6,7},{7,6},{8,9},{9,8},{10,11... | collective-permute-start | bytes 9224 | tf_op jit(solution)/shard_map/ppermute | solution.py:394
  12.8 4.8 %all-to-all-done.got = f32[16,16,128]{2,1,0:T(8,128)S(1)} async-done(((f32[16,16,128]{2,1,0:T(8,128)}), f32[16,16,128]{2,1,0:T(8,128)S(1)}, u32[]{:S(2)}, u32[]{:S(2)}) %all-to-all-start) | async-done | bytes 131104 | tf_op jit(solution)/shard_map/all_to_all | solution.py:378
  17.6 5.3 %bead.1 = (f32[4,128]{1,0:T(4,128)S(1)}, f32[4,128]{1,0:T(4,128)S(1)}, f32[4,128]{1,0:T(4,128)S(1)}, f32[4,128]{1,0:T(4,128)S(1)}) custom-call(s32[1]{0:T(128)} %bitcast.rank_ref, f32[16,16,128]{2,1,0:T(8,128)S(1)} %all-to-all-done.got, f32[24,160]{1,0:T(8,128)S(1)} %get-tuple-element.15.weights_hbm), custom_call_target="tpu_custom_call" | custom-call | flops 10000000000 | bytes 1000000 | tf_op jit(solution)/shard_map/bead/pallas_call | solution.py:403
  22.9 0.0 copy-start.2
  23.0 0.1 collective-permute-start.1
  23.0 0.1 collective-permute-start.2
  23.1 1.8 %collective-permute-start.3 = (f32[4,128]{1,0:T(4,128)S(1)}, f32[4,128]{1,0:T(4,128)S(1)}, u32[]{:S(2)}, u32[]{:S(2)}) collective-permute-start(f32[4,128]{1,0:T(4,128)S(1)} %get-tuple-element.19), channel_id=1, source_target_pairs={{0,6},{2,4},{4,2},{6,0},{8,14},{10,12},{12,10},{14,8},{16,22},{18,... | collective-permute-start | bytes 6152 | tf_op jit(solution)/shard_map/ppermute | solution.py:429
  24.9 0.0 collective-permute-done.low.high
  24.9 0.0 collective-permute-done.1.refs_1_
  24.9 1.8 %collective-permute-done.2.refs_2_ = f32[4,128]{1,0:T(4,128)S(1)} collective-permute-done((f32[4,128]{1,0:T(4,128)S(1)}, f32[4,128]{1,0:T(4,128)S(1)}, u32[]{:S(2)}, u32[]{:S(2)}) %collective-permute-start.2) | collective-permute-done | bytes 2080 | tf_op jit(solution)/shard_map/ppermute | solution.py:429
  26.7 0.0 collective-permute-done.3.refs_3_
  26.7 0.0 copy-done.2
  26.7 0.6 %move.1 = (f32[3,4,128]{2,1,0:T(4,128)}, f32[3,4,128]{2,1,0:T(4,128)}, f32[4,128]{1,0:T(4,128)}) custom-call(s32[1]{0:T(128)} %bitcast.rank_ref, f32[3,4,128]{2,1,0:T(4,128)S(1)} %bitcast.9, f32[3,4,128]{2,1,0:T(4,128)S(1)} %bitcast.10, f32[6,128]{1,0:T(8,128)S(1)} %collective-permute-done.low.high, f32[6,128]{1,0:T(8,128)S(1)} %collective-permute-done.low.high, ...), custom_call_target="tpu_custom_call" | custom-call | tf_op jit(solution)/shard_map/move/pallas_call | solution.py:431
Async XLA Ops:
  2.1 7.6 %copy-start = (f32[16,16,128]{2,1,0:T(8,128)S(1)}, f32[16,16,128]{2,1,0:T(8,128)}, u32[]{:S(2)}) copy-start(f32[16,16,128]{2,1,0:T(8,128)} %pack.1.after) | copy-start | bytes 393220
  2.1 7.6 %copy-start.1 = (f32[4,3,128]{2,0,1:T(4,128)S(1)}, f32[4,3,128]{2,0,1:T(4,128)}, u32[]{:S(2)}) copy-start(f32[4,3,128]{2,0,1:T(4,128)} %param.11) | copy-start | bytes 18436
  2.1 7.6 %copy-start.4 = (s32[3,2048]{1,0:T(4,128)S(1)}, s32[3,2048]{1,0:T(4,128)}, u32[]{:S(2)}) copy-start(s32[3,2048]{1,0:T(4,128)} %k_index.1) | copy-start | bytes 73732
  2.1 7.6 %copy-start.5 = (f32[2048]{0:T(1024)S(1)}, f32[2048]{0:T(1024)}, u32[]{:S(2)}) copy-start(f32[2048]{0:T(1024)} %param.17) | copy-start | bytes 24580
  2.2 15.4 %all-to-all-start = ((f32[16,16,128]{2,1,0:T(8,128)}), f32[16,16,128]{2,1,0:T(8,128)S(1)}, u32[]{:S(2)}, u32[]{:S(2)}) async-start(f32[16,16,128]{2,1,0:T(8,128)} %pack.1.after), calls=%async_computation | async-start | bytes 262144 | tf_op jit(solution)/shard_map/all_to_all | solution.py:378
  9.7 0.7 %copy-start.3 = (s32[128]{0:T(128)S(1)}, s32[128]{0:T(128)}, u32[]{:S(2)}) copy-start(s32[128]{0:T(128)} %param.14) | copy-start | bytes 1540
  9.7 0.7 %copy-start.6 = (f32[8]{0:T(128)S(1)}, f32[8]{0:T(128)}, u32[]{:S(2)}) copy-start(f32[8]{0:T(128)} %mass_table.1) | copy-start | bytes 100
  11.2 13.7 %collective-permute-start = (f32[6,128]{1,0:T(8,128)S(1)}, f32[6,128]{1,0:T(8,128)S(1)}, u32[]{:S(2)}, u32[]{:S(2)}) collective-permute-start(f32[6,128]{1,0:T(8,128)S(1)} %get-tuple-element.13), channel_id=1, source_target_pairs={{0,1},{1,0},{2,3},{3,2},{4,5},{5,4},{6,7},{7,6},{8,9},{9,8},{10,11... | collective-permute-start | bytes 9224 | tf_op jit(solution)/shard_map/ppermute | solution.py:394
  22.9 3.7 %copy-start.2 = (f32[4,3,128]{2,0,1:T(4,128)S(1)}, f32[4,3,128]{2,0,1:T(4,128)}, u32[]{:S(2)}) copy-start(f32[4,3,128]{2,0,1:T(4,128)} %param.12) | copy-start | bytes 18436
  23.0 1.9 %collective-permute-start.1 = (f32[4,128]{1,0:T(4,128)S(1)}, f32[4,128]{1,0:T(4,128)S(1)}, u32[]{:S(2)}, u32[]{:S(2)}) collective-permute-start(f32[4,128]{1,0:T(4,128)S(1)} %get-tuple-element.17), channel_id=1, source_target_pairs={{0,2},{2,0},{4,6},{6,4},{8,10},{10,8},{12,14},{14,12},{16,18},{18,... | collective-permute-start | bytes 6152 | tf_op jit(solution)/shard_map/ppermute | solution.py:429
  23.0 3.7 %collective-permute-start.2 = (f32[4,128]{1,0:T(4,128)S(1)}, f32[4,128]{1,0:T(4,128)S(1)}, u32[]{:S(2)}, u32[]{:S(2)}) collective-permute-start(f32[4,128]{1,0:T(4,128)S(1)} %get-tuple-element.18), channel_id=1, source_target_pairs={{0,4},{2,6},{4,0},{6,2},{8,12},{10,14},{12,8},{14,10},{16,20},{18,... | collective-permute-start | bytes 6152 | tf_op jit(solution)/shard_map/ppermute | solution.py:429
  23.1 3.6 %collective-permute-start.3 = (f32[4,128]{1,0:T(4,128)S(1)}, f32[4,128]{1,0:T(4,128)S(1)}, u32[]{:S(2)}, u32[]{:S(2)}) collective-permute-start(f32[4,128]{1,0:T(4,128)S(1)} %get-tuple-element.19), channel_id=1, source_target_pairs={{0,6},{2,4},{4,2},{6,0},{8,14},{10,12},{12,10},{14,8},{16,22},{18,... | collective-permute-start | bytes 6152 | tf_op jit(solution)/shard_map/ppermute | solution.py:429

commit v5 on v4

--- a/solution.py
+++ b/solution.py
@@ -99,17 +99,52 @@
     return found
 
 
-def pack_kernel(ranks, pos, charge, species, neighbors, chi_table, hard_table, bond_table, out):
+def pack_kernel(
+    pos_hbm,
+    charge_hbm,
+    species_hbm,
+    neighbors_hbm,
+    chi_hbm,
+    hard_hbm,
+    bond_hbm,
+    out,
+    pos,
+    charge,
+    species,
+    neighbors,
+    chi_table,
+    hard_table,
+    bond_table,
+    arrived,
+):
+    sources = (pos_hbm, charge_hbm, species_hbm, neighbors_hbm, chi_hbm, hard_hbm, bond_hbm)
+    targets = (pos, charge, species, neighbors, chi_table, hard_table, bond_table)
+    copies = [
+        pltpu.make_async_copy(source, target, arrived.at[i])
+        for i, (source, target) in enumerate(zip(sources, targets))
+    ]
+    for copy in copies:
+        copy.start()
+    for copy in copies:
+        copy.wait()
     dims, beads, width = pos.shape
-    near = neighbors[...].astype(F32)
     chi, hard, bond = lookup((chi_table, hard_table, bond_table), species[...])
     shared = [chi, mixing / hard, bond, jnp.zeros((1, width), F32)]
     for b in range(beads):
         own = [pos[d, b : b + 1, :] for d in range(dims)] + [charge[b : b + 1, :]]
-        block = jnp.concatenate(own + shared, 0)
-        for rank in range(b, ranks, beads):
-            out[rank, 0:8, :] = near
-            out[rank, 8:16, :] = block
+        out[b] = jnp.concatenate(own + shared, 0)
+    out[beads] = neighbors[...].astype(F32)
+
+
+def sort_kernel(beads, groups, rank_ref, *refs):
+    got, outs = refs[:groups], refs[groups:]
+    me, group = rank_ref[0] % beads, rank_ref[0] // beads
+    for k in range(groups):
+        source = partner(group, -k, groups)
+        near = got[k][beads]
+        for t in range(beads):
+            outs[t][source, 0:8, :] = near
+            outs[t][source, 8:16, :] = got[k][partner(me, t, beads)]
 
 
 def weight_kernel(k_index, kernel, pos, species, mass_table, after, out, edges, pull):
@@ -149,12 +184,12 @@
     inverse_atoms,
     beads,
     rank_ref,
-    got,
     weights_hbm,
     *refs,
 ):
-    outs = refs[:beads]
+    blocks, outs = refs[:beads], refs[beads : 2 * beads]
     (
+        got,
         cos_high,
         cos_low,
         sin_high,
@@ -166,10 +201,15 @@
         weights,
         mine,
         arrived,
-    ) = refs[beads:]
+    ) = refs[2 * beads :]
     bring = pltpu.make_async_copy(weights_hbm, weights, arrived)
     bring.start()
     ranks, _, width = got.shape
+    me = rank_ref[0] % beads
+    for t in range(beads):
+        source = partner(me, -t, beads)
+        for group in range(ranks // beads):
+            got[group * beads + source] = blocks[t][group]
     lane = lax.broadcasted_iota(jnp.int32, (8, width), 1)
     row = lax.broadcasted_iota(jnp.int32, (8, width), 0)
     multiple = (row + 1).astype(F32)
@@ -308,7 +348,6 @@
         mine[:, cut] = jnp.where(
             row == 0, fx, jnp.where(row == 1, fy, jnp.where(row == 2, fz, q[:, cut]))
         )
-    me = rank_ref[0] % beads
     for t in range(beads):
         there = pl.multiple_of(partner(me, t, beads) * width, width)
         outs[t][...] = mine[0:4, pl.ds(there, width)]
@@ -338,6 +377,11 @@
 VMEM = pl.BlockSpec(memory_space=pltpu.VMEM)
 SMEM = pl.BlockSpec(memory_space=pltpu.SMEM)
 ANY = pl.BlockSpec(memory_space=pl.ANY)
+HBM = pl.BlockSpec(memory_space=pltpu.HBM)
+
+
+def stay(x):
+    return pltpu.with_memory_space_constraint(x, pltpu.HBM)
 
 
 def params(mebibytes):
@@ -368,14 +412,45 @@
     places = positions.transpose(1, 0, 2)
     speeds = velocities.transpose(1, 0, 2)
 
+    rank = lax.axis_index("atoms").astype(jnp.int32)[None]
+    groups = ranks // beads
+
+    def among_groups(x, k):
+        pairs = [(r, partner(r // beads, k, groups) * beads + r % beads) for r in range(ranks)]
+        return lax.ppermute(x, "atoms", pairs)
+
+    def in_group(x, t):
+        pairs = [(r, r // beads * beads + partner(r % beads, t, beads)) for r in range(ranks)]
+        return lax.ppermute(x, "atoms", pairs)
+
     packed = pl.pallas_call(
-        functools.partial(pack_kernel, ranks),
-        out_shape=shape((ranks, 16, width), F32),
-        in_specs=[VMEM] * 4 + [SMEM] * 3,
+        pack_kernel,
+        out_shape=shape((beads + 1, 8, width), F32),
+        in_specs=[HBM] * 7,
         out_specs=VMEM,
+        scratch_shapes=[
+            pltpu.VMEM(places.shape, F32),
+            pltpu.VMEM(charges_in.shape, F32),
+            pltpu.VMEM(kinds.shape, jnp.int32),
+            pltpu.VMEM(neighbors.shape, jnp.int32),
+            pltpu.SMEM((SPECIES,), F32),
+            pltpu.SMEM((SPECIES,), F32),
+            pltpu.SMEM((SPECIES,), F32),
+            pltpu.SemaphoreType.DMA((7,)),
+        ],
+        compiler_params=params(4),
         name="pack",
-    )(places, charges_in, kinds, neighbors, chi_table, hard_table, bond_table)
-    got = lax.all_to_all(packed, "atoms", 0, 0, tiled=True)
+    )(*map(stay, (places, charges_in, kinds, neighbors, chi_table, hard_table, bond_table)))
+    gathered = [packed] + [among_groups(packed, k) for k in range(1, groups)]
+    sorted_blocks = pl.pallas_call(
+        functools.partial(sort_kernel, beads, groups),
+        out_shape=[shape((groups, 16, width), F32)] * beads,
+        in_specs=[SMEM] + [VMEM] * groups,
+        out_specs=[VMEM] * beads,
+        compiler_params=params(4),
+        name="sort",
+    )(rank, *gathered)
+    blocks = [sorted_blocks[0]] + [in_group(sorted_blocks[t], t) for t in range(1, beads)]
 
     weights, edges, pull = pl.pallas_call(
         weight_kernel,
@@ -399,13 +474,13 @@
         high = lax.ppermute(edges[:dims], "beads", [(b, a) for a, b in forward])
         low_at, high_at = 0, 0
 
-    rank = lax.axis_index("atoms").astype(jnp.int32)[None]
     results = pl.pallas_call(
         functools.partial(bead_kernel, scale, 1.0 / atoms, beads),
         out_shape=[shape((4, width), F32)] * beads,
-        in_specs=[SMEM, VMEM, ANY],
+        in_specs=[SMEM, ANY] + [VMEM] * beads,
         out_specs=[VMEM] * beads,
         scratch_shapes=[
+            pltpu.VMEM((ranks, 16, width), F32),
             pltpu.VMEM((MODES, atoms), BF16),
             pltpu.VMEM((MODES, atoms), BF16),
             pltpu.VMEM((MODES, atoms), BF16),
@@ -421,12 +496,9 @@
         compiler_params=params(24),
         name="bead",
         cost_estimate=pl.CostEstimate(flops=10**10, bytes_accessed=10**6, transcendentals=0),
-    )(rank, got, weights)
-
-    home = [results[0]]
-    for t in range(1, beads):
-        pairs = [(r, r // beads * beads + partner(r % beads, t, beads)) for r in range(ranks)]
-        home.append(lax.ppermute(results[t], "atoms", pairs))
+    )(rank, weights, *blocks)
+
+    home = [results[0]] + [in_group(results[t], t) for t in range(1, beads)]
 
     new_places, new_speeds, charge = pl.pallas_call(
         functools.partial(move_kernel, low_at, high_at),

time: 27.6 us -> 28.2 us (1.022)
  waiting for transfers between devices: 6.57 us -> 8 us
  Pallas kernels: 8.35 us -> 7.79 us
    ppermute x3 -> x9, starting transfers between devices: 1.93 us -> 9.54 us  [the longest x3 5.68 us: among_groups(): return lax.ppermute(x, 'atoms', pairs)]
    all_to_all x1 -> x0, starting transfers between devices: 7.5 us -> none  [body(): got = lax.all_to_all(packed, 'atoms', 0, 0, tiled=True)]
    ppermute x3 -> x9, waiting for transfers between devices: 1.79 us -> 8 us  [the longest x3 5.58 us: among_groups(): return lax.ppermute(x, 'atoms', pairs)]
    all_to_all x1 -> x0, waiting for transfers between devices: 4.78 us -> none  [body(): got = lax.all_to_all(packed, 'atoms', 0, 0, tiled=True)]
    pallas_call x1 -> x2, Pallas kernels: 1.5 us -> 0.92 us  [the longest x1 0.9 us: body(): pl.pallas_call(pack_kernel, out_shape=shape((beads + 1, 8, width), F32),...]
    unnamed x14 -> x12, local copies, waits for them, and re-layouts: 0.64 us -> 0.38 us
  transfers between devices with their start and end apart: 5 -> 10, of which waited for: 2 -> 5; matrix products, arithmetic and copies ran while one was open for 0% -> 0% of each run, Pallas kernels for 23% -> 22%
where the time goes in v5:
time: 28.2 us; the launch traced here: 28 us
  starting transfers between devices  11.1 us (39%)
  waiting for transfers between devices  8 us (28%)
  Pallas kernels  7.79 us (28%)
  between operations  0.7 us (2%)
  local copies, waits for them, and re-layouts  0.38 us (1%)
    ppermute x3, starting transfers between devices, among_groups(): return lax.ppermute(x, 'atoms', pairs)  5.68 us
    ppermute x3, waiting for transfers between devices, among_groups(): return lax.ppermute(x, 'atoms', pairs)  5.58 us
    pallas_call x1, Pallas kernels, body(): pl.pallas_call(functools.partial(bead_kernel, scale, 1.0 / atoms, beads),...  5.36 us
    ppermute x6, starting transfers between devices, in_group(): return lax.ppermute(x, 'atoms', pairs)  3.86 us
    ppermute x6, waiting for transfers between devices, in_group(): return lax.ppermute(x, 'atoms', pairs)  2.42 us
    ppermute x1, starting transfers between devices, body(): low = high = lax.ppermute(edges, 'beads', [(0, 1), (1, 0)])  1.58 us
    pallas_call x1, Pallas kernels, body(): pl.pallas_call(pack_kernel, out_shape=shape((beads + 1, 8, width), F32),...  0.9 us
    pallas_call x1, Pallas kernels, body(): pl.pallas_call(weight_kernel, out_shape=(shape((24, MODES), F32), shape((...  0.89 us
  transfers between devices with their start and end apart: 10, of which 5 were waited for; matrix products, arithmetic and copies ran while one was open for 0% of the time, Pallas kernels for 22%

profile of v5, /device:TPU:0, one launch (start us, length us, event | category | flops | bytes accessed | tf_op | source)
XLA Modules:
  0.0 28.0 jit_solution(5524444268330539168)
XLA Ops:
  0.6 0.9 %pack.1.after.refs_0_ = f32[5,8,128]{2,1,0:T(8,128)S(1)} custom-call(f32[3,4,128]{2,1,0:T(4,128)} %bitcast.7, f32[4,128]{1,0:T(4,128)} %charge_hbm.1, s32[1,128]{1,0:T(1,128)} %bitcast.11, s32[8,128]{1,0:T(8,128)} %neighbors_hbm.1, f32[8]{0:T(128)} %chi_hbm.1, f32[8]{0:T(128)} %hard_hbm.1, f32[8]{0:T(128)} %bond_hbm.1), custom_call_target="tpu_custom_call" | custom-call | tf_op jit(solution)/shard_map/pack/pallas_call | solution.py:426
  1.5 3.1 %collective-permute-start.1 = (f32[5,8,128]{2,1,0:T(8,128)S(1)}, f32[5,8,128]{2,1,0:T(8,128)S(1)}, u32[]{:S(2)}, u32[]{:S(2)}) collective-permute-start(f32[5,8,128]{2,1,0:T(8,128)S(1)} %pack.1.after.refs_0_), channel_id=1, source_target_pairs={{0,8},{2,10},{4,12},{6,14},{8,0},{10,2},{12,4},{14,6},{16,24},{18,... | collective-permute-start | bytes 61448 | tf_op jit(solution)/shard_map/ppermute | solution.py:420
  4.6 2.6 %collective-permute-start.2 = (f32[5,8,128]{2,1,0:T(8,128)S(1)}, f32[5,8,128]{2,1,0:T(8,128)S(1)}, u32[]{:S(2)}, u32[]{:S(2)}) collective-permute-start(f32[5,8,128]{2,1,0:T(8,128)S(1)} %pack.1.after.refs_0_), channel_id=1, source_target_pairs={{0,16},{2,18},{4,20},{6,22},{8,24},{10,26},{12,28},{14,30},{16,0},... | collective-permute-start | bytes 61448 | tf_op jit(solution)/shard_map/ppermute | solution.py:420
  7.2 0.0 collective-permute-start.3
  7.2 0.0 collective-permute-done.1.refs_1_
  7.2 2.3 %collective-permute-done.2.refs_2_ = f32[5,8,128]{2,1,0:T(8,128)S(1)} collective-permute-done((f32[5,8,128]{2,1,0:T(8,128)S(1)}, f32[5,8,128]{2,1,0:T(8,128)S(1)}, u32[]{:S(2)}, u32[]{:S(2)}) %collective-permute-start.2) | collective-permute-done | bytes 20512 | tf_op jit(solution)/shard_map/ppermute | solution.py:420
  9.5 3.3 %collective-permute-done.3.refs_3_ = f32[5,8,128]{2,1,0:T(8,128)S(1)} collective-permute-done((f32[5,8,128]{2,1,0:T(8,128)S(1)}, f32[5,8,128]{2,1,0:T(8,128)S(1)}, u32[]{:S(2)}, u32[]{:S(2)}) %collective-permute-start.3) | collective-permute-done | bytes 20512 | tf_op jit(solution)/shard_map/ppermute | solution.py:420
  12.8 0.0 copy-start.3
  12.8 0.0 copy-start.4
  12.8 0.0 copy-start
  12.8 0.1 collective-permute-start.4
  12.9 1.6 %collective-permute-start.5 = (f32[4,16,128]{2,1,0:T(8,128)S(1)}, f32[4,16,128]{2,1,0:T(8,128)S(1)}, u32[]{:S(2)}, u32[]{:S(2)}) collective-permute-start(f32[4,16,128]{2,1,0:T(8,128)S(1)} %get-tuple-element.22), channel_id=1, source_target_pairs={{0,4},{2,6},{4,0},{6,2},{8,12},{10,14},{12,8},{14,10},{16,20},{18,... | collective-permute-start | bytes 98312 | tf_op jit(solution)/shard_map/ppermute | solution.py:424
  14.5 0.0 copy-start.2
  14.5 0.0 copy-start.5
  14.5 0.3 %collective-permute-start.6 = (f32[4,16,128]{2,1,0:T(8,128)S(1)}, f32[4,16,128]{2,1,0:T(8,128)S(1)}, u32[]{:S(2)}, u32[]{:S(2)}) collective-permute-start(f32[4,16,128]{2,1,0:T(8,128)S(1)} %get-tuple-element.23), channel_id=1, source_target_pairs={{0,6},{2,4},{4,2},{6,0},{8,14},{10,12},{12,10},{14,8},{16,22},{18,... | collective-permute-start | bytes 98312 | tf_op jit(solution)/shard_map/ppermute | solution.py:424
  14.8 0.0 copy-done.3
  14.8 0.0 copy-done.4
  14.8 0.0 copy-done
  14.8 0.3 %copy-done.2 = s32[128]{0:T(128)S(1)} copy-done((s32[128]{0:T(128)S(1)}, s32[128]{0:T(128)}, u32[]{:S(2)}) %copy-start.2) | copy-done | bytes 536
  15.1 0.0 copy-done.5
  15.1 0.9 %weights.1 = (f32[24,160]{1,0:T(8,128)S(1)}, f32[6,128]{1,0:T(8,128)S(1)}, f32[1,128]{1,0:T(1,128)S(1)}) custom-call(s32[3,2048]{1,0:T(4,128)S(1)} %copy-done.3, f32[1,2048]{1,0:T(1,128)S(1)} %bitcast.13, f32[3,4,128]{2,1,0:T(4,128)S(1)} %bitcast.8, s32[1,128]{1,0:T(1,128)S(1)} %bitcast.12, f32[8]{0:T(128)S(1)} %copy-done.5, f32[5,8,128]{2,1,0:T(8,128)S(1)} %pack.1.after.refs_0_), custom_call_target="tpu_custom_call" | custom-call | flops 1000000000 | bytes 100000 | tf_op jit(solution)/shard_map/weights/pallas_call | solution.py:455
  16.0 1.6 %collective-permute-start = (f32[6,128]{1,0:T(8,128)S(1)}, f32[6,128]{1,0:T(8,128)S(1)}, u32[]{:S(2)}, u32[]{:S(2)}) collective-permute-start(f32[6,128]{1,0:T(8,128)S(1)} %get-tuple-element.17), channel_id=1, source_target_pairs={{0,1},{1,0},{2,3},{3,2},{4,5},{5,4},{6,7},{7,6},{8,9},{9,8},{10,11... | collective-permute-start | bytes 9224 | tf_op jit(solution)/shard_map/ppermute | solution.py:469
  17.6 0.0 collective-permute-done.4.refs_1_
  17.6 0.0 collective-permute-done.5.refs_2_
  17.6 0.2 collective-permute-done.6.refs_3_
  17.8 5.4 %bead.1 = (f32[4,128]{1,0:T(4,128)S(1)}, f32[4,128]{1,0:T(4,128)S(1)}, f32[4,128]{1,0:T(4,128)S(1)}, f32[4,128]{1,0:T(4,128)S(1)}) custom-call(s32[1]{0:T(128)} %bitcast.rank_ref, f32[24,160]{1,0:T(8,128)S(1)} %get-tuple-element.19.weights_hbm, f32[4,16,128]{2,1,0:T(8,128)S(1)} %get-tuple-element.20.refs_0_, ...), custom_call_target="tpu_custom_call" | custom-call | flops 10000000000 | bytes 1000000 | tf_op jit(solution)/shard_map/bead/pallas_call | solution.py:477
  23.2 0.0 copy-start.1
  23.2 0.2 collective-permute-start.7
  23.4 0.9 %collective-permute-start.8 = (f32[4,128]{1,0:T(4,128)S(1)}, f32[4,128]{1,0:T(4,128)S(1)}, u32[]{:S(2)}, u32[]{:S(2)}) collective-permute-start(f32[4,128]{1,0:T(4,128)S(1)} %get-tuple-element.26), channel_id=1, source_target_pairs={{0,4},{2,6},{4,0},{6,2},{8,12},{10,14},{12,8},{14,10},{16,20},{18,... | collective-permute-start | bytes 6152 | tf_op jit(solution)/shard_map/ppermute | solution.py:424
  24.3 0.8 %collective-permute-start.9 = (f32[4,128]{1,0:T(4,128)S(1)}, f32[4,128]{1,0:T(4,128)S(1)}, u32[]{:S(2)}, u32[]{:S(2)}) collective-permute-start(f32[4,128]{1,0:T(4,128)S(1)} %get-tuple-element.27), channel_id=1, source_target_pairs={{0,6},{2,4},{4,2},{6,0},{8,14},{10,12},{12,10},{14,8},{16,22},{18,... | collective-permute-start | bytes 6152 | tf_op jit(solution)/shard_map/ppermute | solution.py:424
  25.1 0.0 collective-permute-done.low.high
  25.1 0.0 collective-permute-done.7.refs_1_
  25.1 1.9 %collective-permute-done.8.refs_2_ = f32[4,128]{1,0:T(4,128)S(1)} collective-permute-done((f32[4,128]{1,0:T(4,128)S(1)}, f32[4,128]{1,0:T(4,128)S(1)}, u32[]{:S(2)}, u32[]{:S(2)}) %collective-permute-start.8) | collective-permute-done | bytes 2080 | tf_op jit(solution)/shard_map/ppermute | solution.py:424
  27.0 0.3 %collective-permute-done.9.refs_3_ = f32[4,128]{1,0:T(4,128)S(1)} collective-permute-done((f32[4,128]{1,0:T(4,128)S(1)}, f32[4,128]{1,0:T(4,128)S(1)}, u32[]{:S(2)}, u32[]{:S(2)}) %collective-permute-start.9) | collective-permute-done | bytes 2080 | tf_op jit(solution)/shard_map/ppermute | solution.py:424
  27.4 0.0 copy-done.1
  27.4 0.6 %move.1 = (f32[3,4,128]{2,1,0:T(4,128)}, f32[3,4,128]{2,1,0:T(4,128)}, f32[4,128]{1,0:T(4,128)}) custom-call(s32[1]{0:T(128)} %bitcast.rank_ref, f32[3,4,128]{2,1,0:T(4,128)S(1)} %bitcast.9, f32[3,4,128]{2,1,0:T(4,128)S(1)} %bitcast.10, f32[6,128]{1,0:T(8,128)S(1)} %collective-permute-done.low.high, f32[6,128]{1,0:T(8,128)S(1)} %collective-permute-done.low.high, ...), custom_call_target="tpu_custom_call" | custom-call | tf_op jit(solution)/shard_map/move/pallas_call | solution.py:503
  (1 shorter events, 0.0 us)
Async XLA Ops:
  1.5 5.7 %collective-permute-start.1 = (f32[5,8,128]{2,1,0:T(8,128)S(1)}, f32[5,8,128]{2,1,0:T(8,128)S(1)}, u32[]{:S(2)}, u32[]{:S(2)}) collective-permute-start(f32[5,8,128]{2,1,0:T(8,128)S(1)} %pack.1.after.refs_0_), channel_id=1, source_target_pairs={{0,8},{2,10},{4,12},{6,14},{8,0},{10,2},{12,4},{14,6},{16,24},{18,... | collective-permute-start | bytes 61448 | tf_op jit(solution)/shard_map/ppermute | solution.py:420
  4.6 4.9 %collective-permute-start.2 = (f32[5,8,128]{2,1,0:T(8,128)S(1)}, f32[5,8,128]{2,1,0:T(8,128)S(1)}, u32[]{:S(2)}, u32[]{:S(2)}) collective-permute-start(f32[5,8,128]{2,1,0:T(8,128)S(1)} %pack.1.after.refs_0_), channel_id=1, source_target_pairs={{0,16},{2,18},{4,20},{6,22},{8,24},{10,26},{12,28},{14,30},{16,0},... | collective-permute-start | bytes 61448 | tf_op jit(solution)/shard_map/ppermute | solution.py:420
  7.2 5.6 %collective-permute-start.3 = (f32[5,8,128]{2,1,0:T(8,128)S(1)}, f32[5,8,128]{2,1,0:T(8,128)S(1)}, u32[]{:S(2)}, u32[]{:S(2)}) collective-permute-start(f32[5,8,128]{2,1,0:T(8,128)S(1)} %pack.1.after.refs_0_), channel_id=1, source_target_pairs={{0,24},{2,26},{4,28},{6,30},{8,16},{10,18},{12,20},{14,22},{16,8},... | collective-permute-start | bytes 61448 | tf_op jit(solution)/shard_map/ppermute | solution.py:420
  12.8 2.0 %copy-start.3 = (s32[3,2048]{1,0:T(4,128)S(1)}, s32[3,2048]{1,0:T(4,128)}, u32[]{:S(2)}) copy-start(s32[3,2048]{1,0:T(4,128)} %k_index.1) | copy-start | bytes 73732
  12.8 2.0 %copy-start.4 = (f32[2048]{0:T(1024)S(1)}, f32[2048]{0:T(1024)}, u32[]{:S(2)}) copy-start(f32[2048]{0:T(1024)} %param.17) | copy-start | bytes 24580
  12.8 2.0 %copy-start = (f32[4,3,128]{2,0,1:T(4,128)S(1)}, f32[4,3,128]{2,0,1:T(4,128)}, u32[]{:S(2)}) copy-start(f32[4,3,128]{2,0,1:T(4,128)} %param.11) | copy-start | bytes 18436
  12.8 4.8 %collective-permute-start.4 = (f32[4,16,128]{2,1,0:T(8,128)S(1)}, f32[4,16,128]{2,1,0:T(8,128)S(1)}, u32[]{:S(2)}, u32[]{:S(2)}) collective-permute-start(f32[4,16,128]{2,1,0:T(8,128)S(1)} %get-tuple-element.21), channel_id=1, source_target_pairs={{0,2},{2,0},{4,6},{6,4},{8,10},{10,8},{12,14},{14,12},{16,18},{18,... | collective-permute-start | bytes 98312 | tf_op jit(solution)/shard_map/ppermute | solution.py:424
  12.9 4.7 %collective-permute-start.5 = (f32[4,16,128]{2,1,0:T(8,128)S(1)}, f32[4,16,128]{2,1,0:T(8,128)S(1)}, u32[]{:S(2)}, u32[]{:S(2)}) collective-permute-start(f32[4,16,128]{2,1,0:T(8,128)S(1)} %get-tuple-element.22), channel_id=1, source_target_pairs={{0,4},{2,6},{4,0},{6,2},{8,12},{10,14},{12,8},{14,10},{16,20},{18,... | collective-permute-start | bytes 98312 | tf_op jit(solution)/shard_map/ppermute | solution.py:424
  14.5 0.7 %copy-start.2 = (s32[128]{0:T(128)S(1)}, s32[128]{0:T(128)}, u32[]{:S(2)}) copy-start(s32[128]{0:T(128)} %param.14) | copy-start | bytes 1540
  14.5 0.7 %copy-start.5 = (f32[8]{0:T(128)S(1)}, f32[8]{0:T(128)}, u32[]{:S(2)}) copy-start(f32[8]{0:T(128)} %mass_table.1) | copy-start | bytes 100
  14.5 3.3 %collective-permute-start.6 = (f32[4,16,128]{2,1,0:T(8,128)S(1)}, f32[4,16,128]{2,1,0:T(8,128)S(1)}, u32[]{:S(2)}, u32[]{:S(2)}) collective-permute-start(f32[4,16,128]{2,1,0:T(8,128)S(1)} %get-tuple-element.23), channel_id=1, source_target_pairs={{0,6},{2,4},{4,2},{6,0},{8,14},{10,12},{12,10},{14,8},{16,22},{18,... | collective-permute-start | bytes 98312 | tf_op jit(solution)/shard_map/ppermute | solution.py:424
  16.0 9.1 %collective-permute-start = (f32[6,128]{1,0:T(8,128)S(1)}, f32[6,128]{1,0:T(8,128)S(1)}, u32[]{:S(2)}, u32[]{:S(2)}) collective-permute-start(f32[6,128]{1,0:T(8,128)S(1)} %get-tuple-element.17), channel_id=1, source_target_pairs={{0,1},{1,0},{2,3},{3,2},{4,5},{5,4},{6,7},{7,6},{8,9},{9,8},{10,11... | collective-permute-start | bytes 9224 | tf_op jit(solution)/shard_map/ppermute | solution.py:469
  23.2 4.2 %copy-start.1 = (f32[4,3,128]{2,0,1:T(4,128)S(1)}, f32[4,3,128]{2,0,1:T(4,128)}, u32[]{:S(2)}) copy-start(f32[4,3,128]{2,0,1:T(4,128)} %param.12) | copy-start | bytes 18436
  23.2 1.9 %collective-permute-start.7 = (f32[4,128]{1,0:T(4,128)S(1)}, f32[4,128]{1,0:T(4,128)S(1)}, u32[]{:S(2)}, u32[]{:S(2)}) collective-permute-start(f32[4,128]{1,0:T(4,128)S(1)} %get-tuple-element.25), channel_id=1, source_target_pairs={{0,2},{2,0},{4,6},{6,4},{8,10},{10,8},{12,14},{14,12},{16,18},{18,... | collective-permute-start | bytes 6152 | tf_op jit(solution)/shard_map/ppermute | solution.py:424
  23.4 3.6 %collective-permute-start.8 = (f32[4,128]{1,0:T(4,128)S(1)}, f32[4,128]{1,0:T(4,128)S(1)}, u32[]{:S(2)}, u32[]{:S(2)}) collective-permute-start(f32[4,128]{1,0:T(4,128)S(1)} %get-tuple-element.26), channel_id=1, source_target_pairs={{0,4},{2,6},{4,0},{6,2},{8,12},{10,14},{12,8},{14,10},{16,20},{18,... | collective-permute-start | bytes 6152 | tf_op jit(solution)/shard_map/ppermute | solution.py:424
  24.3 3.0 %collective-permute-start.9 = (f32[4,128]{1,0:T(4,128)S(1)}, f32[4,128]{1,0:T(4,128)S(1)}, u32[]{:S(2)}, u32[]{:S(2)}) collective-permute-start(f32[4,128]{1,0:T(4,128)S(1)} %get-tuple-element.27), channel_id=1, source_target_pairs={{0,6},{2,4},{4,2},{6,0},{8,14},{10,12},{12,10},{14,8},{16,22},{18,... | collective-permute-start | bytes 6152 | tf_op jit(solution)/shard_map/ppermute | solution.py:424

commit v6 on v4

--- a/solution.py
+++ b/solution.py
@@ -99,17 +99,27 @@
     return found
 
 
-def pack_kernel(ranks, pos, charge, species, neighbors, chi_table, hard_table, bond_table, out):
-    dims, beads, width = pos.shape
+def pack_kernel(
+    ranks, pos_hbm, charge_hbm, species_hbm, neighbors_hbm, out, pos, charge, species, neighbors, arrived
+):
+    sources = (pos_hbm, charge_hbm, species_hbm, neighbors_hbm)
+    targets = (pos, charge, species, neighbors)
+    copies = [
+        pltpu.make_async_copy(source, target, arrived.at[i])
+        for i, (source, target) in enumerate(zip(sources, targets))
+    ]
+    for copy in copies:
+        copy.start()
+    for copy in copies:
+        copy.wait()
+    dims, beads, _ = pos.shape
     near = neighbors[...].astype(F32)
-    chi, hard, bond = lookup((chi_table, hard_table, bond_table), species[...])
-    shared = [chi, mixing / hard, bond, jnp.zeros((1, width), F32)]
+    shared = [species[...].astype(F32)] + [near[n : n + 1, :] for n in range(near.shape[0])]
     for b in range(beads):
         own = [pos[d, b : b + 1, :] for d in range(dims)] + [charge[b : b + 1, :]]
-        block = jnp.concatenate(own + shared, 0)
         for rank in range(b, ranks, beads):
-            out[rank, 0:8, :] = near
-            out[rank, 8:16, :] = block
+            for i, line in enumerate(own + shared):
+                out[rank, i] = line
 
 
 def weight_kernel(k_index, kernel, pos, species, mass_table, after, out, edges, pull):
@@ -149,8 +159,11 @@
     inverse_atoms,
     beads,
     rank_ref,
+    weights_hbm,
     got,
-    weights_hbm,
+    chi_hbm,
+    hard_hbm,
+    bond_hbm,
     *refs,
 ):
     outs = refs[:beads]
@@ -165,11 +178,30 @@
         charges,
         weights,
         mine,
+        kinds,
+        chi,
+        hard,
+        bond,
+        chi_table,
+        hard_table,
+        bond_table,
         arrived,
     ) = refs[beads:]
-    bring = pltpu.make_async_copy(weights_hbm, weights, arrived)
-    bring.start()
-    ranks, _, width = got.shape
+    bring = [
+        pltpu.make_async_copy(source, target, arrived.at[i])
+        for i, (source, target) in enumerate(
+            (
+                (weights_hbm, weights),
+                (chi_hbm, chi_table),
+                (hard_hbm, hard_table),
+                (bond_hbm, bond_table),
+            )
+        )
+    ]
+    for copy in bring:
+        copy.start()
+    ranks, lines, _, width = got.shape
+    me = rank_ref[0] % beads
     lane = lax.broadcasted_iota(jnp.int32, (8, width), 1)
     row = lax.broadcasted_iota(jnp.int32, (8, width), 0)
     multiple = (row + 1).astype(F32)
@@ -185,11 +217,11 @@
     def column_sum(x):
         return everywhere(jnp.sum(x, axis=0, keepdims=True))
 
-    chi, hard, bond, charge = [], [], [], []
+    charge, place = [], []
     for j in range(ranks):
-        cx, sx = turns(multiple, got[j, 8:9, :])
-        cy, sy = turns(multiple, got[j, 9:10, :])
-        cz, sz = turns(multiple, got[j, 10:11, :])
+        cx, sx = turns(multiple, got[j, 0])
+        cy, sy = turns(multiple, got[j, 1])
+        cz, sz = turns(multiple, got[j, 2])
         z_cos[:, at(j)] = cz
         z_sin[:, at(j)] = sz
 
@@ -215,12 +247,15 @@
             jnp.concatenate([single, blank], 0),
             jnp.concatenate([blank, blank], 0),
         )
-        charge.append(everywhere(got[j, 11:12, :]))
-        chi.append(everywhere(got[j, 12:13, :]))
-        hard.append(everywhere(got[j, 13:14, :]))
-        bond.append(everywhere(got[j, 14:15, :]))
-
-    bring.wait()
+        charge.append(everywhere(got[j, 3]))
+        kinds[j : j + 1, :] = got[j, 4]
+        near = jnp.concatenate([got[j, i] for i in range(5, lines)], 0)
+        place.append((lane + near.astype(jnp.int32)) & (width - 1))
+
+    for copy in bring:
+        copy.wait()
+    chi[...], hardness, bond[...] = lookup((chi_table, hard_table, bond_table), kinds[...])
+    hard[...] = mixing / hardness
     even, odd, zero = weights[0:8, :], weights[8:16, :], weights[16:24, :]
 
     def coefficients(charge):
@@ -239,7 +274,7 @@
         from_cos = product(rows_of(*v_cos), cos_high[...], cos_low[...], NN)
         from_sin = product(rows_of(*v_sin), sin_high[...], sin_low[...], NN)
         u_c, u_s, u_0 = (a + b for a, b in zip(from_cos, from_sin))
-        weighted = [b * q for b, q in zip(bond, charge)]
+        weighted = [everywhere(bond[j : j + 1, :]) * charge[j] for j in range(ranks)]
         relaxed = []
         total = blank
         for j in range(ranks):
@@ -250,14 +285,15 @@
             after = weighted[(j + 1) % ranks]
             lower = jnp.where(lane < 3 * width // 4, weighted[j], before)
             upper = jnp.where(lane >= width // 4, weighted[j], after)
-            place = (lane + got[j, 0:8, :].astype(jnp.int32)) & (width - 1)
             near = jnp.where(
                 lane < width // 2,
-                jnp.take_along_axis(lower, place, axis=1),
-                jnp.take_along_axis(upper, place, axis=1),
+                jnp.take_along_axis(lower, place[j], axis=1),
+                jnp.take_along_axis(upper, place[j], axis=1),
             )
-            new = (1.0 - mixing) * charge[j] - hard[j] * (
-                chi[j] + potential + bond[j] * column_sum(near)
+            new = (1.0 - mixing) * charge[j] - everywhere(hard[j : j + 1, :]) * (
+                everywhere(chi[j : j + 1, :])
+                + potential
+                + everywhere(bond[j : j + 1, :]) * column_sum(near)
             )
             relaxed.append(new)
             total = total + new
@@ -308,7 +344,6 @@
         mine[:, cut] = jnp.where(
             row == 0, fx, jnp.where(row == 1, fy, jnp.where(row == 2, fz, q[:, cut]))
         )
-    me = rank_ref[0] % beads
     for t in range(beads):
         there = pl.multiple_of(partner(me, t, beads) * width, width)
         outs[t][...] = mine[0:4, pl.ds(there, width)]
@@ -338,6 +373,11 @@
 VMEM = pl.BlockSpec(memory_space=pltpu.VMEM)
 SMEM = pl.BlockSpec(memory_space=pltpu.SMEM)
 ANY = pl.BlockSpec(memory_space=pl.ANY)
+HBM = pl.BlockSpec(memory_space=pltpu.HBM)
+
+
+def stay(x):
+    return pltpu.with_memory_space_constraint(x, pltpu.HBM)
 
 
 def params(mebibytes):
@@ -368,13 +408,27 @@
     places = positions.transpose(1, 0, 2)
     speeds = velocities.transpose(1, 0, 2)
 
+    rank = lax.axis_index("atoms").astype(jnp.int32)[None]
+    def in_group(x, t):
+        pairs = [(r, r // beads * beads + partner(r % beads, t, beads)) for r in range(ranks)]
+        return lax.ppermute(x, "atoms", pairs)
+
+    lines = dims + 2 + neighbors.shape[0]
     packed = pl.pallas_call(
         functools.partial(pack_kernel, ranks),
-        out_shape=shape((ranks, 16, width), F32),
-        in_specs=[VMEM] * 4 + [SMEM] * 3,
+        out_shape=shape((ranks, lines, 1, width), F32),
+        in_specs=[HBM] * 4,
         out_specs=VMEM,
+        scratch_shapes=[
+            pltpu.VMEM(places.shape, F32),
+            pltpu.VMEM(charges_in.shape, F32),
+            pltpu.VMEM(kinds.shape, jnp.int32),
+            pltpu.VMEM(neighbors.shape, jnp.int32),
+            pltpu.SemaphoreType.DMA((4,)),
+        ],
+        compiler_params=params(4),
         name="pack",
-    )(places, charges_in, kinds, neighbors, chi_table, hard_table, bond_table)
+    )(*map(stay, (places, charges_in, kinds, neighbors)))
     got = lax.all_to_all(packed, "atoms", 0, 0, tiled=True)
 
     weights, edges, pull = pl.pallas_call(
@@ -399,11 +453,10 @@
         high = lax.ppermute(edges[:dims], "beads", [(b, a) for a, b in forward])
         low_at, high_at = 0, 0
 
-    rank = lax.axis_index("atoms").astype(jnp.int32)[None]
     results = pl.pallas_call(
         functools.partial(bead_kernel, scale, 1.0 / atoms, beads),
         out_shape=[shape((4, width), F32)] * beads,
-        in_specs=[SMEM, VMEM, ANY],
+        in_specs=[SMEM, ANY, VMEM] + [HBM] * 3,
         out_specs=[VMEM] * beads,
         scratch_shapes=[
             pltpu.VMEM((MODES, atoms), BF16),
@@ -416,17 +469,21 @@
             pltpu.VMEM((8, atoms), F32),
             pltpu.VMEM((24, MODES), F32),
             pltpu.VMEM((8, beads * width), F32),
-            pltpu.SemaphoreType.DMA,
+            pltpu.VMEM((ranks, width), F32),
+            pltpu.VMEM((ranks, width), F32),
+            pltpu.VMEM((ranks, width), F32),
+            pltpu.VMEM((ranks, width), F32),
+            pltpu.SMEM((SPECIES,), F32),
+            pltpu.SMEM((SPECIES,), F32),
+            pltpu.SMEM((SPECIES,), F32),
+            pltpu.SemaphoreType.DMA((4,)),
         ],
         compiler_params=params(24),
         name="bead",
         cost_estimate=pl.CostEstimate(flops=10**10, bytes_accessed=10**6, transcendentals=0),
-    )(rank, got, weights)
-
-    home = [results[0]]
-    for t in range(1, beads):
-        pairs = [(r, r // beads * beads + partner(r % beads, t, beads)) for r in range(ranks)]
-        home.append(lax.ppermute(results[t], "atoms", pairs))
+    )(rank, weights, got, *map(stay, (chi_table, hard_table, bond_table)))
+
+    home = [results[0]] + [in_group(results[t], t) for t in range(1, beads)]
 
     new_places, new_speeds, charge = pl.pallas_call(
         functools.partial(move_kernel, low_at, high_at),

time: 27.6 us -> 27.3 us (0.989)
  waiting for transfers between devices: 6.57 us -> 6.18 us
    all_to_all x1, waiting for transfers between devices: 4.78 us -> 4.39 us  [body(): got = lax.all_to_all(packed, 'atoms', 0, 0, tiled=True)]
    unnamed x14 -> x12, local copies, waits for them, and re-layouts: 0.64 us -> 0.65 us
where the time goes in v6:
time: 27.3 us; the launch traced here: 27 us
  starting transfers between devices  11 us (40%)
  Pallas kernels  8.38 us (31%)
  waiting for transfers between devices  6.18 us (23%)
  between operations  0.75 us (3%)
  local copies, waits for them, and re-layouts  0.65 us (2%)
    all_to_all x1, starting transfers between devices, body(): got = lax.all_to_all(packed, 'atoms', 0, 0, tiled=True)  7.5 us
    pallas_call x1, Pallas kernels, body(): pl.pallas_call(functools.partial(bead_kernel, scale, 1.0 / atoms, beads),...  5.42 us
    all_to_all x1, waiting for transfers between devices, body(): got = lax.all_to_all(packed, 'atoms', 0, 0, tiled=True)  4.39 us
    ppermute x3, starting transfers between devices, in_group(): return lax.ppermute(x, 'atoms', pairs)  1.93 us
    ppermute x3, waiting for transfers between devices, in_group(): return lax.ppermute(x, 'atoms', pairs)  1.79 us
    ppermute x1, starting transfers between devices, body(): low = high = lax.ppermute(edges, 'beads', [(0, 1), (1, 0)])  1.58 us
    pallas_call x1, Pallas kernels, body(): pl.pallas_call(functools.partial(pack_kernel, ranks), out_shape=shape((ra...  1.45 us
    pallas_call x1, Pallas kernels, body(): pl.pallas_call(weight_kernel, out_shape=(shape((24, MODES), F32), shape((...  0.89 us
  transfers between devices with their start and end apart: 5, of which 2 were waited for; matrix products, arithmetic and copies ran while one was open for 0% of the time, Pallas kernels for 23%

profile of v6, /device:TPU:0, one launch (start us, length us, event | category | flops | bytes accessed | tf_op | source)
XLA Modules:
  0.0 27.0 jit_solution(13209730668810442091)
XLA Ops:
  0.6 1.4 %pack.1.after = f32[16,13,1,128]{3,2,1,0:T(1,128)} custom-call(f32[3,4,128]{2,1,0:T(4,128)} %bitcast.7, f32[4,128]{1,0:T(4,128)} %charge_hbm.1, s32[1,128]{1,0:T(1,128)} %bitcast.11, s32[8,128]{1,0:T(8,128)} %neighbors_hbm.1), custom_call_target="tpu_custom_call" | custom-call | tf_op jit(solution)/shard_map/pack/pallas_call | solution.py:417
  2.1 0.0 copy-start
  2.1 0.0 copy-start.3
  2.1 0.0 copy-start.4
  2.1 7.5 %all-to-all-start = ((f32[16,13,1,128]{3,2,1,0:T(1,128)}), f32[16,13,1,128]{3,2,1,0:T(1,128)S(1)}, u32[]{:S(2)}, u32[]{:S(2)}) async-start(f32[16,13,1,128]{3,2,1,0:T(1,128)} %pack.1.after), calls=%async_computation | async-start | bytes 212992 | tf_op jit(solution)/shard_map/all_to_all | solution.py:432
  9.6 0.0 copy-start.2
  9.6 0.0 copy-start.5
  9.7 0.0 copy-done
  9.7 0.0 copy-done.3
  9.7 0.0 copy-done.4
  9.7 0.6 %copy-done.2 = s32[128]{0:T(128)S(1)} copy-done((s32[128]{0:T(128)S(1)}, s32[128]{0:T(128)}, u32[]{:S(2)}) %copy-start.2) | copy-done | bytes 536
  10.3 0.0 copy-done.5
  10.3 0.9 %weights.1 = (f32[24,160]{1,0:T(8,128)S(1)}, f32[6,128]{1,0:T(8,128)S(1)}, f32[1,128]{1,0:T(1,128)S(1)}) custom-call(s32[3,2048]{1,0:T(4,128)S(1)} %copy-done.3, f32[1,2048]{1,0:T(1,128)S(1)} %bitcast.13, f32[3,4,128]{2,1,0:T(4,128)S(1)} %bitcast.8, s32[1,128]{1,0:T(1,128)S(1)} %bitcast.12, f32[8]{0:T(128)S(1)} %copy-done.5, f32[16,13,1,128]{3,2,1,0:T(1,128)} %pack.1.after), custom_call_target="tpu_custom_call" | custom-call | flops 1000000000 | bytes 100000 | tf_op jit(solution)/shard_map/weights/pallas_call | solution.py:434
  11.2 1.6 %collective-permute-start = (f32[6,128]{1,0:T(8,128)S(1)}, f32[6,128]{1,0:T(8,128)S(1)}, u32[]{:S(2)}, u32[]{:S(2)}) collective-permute-start(f32[6,128]{1,0:T(8,128)S(1)} %get-tuple-element.13), channel_id=1, source_target_pairs={{0,1},{1,0},{2,3},{3,2},{4,5},{5,4},{6,7},{7,6},{8,9},{9,8},{10,11... | collective-permute-start | bytes 9224 | tf_op jit(solution)/shard_map/ppermute | solution.py:448
  12.8 4.4 %all-to-all-done.got = f32[16,13,1,128]{3,2,1,0:T(1,128)S(1)} async-done(((f32[16,13,1,128]{3,2,1,0:T(1,128)}), f32[16,13,1,128]{3,2,1,0:T(1,128)S(1)}, u32[]{:S(2)}, u32[]{:S(2)}) %all-to-all-start) | async-done | bytes 106528 | tf_op jit(solution)/shard_map/all_to_all | solution.py:432
  17.2 5.4 %bead.1 = (f32[4,128]{1,0:T(4,128)S(1)}, f32[4,128]{1,0:T(4,128)S(1)}, f32[4,128]{1,0:T(4,128)S(1)}, f32[4,128]{1,0:T(4,128)S(1)}) custom-call(s32[1]{0:T(128)} %bitcast.rank_ref, f32[24,160]{1,0:T(8,128)S(1)} %get-tuple-element.15.weights_hbm, f32[16,13,1,128]{3,2,1,0:T(1,128)S(1)} %all-to-all-done.got, f32[8]{0:T(128)} %chi_hbm.1, f32[8]{0:T(128)} %hard_hbm.1, ...), custom_call_target="tpu_custom_call" | custom-call | flops 10000000000 | bytes 1000000 | tf_op jit(solution)/shard_map/bead/pallas_call | solution.py:456
  22.6 0.0 copy-start.1
  22.6 0.1 collective-permute-start.1
  22.7 0.1 collective-permute-start.2
  22.8 1.8 %collective-permute-start.3 = (f32[4,128]{1,0:T(4,128)S(1)}, f32[4,128]{1,0:T(4,128)S(1)}, u32[]{:S(2)}, u32[]{:S(2)}) collective-permute-start(f32[4,128]{1,0:T(4,128)S(1)} %get-tuple-element.19), channel_id=1, source_target_pairs={{0,6},{2,4},{4,2},{6,0},{8,14},{10,12},{12,10},{14,8},{16,22},{18,... | collective-permute-start | bytes 6152 | tf_op jit(solution)/shard_map/ppermute | solution.py:414
  24.6 0.0 collective-permute-done.low.high
  24.6 0.0 collective-permute-done.1.refs_1_
  24.6 1.8 %collective-permute-done.2.refs_2_ = f32[4,128]{1,0:T(4,128)S(1)} collective-permute-done((f32[4,128]{1,0:T(4,128)S(1)}, f32[4,128]{1,0:T(4,128)S(1)}, u32[]{:S(2)}, u32[]{:S(2)}) %collective-permute-start.2) | collective-permute-done | bytes 2080 | tf_op jit(solution)/shard_map/ppermute | solution.py:414
  26.3 0.0 collective-permute-done.3.refs_3_
  26.3 0.0 copy-done.1
  26.4 0.6 %move.1 = (f32[3,4,128]{2,1,0:T(4,128)}, f32[3,4,128]{2,1,0:T(4,128)}, f32[4,128]{1,0:T(4,128)}) custom-call(s32[1]{0:T(128)} %bitcast.rank_ref, f32[3,4,128]{2,1,0:T(4,128)S(1)} %bitcast.9, f32[3,4,128]{2,1,0:T(4,128)S(1)} %bitcast.10, f32[6,128]{1,0:T(8,128)S(1)} %collective-permute-done.low.high, f32[6,128]{1,0:T(8,128)S(1)} %collective-permute-done.low.high, ...), custom_call_target="tpu_custom_call" | custom-call | tf_op jit(solution)/shard_map/move/pallas_call | solution.py:488
Async XLA Ops:
  2.1 7.6 %copy-start = (f32[4,3,128]{2,0,1:T(4,128)S(1)}, f32[4,3,128]{2,0,1:T(4,128)}, u32[]{:S(2)}) copy-start(f32[4,3,128]{2,0,1:T(4,128)} %param.11) | copy-start | bytes 18436
  2.1 7.6 %copy-start.3 = (s32[3,2048]{1,0:T(4,128)S(1)}, s32[3,2048]{1,0:T(4,128)}, u32[]{:S(2)}) copy-start(s32[3,2048]{1,0:T(4,128)} %k_index.1) | copy-start | bytes 73732
  2.1 7.6 %copy-start.4 = (f32[2048]{0:T(1024)S(1)}, f32[2048]{0:T(1024)}, u32[]{:S(2)}) copy-start(f32[2048]{0:T(1024)} %param.17) | copy-start | bytes 24580
  2.1 15.0 %all-to-all-start = ((f32[16,13,1,128]{3,2,1,0:T(1,128)}), f32[16,13,1,128]{3,2,1,0:T(1,128)S(1)}, u32[]{:S(2)}, u32[]{:S(2)}) async-start(f32[16,13,1,128]{3,2,1,0:T(1,128)} %pack.1.after), calls=%async_computation | async-start | bytes 212992 | tf_op jit(solution)/shard_map/all_to_all | solution.py:432
  9.6 0.7 %copy-start.2 = (s32[128]{0:T(128)S(1)}, s32[128]{0:T(128)}, u32[]{:S(2)}) copy-start(s32[128]{0:T(128)} %param.14) | copy-start | bytes 1540
  9.6 0.7 %copy-start.5 = (f32[8]{0:T(128)S(1)}, f32[8]{0:T(128)}, u32[]{:S(2)}) copy-start(f32[8]{0:T(128)} %mass_table.1) | copy-start | bytes 100
  11.2 13.4 %collective-permute-start = (f32[6,128]{1,0:T(8,128)S(1)}, f32[6,128]{1,0:T(8,128)S(1)}, u32[]{:S(2)}, u32[]{:S(2)}) collective-permute-start(f32[6,128]{1,0:T(8,128)S(1)} %get-tuple-element.13), channel_id=1, source_target_pairs={{0,1},{1,0},{2,3},{3,2},{4,5},{5,4},{6,7},{7,6},{8,9},{9,8},{10,11... | collective-permute-start | bytes 9224 | tf_op jit(solution)/shard_map/ppermute | solution.py:448
  22.6 3.7 %copy-start.1 = (f32[4,3,128]{2,0,1:T(4,128)S(1)}, f32[4,3,128]{2,0,1:T(4,128)}, u32[]{:S(2)}) copy-start(f32[4,3,128]{2,0,1:T(4,128)} %param.12) | copy-start | bytes 18436
  22.6 1.9 %collective-permute-start.1 = (f32[4,128]{1,0:T(4,128)S(1)}, f32[4,128]{1,0:T(4,128)S(1)}, u32[]{:S(2)}, u32[]{:S(2)}) collective-permute-start(f32[4,128]{1,0:T(4,128)S(1)} %get-tuple-element.17), channel_id=1, source_target_pairs={{0,2},{2,0},{4,6},{6,4},{8,10},{10,8},{12,14},{14,12},{16,18},{18,... | collective-permute-start | bytes 6152 | tf_op jit(solution)/shard_map/ppermute | solution.py:414
  22.7 3.7 %collective-permute-start.2 = (f32[4,128]{1,0:T(4,128)S(1)}, f32[4,128]{1,0:T(4,128)S(1)}, u32[]{:S(2)}, u32[]{:S(2)}) collective-permute-start(f32[4,128]{1,0:T(4,128)S(1)} %get-tuple-element.18), channel_id=1, source_target_pairs={{0,4},{2,6},{4,0},{6,2},{8,12},{10,14},{12,8},{14,10},{16,20},{18,... | collective-permute-start | bytes 6152 | tf_op jit(solution)/shard_map/ppermute | solution.py:414
  22.8 3.6 %collective-permute-start.3 = (f32[4,128]{1,0:T(4,128)S(1)}, f32[4,128]{1,0:T(4,128)S(1)}, u32[]{:S(2)}, u32[]{:S(2)}) collective-permute-start(f32[4,128]{1,0:T(4,128)S(1)} %get-tuple-element.19), channel_id=1, source_target_pairs={{0,6},{2,4},{4,2},{6,0},{8,14},{10,12},{12,10},{14,8},{16,22},{18,... | collective-permute-start | bytes 6152 | tf_op jit(solution)/shard_map/ppermute | solution.py:414

commit v7 on v6

--- a/solution.py
+++ b/solution.py
@@ -12,7 +12,9 @@
 QITERS = 2
 SPECIES = 8
 KMAX = 8
-MODES = 160
+MODES = 128
+REST = 32
+ROWS = 4 * (MODES + REST)
 
 two_pi = 2.0 * math.pi
 ewald_gain = 4.0
@@ -72,17 +74,8 @@
     return jnp.concatenate([high, both, low], 0)
 
 
-def product(left, high, low, dims):
-    main = lax.dot_general(left, high, dims, preferred_element_type=F32)
-    one = main[0:8] + main[32:40]
-    two = main[8:16] + main[40:48]
-    rest = main[16:24] + main[24:32]
-    if low is not None:
-        minor = lax.dot_general(left[0:32], low, dims, preferred_element_type=F32)
-        one = one + minor[0:8]
-        two = two + minor[8:16]
-        rest = rest + minor[16:24]
-    return one, two, rest
+def summed(x):
+    return x[0:8] + x[32:40], x[8:16] + x[40:48], x[16:24] + x[24:32]
 
 
 def partner(me, t, count):
@@ -140,7 +133,8 @@
     with_p = jnp.where(q > 0, wide + q - 1, jnp.where(q < 0, wide + 7 - q, 135 + p))
     without_p = jnp.where(q > 0, 127 + q, 144)
     mode = jnp.where(p > 0, with_p, without_p)
-    at = lax.broadcasted_iota(jnp.int32, (MODES, count), 0)
+    at = lax.broadcasted_iota(jnp.int32, (MODES + 4 * REST, count), 0)
+    at = jnp.where(at < MODES, at, MODES + (at & (REST - 1)))
     chosen = jnp.where(at == mode, 1.0, 0.0).astype(BF16)
     row = lax.broadcasted_iota(jnp.int32, (8, count), 0)
     weight = kernel[...]
@@ -148,9 +142,12 @@
     even = jnp.where(here, weight, 0.0)
     odd = jnp.where(here, jnp.where(r < 0, -weight, weight), 0.0)
     zero = jnp.where((row == 0) & (r == 0), weight, 0.0)
-    even, odd, zero = product(rows_of(even, odd, zero), chosen, None, NT)
+    even, odd, zero = summed(
+        lax.dot_general(rows_of(even, odd, zero), chosen, NT, preferred_element_type=F32)
+    )
+    lane = lax.broadcasted_iota(jnp.int32, even.shape, 1)
     out[0:8, :] = even
-    out[8:16, :] = odd
+    out[8:16, :] = jnp.where((lane >= MODES) & (lane < MODES + 2 * REST), -odd, odd)
     out[16:24, :] = zero
 
 
@@ -168,10 +165,7 @@
 ):
     outs = refs[:beads]
     (
-        cos_high,
-        cos_low,
-        sin_high,
-        sin_low,
+        table,
         left,
         z_cos,
         z_sin,
@@ -225,25 +219,23 @@
         z_cos[:, at(j)] = cz
         z_sin[:, at(j)] = sz
 
-        def keep(rows, cosine, sine):
-            high, low = halves(cosine)
-            cos_high[rows, at(j)] = high
-            cos_low[rows, at(j)] = low
-            high, low = halves(sine)
-            sin_high[rows, at(j)] = high
-            sin_low[rows, at(j)] = low
+        def keep(start, step, cosine, sine):
+            for part, x in enumerate(halves(cosine) + halves(sine)):
+                table[start + part * step : start + part * step + 16, at(j)] = x
 
         for p in range(8):
             cp, sp = everywhere(cx[p : p + 1]), everywhere(sx[p : p + 1])
             cc, ss, sc, cs = cp * cy, sp * sy, sp * cy, cp * sy
             keep(
-                slice(16 * p, 16 * p + 16),
+                16 * p,
+                MODES,
                 jnp.concatenate([cc - ss, cc + ss], 0),
                 jnp.concatenate([sc + cs, sc - cs], 0),
             )
-        keep(slice(128, 144), jnp.concatenate([cy, cx], 0), jnp.concatenate([sy, sx], 0))
+        keep(4 * MODES, REST, jnp.concatenate([cy, cx], 0), jnp.concatenate([sy, sx], 0))
         keep(
-            slice(144, 160),
+            4 * MODES + 16,
+            REST,
             jnp.concatenate([single, blank], 0),
             jnp.concatenate([blank, blank], 0),
         )
@@ -257,23 +249,53 @@
     chi[...], hardness, bond[...] = lookup((chi_table, hard_table, bond_table), kinds[...])
     hard[...] = mixing / hardness
     even, odd, zero = weights[0:8, :], weights[8:16, :], weights[16:24, :]
+    tile = lax.broadcasted_iota(jnp.int32, (8, 4 * REST), 1)
+    is_sum = (tile & REST) == 0
+    sign = jnp.where(tile < 2 * REST, -1.0, 1.0)
+    main, rest = slice(0, MODES), slice(MODES, MODES + 4 * REST)
+
+    def turned(x, lanes):
+        return jnp.concatenate([x[:, lanes:], x[:, :lanes]], 1)
+
+    def folded(x):
+        cosine = x[:, 0:MODES] + x[:, MODES : 2 * MODES]
+        sine = x[:, 2 * MODES : 3 * MODES] + x[:, 3 * MODES : 4 * MODES]
+        last = x[:, 4 * MODES :]
+        last = jnp.where(is_sum, last + turned(last, REST), 0.0)
+        return cosine, sine, last + turned(last, 3 * REST)
 
     def coefficients(charge):
         for j in range(ranks):
             left[:, at(j)] = rows_of(
                 charge[j] * z_cos[:, at(j)], charge[j] * z_sin[:, at(j)], charge[j] * single
             )
-        t_cc, t_cs, t_c0 = product(left[...], cos_high[...], cos_low[...], NT)
-        t_sc, t_ss, t_s0 = product(left[...], sin_high[...], sin_low[...], NT)
-        v_cos = (even * t_cc - odd * t_ss, even * t_cs + odd * t_sc, zero * t_c0)
-        v_sin = (even * t_sc + odd * t_cs, even * t_ss - odd * t_cc, zero * t_s0)
-        return v_cos, v_sin
+        products = lax.dot_general(left[...], table[...], NT, preferred_element_type=F32)
+        (t_cc, t_sc, r_c), (t_cs, t_ss, r_s), (t_c0, t_s0, r_0) = map(folded, summed(products))
+        w, o, z = even[:, main], odd[:, main], zero[:, main]
+        wr, signed, zr = even[:, rest], odd[:, rest], zero[:, rest]
+        with_cos = (
+            w * t_cc - o * t_ss,
+            w * t_sc + o * t_cs,
+            wr * r_c + signed * turned(r_s, 2 * REST),
+        )
+        with_sin = (
+            w * t_cs + o * t_sc,
+            w * t_ss - o * t_cc,
+            wr * r_s - signed * turned(r_c, 2 * REST),
+        )
+        alone = (z * t_c0, z * t_s0, zr * r_0)
+        return with_cos, with_sin, alone
+
+    def matrix(parts):
+        x = rows_of(*(jnp.concatenate(part, 1) for part in parts))
+        cosine, sine, last = x[:, 0:MODES], x[:, MODES : 2 * MODES], x[:, 2 * MODES :]
+        return jnp.concatenate([cosine, cosine, sine, sine, last], 1)
 
     for rounds in range(QITERS):
-        v_cos, v_sin = coefficients(charge)
-        from_cos = product(rows_of(*v_cos), cos_high[...], cos_low[...], NN)
-        from_sin = product(rows_of(*v_sin), sin_high[...], sin_low[...], NN)
-        u_c, u_s, u_0 = (a + b for a, b in zip(from_cos, from_sin))
+        products = lax.dot_general(
+            matrix(coefficients(charge)), table[...], NN, preferred_element_type=F32
+        )
+        u_c, u_s, u_0 = summed(products)
         weighted = [everywhere(bond[j : j + 1, :]) * charge[j] for j in range(ranks)]
         relaxed = []
         total = blank
@@ -302,37 +324,42 @@
 
     for j in range(ranks):
         charges[:, at(j)] = charge[j]
-    (v_cc, v_cs, v_c0), (v_sc, v_ss, v_s0) = coefficients(charge)
+    parts = coefficients(charge)
     mode = lax.broadcasted_iota(jnp.int32, (8, MODES), 1)
     inner = mode & 15
-    wave_x = jnp.where(
-        mode < 128, (mode >> 4) + 1, jnp.where((mode >= 136) & (mode < 144), mode - 135, 0)
-    ).astype(F32)
-    wave_y = jnp.where(
-        mode < 128,
-        jnp.where(inner < 8, inner + 1, 7 - inner),
-        jnp.where(mode < 136, mode - 127, 0),
-    ).astype(F32)
+    few = tile & (REST - 1)
+    waves = (
+        (
+            (mode >> 4) + 1,
+            jnp.where((few >= 8) & (few < 16), few - 7, 0),
+        ),
+        (
+            jnp.where(inner < 8, inner + 1, 7 - inner),
+            jnp.where(few < 8, few + 1, 0),
+        ),
+    )
+
+    def slope(part, wave):
+        cosine, sine, last = part
+        for_main, for_rest = (x.astype(F32) for x in wave)
+        return -for_main * sine, for_main * cosine, sign * for_rest * turned(last, 2 * REST)
+
+    stacked = [matrix([slope(part, wave) for part in parts]) for wave in waves]
     span = beads * width
     base = pl.multiple_of((rank_ref[0] // beads) * span, span)
     own = pl.ds(base, span)
-    ch, cl, sh, sl = (ref[:, own] for ref in (cos_high, cos_low, sin_high, sin_low))
     zc, zs, q = z_cos[:, own], z_sin[:, own], charges[:, own]
-
-    def field(for_cos, for_sin):
-        a = product(rows_of(*for_cos), ch, cl, NN)
-        b = product(rows_of(*for_sin), sh, sl, NN)
-        return (one + two for one, two in zip(a, b))
-
-    def force(wave):
-        u_c, u_s, u_0 = field(
-            (-wave * v_sc, -wave * v_ss, -wave * v_s0), (wave * v_cc, wave * v_cs, wave * v_c0)
-        )
-        return zc * u_c + zs * u_s + u_0
-
-    along_x = force(wave_x)
-    along_y = force(wave_y)
-    u_c, u_s, _ = field((v_cc, v_cs, v_c0), (v_sc, v_ss, v_s0))
+    products = lax.dot_general(
+        jnp.concatenate(stacked + [matrix(parts)], 0),
+        table[:, own],
+        NN,
+        preferred_element_type=F32,
+    )
+    (x_c, x_s, x_0), (y_c, y_s, y_0), (u_c, u_s, _) = (
+        summed(products[48 * i : 48 * i + 48]) for i in range(3)
+    )
+    along_x = zc * x_c + zs * x_s + x_0
+    along_y = zc * y_c + zs * y_s + y_0
     wide_multiple = jnp.broadcast_to(multiple[:, 0:1], (8, span))
     along_z = wide_multiple * (zs * u_c - zc * u_s)
     factor = (two_pi * scale) * q
@@ -434,7 +461,7 @@
     weights, edges, pull = pl.pallas_call(
         weight_kernel,
         out_shape=(
-            shape((24, MODES), F32),
+            shape((24, MODES + 4 * REST), F32),
             shape((2 * dims, width), F32),
             shape((1, width), F32),
         ),
@@ -459,15 +486,12 @@
         in_specs=[SMEM, ANY, VMEM] + [HBM] * 3,
         out_specs=[VMEM] * beads,
         scratch_shapes=[
-            pltpu.VMEM((MODES, atoms), BF16),
-            pltpu.VMEM((MODES, atoms), BF16),
-            pltpu.VMEM((MODES, atoms), BF16),
-            pltpu.VMEM((MODES, atoms), BF16),
+            pltpu.VMEM((ROWS, atoms), BF16),
             pltpu.VMEM((48, atoms), BF16),
             pltpu.VMEM((8, atoms), F32),
             pltpu.VMEM((8, atoms), F32),
             pltpu.VMEM((8, atoms), F32),
-            pltpu.VMEM((24, MODES), F32),
+            pltpu.VMEM((24, MODES + 4 * REST), F32),
             pltpu.VMEM((8, beads * width), F32),
             pltpu.VMEM((ranks, width), F32),
             pltpu.VMEM((ranks, width), F32),

time: 27.3 us -> 28.2 us (1.033)
  Pallas kernels: 8.38 us -> 9.44 us
    pallas_call x1, Pallas kernels: 5.42 us -> 6.38 us  [body(): pl.pallas_call(functools.partial(bead_kernel, scale, 1.0 / atoms, beads),...]
  transfers between devices with their start and end apart: 5 -> 5, of which waited for: 2 -> 2; matrix products, arithmetic and copies ran while one was open for 0% -> 0% of each run, Pallas kernels for 23% -> 26%
where the time goes in v7:
time: 28.2 us; the launch traced here: 27.9 us
  starting transfers between devices  11 us (39%)
  Pallas kernels  9.44 us (33%)
  waiting for transfers between devices  6.07 us (22%)
  between operations  0.75 us (3%)
  local copies, waits for them, and re-layouts  0.65 us (2%)
    all_to_all x1, starting transfers between devices, body(): got = lax.all_to_all(packed, 'atoms', 0, 0, tiled=True)  7.5 us
    pallas_call x1, Pallas kernels, body(): pl.pallas_call(functools.partial(bead_kernel, scale, 1.0 / atoms, beads),...  6.38 us
    all_to_all x1, waiting for transfers between devices, body(): got = lax.all_to_all(packed, 'atoms', 0, 0, tiled=True)  4.28 us
    ppermute x3, starting transfers between devices, in_group(): return lax.ppermute(x, 'atoms', pairs)  1.93 us
    ppermute x3, waiting for transfers between devices, in_group(): return lax.ppermute(x, 'atoms', pairs)  1.79 us
    ppermute x1, starting transfers between devices, body(): low = high = lax.ppermute(edges, 'beads', [(0, 1), (1, 0)])  1.59 us
    pallas_call x1, Pallas kernels, body(): pl.pallas_call(functools.partial(pack_kernel, ranks), out_shape=shape((ra...  1.45 us
    pallas_call x1, Pallas kernels, body(): pl.pallas_call(weight_kernel, out_shape=(shape((24, MODES + 4 * REST), F3...  0.99 us
  transfers between devices with their start and end apart: 5, of which 2 were waited for; matrix products, arithmetic and copies ran while one was open for 0% of the time, Pallas kernels for 26%

profile of v7, /device:TPU:0, one launch (start us, length us, event | category | flops | bytes accessed | tf_op | source)
XLA Modules:
  0.0 27.9 jit_solution(12043796474184573515)
XLA Ops:
  0.6 1.4 %pack.1.after = f32[16,13,1,128]{3,2,1,0:T(1,128)} custom-call(f32[3,4,128]{2,1,0:T(4,128)} %bitcast.7, f32[4,128]{1,0:T(4,128)} %charge_hbm.1, s32[1,128]{1,0:T(1,128)} %bitcast.11, s32[8,128]{1,0:T(8,128)} %neighbors_hbm.1), custom_call_target="tpu_custom_call" | custom-call | tf_op jit(solution)/shard_map/pack/pallas_call | solution.py:444
  2.1 0.0 copy-start
  2.1 0.0 copy-start.3
  2.1 0.0 copy-start.4
  2.1 7.5 %all-to-all-start = ((f32[16,13,1,128]{3,2,1,0:T(1,128)}), f32[16,13,1,128]{3,2,1,0:T(1,128)S(1)}, u32[]{:S(2)}, u32[]{:S(2)}) async-start(f32[16,13,1,128]{3,2,1,0:T(1,128)} %pack.1.after), calls=%async_computation | async-start | bytes 212992 | tf_op jit(solution)/shard_map/all_to_all | solution.py:459
  9.6 0.0 copy-start.2
  9.6 0.0 copy-start.5
  9.7 0.0 copy-done
  9.7 0.0 copy-done.3
  9.7 0.0 copy-done.4
  9.7 0.6 %copy-done.2 = s32[128]{0:T(128)S(1)} copy-done((s32[128]{0:T(128)S(1)}, s32[128]{0:T(128)}, u32[]{:S(2)}) %copy-start.2) | copy-done | bytes 536
  10.3 0.0 copy-done.5
  10.3 1.0 %weights.1 = (f32[24,256]{1,0:T(8,128)S(1)}, f32[6,128]{1,0:T(8,128)S(1)}, f32[1,128]{1,0:T(1,128)S(1)}) custom-call(s32[3,2048]{1,0:T(4,128)S(1)} %copy-done.3, f32[1,2048]{1,0:T(1,128)S(1)} %bitcast.13, f32[3,4,128]{2,1,0:T(4,128)S(1)} %bitcast.8, s32[1,128]{1,0:T(1,128)S(1)} %bitcast.12, f32[8]{0:T(128)S(1)} %copy-done.5, f32[16,13,1,128]{3,2,1,0:T(1,128)} %pack.1.after), custom_call_target="tpu_custom_call" | custom-call | flops 1000000000 | bytes 100000 | tf_op jit(solution)/shard_map/weights/pallas_call | solution.py:461
  11.3 1.6 %collective-permute-start = (f32[6,128]{1,0:T(8,128)S(1)}, f32[6,128]{1,0:T(8,128)S(1)}, u32[]{:S(2)}, u32[]{:S(2)}) collective-permute-start(f32[6,128]{1,0:T(8,128)S(1)} %get-tuple-element.13), channel_id=1, source_target_pairs={{0,1},{1,0},{2,3},{3,2},{4,5},{5,4},{6,7},{7,6},{8,9},{9,8},{10,11... | collective-permute-start | bytes 9224 | tf_op jit(solution)/shard_map/ppermute | solution.py:475
  12.9 4.3 %all-to-all-done.got = f32[16,13,1,128]{3,2,1,0:T(1,128)S(1)} async-done(((f32[16,13,1,128]{3,2,1,0:T(1,128)}), f32[16,13,1,128]{3,2,1,0:T(1,128)S(1)}, u32[]{:S(2)}, u32[]{:S(2)}) %all-to-all-start) | async-done | bytes 106528 | tf_op jit(solution)/shard_map/all_to_all | solution.py:459
  17.2 6.4 %bead.1 = (f32[4,128]{1,0:T(4,128)S(1)}, f32[4,128]{1,0:T(4,128)S(1)}, f32[4,128]{1,0:T(4,128)S(1)}, f32[4,128]{1,0:T(4,128)S(1)}) custom-call(s32[1]{0:T(128)} %bitcast.rank_ref, f32[24,256]{1,0:T(8,128)S(1)} %get-tuple-element.15.weights_hbm, f32[16,13,1,128]{3,2,1,0:T(1,128)S(1)} %all-to-all-done.got, f32[8]{0:T(128)} %chi_hbm.1, f32[8]{0:T(128)} %hard_hbm.1, ...), custom_call_target="tpu_custom_call" | custom-call | flops 10000000000 | bytes 1000000 | tf_op jit(solution)/shard_map/bead/pallas_call | solution.py:483
  23.6 0.0 copy-start.1
  23.6 0.1 collective-permute-start.1
  23.6 0.1 collective-permute-start.2
  23.7 1.8 %collective-permute-start.3 = (f32[4,128]{1,0:T(4,128)S(1)}, f32[4,128]{1,0:T(4,128)S(1)}, u32[]{:S(2)}, u32[]{:S(2)}) collective-permute-start(f32[4,128]{1,0:T(4,128)S(1)} %get-tuple-element.19), channel_id=1, source_target_pairs={{0,6},{2,4},{4,2},{6,0},{8,14},{10,12},{12,10},{14,8},{16,22},{18,... | collective-permute-start | bytes 6152 | tf_op jit(solution)/shard_map/ppermute | solution.py:441
  25.5 0.0 collective-permute-done.low.high
  25.5 0.0 collective-permute-done.1.refs_1_
  25.5 1.8 %collective-permute-done.2.refs_2_ = f32[4,128]{1,0:T(4,128)S(1)} collective-permute-done((f32[4,128]{1,0:T(4,128)S(1)}, f32[4,128]{1,0:T(4,128)S(1)}, u32[]{:S(2)}, u32[]{:S(2)}) %collective-permute-start.2) | collective-permute-done | bytes 2080 | tf_op jit(solution)/shard_map/ppermute | solution.py:441
  27.3 0.0 collective-permute-done.3.refs_3_
  27.3 0.0 copy-done.1
  27.3 0.6 %move.1 = (f32[3,4,128]{2,1,0:T(4,128)}, f32[3,4,128]{2,1,0:T(4,128)}, f32[4,128]{1,0:T(4,128)}) custom-call(s32[1]{0:T(128)} %bitcast.rank_ref, f32[3,4,128]{2,1,0:T(4,128)S(1)} %bitcast.9, f32[3,4,128]{2,1,0:T(4,128)S(1)} %bitcast.10, f32[6,128]{1,0:T(8,128)S(1)} %collective-permute-done.low.high, f32[6,128]{1,0:T(8,128)S(1)} %collective-permute-done.low.high, ...), custom_call_target="tpu_custom_call" | custom-call | tf_op jit(solution)/shard_map/move/pallas_call | solution.py:512
Async XLA Ops:
  2.1 7.6 %copy-start = (f32[4,3,128]{2,0,1:T(4,128)S(1)}, f32[4,3,128]{2,0,1:T(4,128)}, u32[]{:S(2)}) copy-start(f32[4,3,128]{2,0,1:T(4,128)} %param.11) | copy-start | bytes 18436
  2.1 7.6 %copy-start.3 = (s32[3,2048]{1,0:T(4,128)S(1)}, s32[3,2048]{1,0:T(4,128)}, u32[]{:S(2)}) copy-start(s32[3,2048]{1,0:T(4,128)} %k_index.1) | copy-start | bytes 73732
  2.1 7.6 %copy-start.4 = (f32[2048]{0:T(1024)S(1)}, f32[2048]{0:T(1024)}, u32[]{:S(2)}) copy-start(f32[2048]{0:T(1024)} %param.17) | copy-start | bytes 24580
  2.1 15.0 %all-to-all-start = ((f32[16,13,1,128]{3,2,1,0:T(1,128)}), f32[16,13,1,128]{3,2,1,0:T(1,128)S(1)}, u32[]{:S(2)}, u32[]{:S(2)}) async-start(f32[16,13,1,128]{3,2,1,0:T(1,128)} %pack.1.after), calls=%async_computation | async-start | bytes 212992 | tf_op jit(solution)/shard_map/all_to_all | solution.py:459
  9.6 0.7 %copy-start.2 = (s32[128]{0:T(128)S(1)}, s32[128]{0:T(128)}, u32[]{:S(2)}) copy-start(s32[128]{0:T(128)} %param.14) | copy-start | bytes 1540
  9.6 0.7 %copy-start.5 = (f32[8]{0:T(128)S(1)}, f32[8]{0:T(128)}, u32[]{:S(2)}) copy-start(f32[8]{0:T(128)} %mass_table.1) | copy-start | bytes 100
  11.3 14.2 %collective-permute-start = (f32[6,128]{1,0:T(8,128)S(1)}, f32[6,128]{1,0:T(8,128)S(1)}, u32[]{:S(2)}, u32[]{:S(2)}) collective-permute-start(f32[6,128]{1,0:T(8,128)S(1)} %get-tuple-element.13), channel_id=1, source_target_pairs={{0,1},{1,0},{2,3},{3,2},{4,5},{5,4},{6,7},{7,6},{8,9},{9,8},{10,11... | collective-permute-start | bytes 9224 | tf_op jit(solution)/shard_map/ppermute | solution.py:475
  23.6 3.7 %copy-start.1 = (f32[4,3,128]{2,0,1:T(4,128)S(1)}, f32[4,3,128]{2,0,1:T(4,128)}, u32[]{:S(2)}) copy-start(f32[4,3,128]{2,0,1:T(4,128)} %param.12) | copy-start | bytes 18436
  23.6 1.9 %collective-permute-start.1 = (f32[4,128]{1,0:T(4,128)S(1)}, f32[4,128]{1,0:T(4,128)S(1)}, u32[]{:S(2)}, u32[]{:S(2)}) collective-permute-start(f32[4,128]{1,0:T(4,128)S(1)} %get-tuple-element.17), channel_id=1, source_target_pairs={{0,2},{2,0},{4,6},{6,4},{8,10},{10,8},{12,14},{14,12},{16,18},{18,... | collective-permute-start | bytes 6152 | tf_op jit(solution)/shard_map/ppermute | solution.py:441
  23.6 3.7 %collective-permute-start.2 = (f32[4,128]{1,0:T(4,128)S(1)}, f32[4,128]{1,0:T(4,128)S(1)}, u32[]{:S(2)}, u32[]{:S(2)}) collective-permute-start(f32[4,128]{1,0:T(4,128)S(1)} %get-tuple-element.18), channel_id=1, source_target_pairs={{0,4},{2,6},{4,0},{6,2},{8,12},{10,14},{12,8},{14,10},{16,20},{18,... | collective-permute-start | bytes 6152 | tf_op jit(solution)/shard_map/ppermute | solution.py:441
  23.7 3.6 %collective-permute-start.3 = (f32[4,128]{1,0:T(4,128)S(1)}, f32[4,128]{1,0:T(4,128)S(1)}, u32[]{:S(2)}, u32[]{:S(2)}) collective-permute-start(f32[4,128]{1,0:T(4,128)S(1)} %get-tuple-element.19), channel_id=1, source_target_pairs={{0,6},{2,4},{4,2},{6,0},{8,14},{10,12},{12,10},{14,8},{16,22},{18,... | collective-permute-start | bytes 6152 | tf_op jit(solution)/shard_map/ppermute | solution.py:441

commit v8 on v6

--- a/solution.py
+++ b/solution.py
@@ -319,20 +319,22 @@
     ch, cl, sh, sl = (ref[:, own] for ref in (cos_high, cos_low, sin_high, sin_low))
     zc, zs, q = z_cos[:, own], z_sin[:, own], charges[:, own]
 
-    def field(for_cos, for_sin):
-        a = product(rows_of(*for_cos), ch, cl, NN)
-        b = product(rows_of(*for_sin), sh, sl, NN)
-        return (one + two for one, two in zip(a, b))
-
-    def force(wave):
-        u_c, u_s, u_0 = field(
-            (-wave * v_sc, -wave * v_ss, -wave * v_s0), (wave * v_cc, wave * v_cs, wave * v_c0)
-        )
-        return zc * u_c + zs * u_s + u_0
-
-    along_x = force(wave_x)
-    along_y = force(wave_y)
-    u_c, u_s, _ = field((v_cc, v_cs, v_c0), (v_sc, v_ss, v_s0))
+    v_cos, v_sin = (v_cc, v_cs, v_c0), (v_sc, v_ss, v_s0)
+    for_cos, for_sin = [rows_of(*v_cos)], [rows_of(*v_sin)]
+    for wave in (wave_x, wave_y):
+        for_cos.append(rows_of(*(-wave * v for v in v_sin)))
+        for_sin.append(rows_of(*(wave * v for v in v_cos)))
+    for_cos, for_sin = jnp.concatenate(for_cos, 0), jnp.concatenate(for_sin, 0)
+    fields = sum(
+        lax.dot_general(rows, part, NN, preferred_element_type=F32)
+        for rows, part in ((for_cos, ch), (for_cos, cl), (for_sin, sh), (for_sin, sl))
+    )
+    (u_c, u_s, _), (x_c, x_s, x_0), (y_c, y_s, y_0) = (
+        (f[0:8] + f[32:40], f[8:16] + f[40:48], f[16:24] + f[24:32])
+        for f in (fields[48 * i : 48 * i + 48] for i in range(3))
+    )
+    along_x = zc * x_c + zs * x_s + x_0
+    along_y = zc * y_c + zs * y_s + y_0
     wide_multiple = jnp.broadcast_to(multiple[:, 0:1], (8, span))
     along_z = wide_multiple * (zs * u_c - zc * u_s)
     factor = (two_pi * scale) * q
@@ -416,7 +418,7 @@
     lines = dims + 2 + neighbors.shape[0]
     packed = pl.pallas_call(
         functools.partial(pack_kernel, ranks),
-        out_shape=shape((ranks, lines, 1, width), F32),
+        out_shape=pltpu.VMEM((ranks, lines, 1, width), F32),
         in_specs=[HBM] * 4,
         out_specs=VMEM,
         scratch_shapes=[
@@ -483,7 +485,8 @@
         cost_estimate=pl.CostEstimate(flops=10**10, bytes_accessed=10**6, transcendentals=0),
     )(rank, weights, got, *map(stay, (chi_table, hard_table, bond_table)))
 
-    home = [results[0]] + [in_group(results[t], t) for t in range(1, beads)]
+    home = [in_group(results[t], t) for t in range(beads - 1, 0, -1)]
+    home = [results[0]] + home[::-1]
 
     new_places, new_speeds, charge = pl.pallas_call(
         functools.partial(move_kernel, low_at, high_at),

time: 27.3 us -> 27.2 us (level)
  no operation moved by 1% of the time
where the time goes in v8:
time: 27.2 us; the launch traced here: 26.9 us
  starting transfers between devices  11 us (40%)
  Pallas kernels  8.31 us (31%)
  waiting for transfers between devices  6.18 us (23%)
  between operations  0.75 us (3%)
  local copies, waits for them, and re-layouts  0.65 us (2%)
    all_to_all x1, starting transfers between devices, body(): got = lax.all_to_all(packed, 'atoms', 0, 0, tiled=True)  7.5 us
    pallas_call x1, Pallas kernels, body(): pl.pallas_call(functools.partial(bead_kernel, scale, 1.0 / atoms, beads),...  5.35 us
    all_to_all x1, waiting for transfers between devices, body(): got = lax.all_to_all(packed, 'atoms', 0, 0, tiled=True)  4.39 us
    ppermute x3, starting transfers between devices, in_group(): return lax.ppermute(x, 'atoms', pairs)  1.93 us
    ppermute x3, waiting for transfers between devices, in_group(): return lax.ppermute(x, 'atoms', pairs)  1.79 us
    ppermute x1, starting transfers between devices, body(): low = high = lax.ppermute(edges, 'beads', [(0, 1), (1, 0)])  1.58 us
    pallas_call x1, Pallas kernels, body(): pl.pallas_call(functools.partial(pack_kernel, ranks), out_shape=pltpu.VME...  1.45 us
    pallas_call x1, Pallas kernels, body(): pl.pallas_call(weight_kernel, out_shape=(shape((24, MODES), F32), shape((...  0.89 us
  transfers between devices with their start and end apart: 5, of which 2 were waited for; matrix products, arithmetic and copies ran while one was open for 0% of the time, Pallas kernels for 23%

profile of v8, /device:TPU:0, one launch (start us, length us, event | category | flops | bytes accessed | tf_op | source)
XLA Modules:
  0.0 26.9 jit_solution(13820474433975881068)
XLA Ops:
  0.6 1.4 %pack.1.after = f32[16,13,1,128]{3,2,1,0:T(1,128)} custom-call(f32[3,4,128]{2,1,0:T(4,128)} %bitcast.7, f32[4,128]{1,0:T(4,128)} %charge_hbm.1, s32[1,128]{1,0:T(1,128)} %bitcast.11, s32[8,128]{1,0:T(8,128)} %neighbors_hbm.1), custom_call_target="tpu_custom_call" | custom-call | tf_op jit(solution)/shard_map/pack/pallas_call | solution.py:419
  2.1 0.0 copy-start
  2.1 0.0 copy-start.3
  2.1 0.0 copy-start.4
  2.1 7.5 %all-to-all-start = ((f32[16,13,1,128]{3,2,1,0:T(1,128)}), f32[16,13,1,128]{3,2,1,0:T(1,128)S(1)}, u32[]{:S(2)}, u32[]{:S(2)}) async-start(f32[16,13,1,128]{3,2,1,0:T(1,128)} %pack.1.after), calls=%async_computation | async-start | bytes 212992 | tf_op jit(solution)/shard_map/all_to_all | solution.py:434
  9.6 0.0 copy-start.2
  9.6 0.0 copy-start.5
  9.7 0.0 copy-done
  9.7 0.0 copy-done.3
  9.7 0.0 copy-done.4
  9.7 0.6 %copy-done.2 = s32[128]{0:T(128)S(1)} copy-done((s32[128]{0:T(128)S(1)}, s32[128]{0:T(128)}, u32[]{:S(2)}) %copy-start.2) | copy-done | bytes 536
  10.3 0.0 copy-done.5
  10.3 0.9 %weights.1 = (f32[24,160]{1,0:T(8,128)S(1)}, f32[6,128]{1,0:T(8,128)S(1)}, f32[1,128]{1,0:T(1,128)S(1)}) custom-call(s32[3,2048]{1,0:T(4,128)S(1)} %copy-done.3, f32[1,2048]{1,0:T(1,128)S(1)} %bitcast.13, f32[3,4,128]{2,1,0:T(4,128)S(1)} %bitcast.8, s32[1,128]{1,0:T(1,128)S(1)} %bitcast.12, f32[8]{0:T(128)S(1)} %copy-done.5, f32[16,13,1,128]{3,2,1,0:T(1,128)} %pack.1.after), custom_call_target="tpu_custom_call" | custom-call | flops 1000000000 | bytes 100000 | tf_op jit(solution)/shard_map/weights/pallas_call | solution.py:436
  11.2 1.6 %collective-permute-start = (f32[6,128]{1,0:T(8,128)S(1)}, f32[6,128]{1,0:T(8,128)S(1)}, u32[]{:S(2)}, u32[]{:S(2)}) collective-permute-start(f32[6,128]{1,0:T(8,128)S(1)} %get-tuple-element.13), channel_id=1, source_target_pairs={{0,1},{1,0},{2,3},{3,2},{4,5},{5,4},{6,7},{7,6},{8,9},{9,8},{10,11... | collective-permute-start | bytes 9224 | tf_op jit(solution)/shard_map/ppermute | solution.py:450
  12.8 4.4 %all-to-all-done.got = f32[16,13,1,128]{3,2,1,0:T(1,128)S(1)} async-done(((f32[16,13,1,128]{3,2,1,0:T(1,128)}), f32[16,13,1,128]{3,2,1,0:T(1,128)S(1)}, u32[]{:S(2)}, u32[]{:S(2)}) %all-to-all-start) | async-done | bytes 106528 | tf_op jit(solution)/shard_map/all_to_all | solution.py:434
  17.2 5.3 %bead.1 = (f32[4,128]{1,0:T(4,128)S(1)}, f32[4,128]{1,0:T(4,128)S(1)}, f32[4,128]{1,0:T(4,128)S(1)}, f32[4,128]{1,0:T(4,128)S(1)}) custom-call(s32[1]{0:T(128)} %bitcast.rank_ref, f32[24,160]{1,0:T(8,128)S(1)} %get-tuple-element.15.weights_hbm, f32[16,13,1,128]{3,2,1,0:T(1,128)S(1)} %all-to-all-done.got, f32[8]{0:T(128)} %chi_hbm.1, f32[8]{0:T(128)} %hard_hbm.1, ...), custom_call_target="tpu_custom_call" | custom-call | flops 10000000000 | bytes 1000000 | tf_op jit(solution)/shard_map/bead/pallas_call | solution.py:458
  22.5 0.0 copy-start.1
  22.5 0.1 collective-permute-start.1
  22.6 0.1 collective-permute-start.2
  22.7 1.8 %collective-permute-start.3 = (f32[4,128]{1,0:T(4,128)S(1)}, f32[4,128]{1,0:T(4,128)S(1)}, u32[]{:S(2)}, u32[]{:S(2)}) collective-permute-start(f32[4,128]{1,0:T(4,128)S(1)} %get-tuple-element.19), channel_id=1, source_target_pairs={{0,6},{2,4},{4,2},{6,0},{8,14},{10,12},{12,10},{14,8},{16,22},{18,... | collective-permute-start | bytes 6152 | tf_op jit(solution)/shard_map/ppermute | solution.py:416
  24.5 0.0 collective-permute-done.low.high
  24.5 0.0 collective-permute-done.1.refs_1_
  24.5 1.8 %collective-permute-done.2.refs_2_ = f32[4,128]{1,0:T(4,128)S(1)} collective-permute-done((f32[4,128]{1,0:T(4,128)S(1)}, f32[4,128]{1,0:T(4,128)S(1)}, u32[]{:S(2)}, u32[]{:S(2)}) %collective-permute-start.2) | collective-permute-done | bytes 2080 | tf_op jit(solution)/shard_map/ppermute | solution.py:416
  26.3 0.0 collective-permute-done.3.refs_3_
  26.3 0.0 copy-done.1
  26.3 0.6 %move.1 = (f32[3,4,128]{2,1,0:T(4,128)}, f32[3,4,128]{2,1,0:T(4,128)}, f32[4,128]{1,0:T(4,128)}) custom-call(s32[1]{0:T(128)} %bitcast.rank_ref, f32[3,4,128]{2,1,0:T(4,128)S(1)} %bitcast.9, f32[3,4,128]{2,1,0:T(4,128)S(1)} %bitcast.10, f32[6,128]{1,0:T(8,128)S(1)} %collective-permute-done.low.high, f32[6,128]{1,0:T(8,128)S(1)} %collective-permute-done.low.high, ...), custom_call_target="tpu_custom_call" | custom-call | tf_op jit(solution)/shard_map/move/pallas_call | solution.py:491
Async XLA Ops:
  2.1 7.6 %copy-start = (f32[4,3,128]{2,0,1:T(4,128)S(1)}, f32[4,3,128]{2,0,1:T(4,128)}, u32[]{:S(2)}) copy-start(f32[4,3,128]{2,0,1:T(4,128)} %param.11) | copy-start | bytes 18436
  2.1 7.6 %copy-start.3 = (s32[3,2048]{1,0:T(4,128)S(1)}, s32[3,2048]{1,0:T(4,128)}, u32[]{:S(2)}) copy-start(s32[3,2048]{1,0:T(4,128)} %k_index.1) | copy-start | bytes 73732
  2.1 7.6 %copy-start.4 = (f32[2048]{0:T(1024)S(1)}, f32[2048]{0:T(1024)}, u32[]{:S(2)}) copy-start(f32[2048]{0:T(1024)} %param.17) | copy-start | bytes 24580
  2.1 15.0 %all-to-all-start = ((f32[16,13,1,128]{3,2,1,0:T(1,128)}), f32[16,13,1,128]{3,2,1,0:T(1,128)S(1)}, u32[]{:S(2)}, u32[]{:S(2)}) async-start(f32[16,13,1,128]{3,2,1,0:T(1,128)} %pack.1.after), calls=%async_computation | async-start | bytes 212992 | tf_op jit(solution)/shard_map/all_to_all | solution.py:434
  9.6 0.7 %copy-start.2 = (s32[128]{0:T(128)S(1)}, s32[128]{0:T(128)}, u32[]{:S(2)}) copy-start(s32[128]{0:T(128)} %param.14) | copy-start | bytes 1540
  9.6 0.7 %copy-start.5 = (f32[8]{0:T(128)S(1)}, f32[8]{0:T(128)}, u32[]{:S(2)}) copy-start(f32[8]{0:T(128)} %mass_table.1) | copy-start | bytes 100
  11.2 13.3 %collective-permute-start = (f32[6,128]{1,0:T(8,128)S(1)}, f32[6,128]{1,0:T(8,128)S(1)}, u32[]{:S(2)}, u32[]{:S(2)}) collective-permute-start(f32[6,128]{1,0:T(8,128)S(1)} %get-tuple-element.13), channel_id=1, source_target_pairs={{0,1},{1,0},{2,3},{3,2},{4,5},{5,4},{6,7},{7,6},{8,9},{9,8},{10,11... | collective-permute-start | bytes 9224 | tf_op jit(solution)/shard_map/ppermute | solution.py:450
  22.5 3.7 %copy-start.1 = (f32[4,3,128]{2,0,1:T(4,128)S(1)}, f32[4,3,128]{2,0,1:T(4,128)}, u32[]{:S(2)}) copy-start(f32[4,3,128]{2,0,1:T(4,128)} %param.12) | copy-start | bytes 18436
  22.5 1.9 %collective-permute-start.1 = (f32[4,128]{1,0:T(4,128)S(1)}, f32[4,128]{1,0:T(4,128)S(1)}, u32[]{:S(2)}, u32[]{:S(2)}) collective-permute-start(f32[4,128]{1,0:T(4,128)S(1)} %get-tuple-element.17), channel_id=1, source_target_pairs={{0,2},{2,0},{4,6},{6,4},{8,10},{10,8},{12,14},{14,12},{16,18},{18,... | collective-permute-start | bytes 6152 | tf_op jit(solution)/shard_map/ppermute | solution.py:416
  22.6 3.7 %collective-permute-start.2 = (f32[4,128]{1,0:T(4,128)S(1)}, f32[4,128]{1,0:T(4,128)S(1)}, u32[]{:S(2)}, u32[]{:S(2)}) collective-permute-start(f32[4,128]{1,0:T(4,128)S(1)} %get-tuple-element.18), channel_id=1, source_target_pairs={{0,4},{2,6},{4,0},{6,2},{8,12},{10,14},{12,8},{14,10},{16,20},{18,... | collective-permute-start | bytes 6152 | tf_op jit(solution)/shard_map/ppermute | solution.py:416
  22.7 3.6 %collective-permute-start.3 = (f32[4,128]{1,0:T(4,128)S(1)}, f32[4,128]{1,0:T(4,128)S(1)}, u32[]{:S(2)}, u32[]{:S(2)}) collective-permute-start(f32[4,128]{1,0:T(4,128)S(1)} %get-tuple-element.19), channel_id=1, source_target_pairs={{0,6},{2,4},{4,2},{6,0},{8,14},{10,12},{12,10},{14,8},{16,22},{18,... | collective-permute-start | bytes 6152 | tf_op jit(solution)/shard_map/ppermute | solution.py:416

commit v9 on v8

--- a/solution.py
+++ b/solution.py
@@ -100,7 +100,17 @@
 
 
 def pack_kernel(
-    ranks, pos_hbm, charge_hbm, species_hbm, neighbors_hbm, out, pos, charge, species, neighbors, arrived
+    ranks,
+    pos_hbm,
+    charge_hbm,
+    species_hbm,
+    neighbors_hbm,
+    out,
+    pos,
+    charge,
+    species,
+    neighbors,
+    arrived,
 ):
     sources = (pos_hbm, charge_hbm, species_hbm, neighbors_hbm)
     targets = (pos, charge, species, neighbors)
@@ -114,12 +124,16 @@
         copy.wait()
     dims, beads, _ = pos.shape
     near = neighbors[...].astype(F32)
-    shared = [species[...].astype(F32)] + [near[n : n + 1, :] for n in range(near.shape[0])]
+    spec = species[...].astype(F32)
     for b in range(beads):
-        own = [pos[d, b : b + 1, :] for d in range(dims)] + [charge[b : b + 1, :]]
-        for rank in range(b, ranks, beads):
-            for i, line in enumerate(own + shared):
-                out[rank, i] = line
+        for d in range(dims):
+            out[b, d] = pos[d, b : b + 1, :]
+        out[b, dims] = charge[b : b + 1, :]
+        out[b, dims + 1] = spec
+        for n in range(near.shape[0]):
+            out[b, dims + 2 + n] = near[n : n + 1, :]
+    for rank in range(beads, ranks):
+        out[rank] = out[rank % beads]
 
 
 def weight_kernel(k_index, kernel, pos, species, mass_table, after, out, edges, pull):
@@ -271,16 +285,19 @@
 
     for rounds in range(QITERS):
         v_cos, v_sin = coefficients(charge)
-        from_cos = product(rows_of(*v_cos), cos_high[...], cos_low[...], NN)
-        from_sin = product(rows_of(*v_sin), sin_high[...], sin_low[...], NN)
-        u_c, u_s, u_0 = (a + b for a, b in zip(from_cos, from_sin))
+        rows_cos, rows_sin = rows_of(*v_cos), rows_of(*v_sin)
+        potential = []
+        for j in range(0, ranks, 2):
+            cut = slice(j * width, (j + 2) * width)
+            from_cos = product(rows_cos, cos_high[:, cut], cos_low[:, cut], NN)
+            from_sin = product(rows_sin, sin_high[:, cut], sin_low[:, cut], NN)
+            u_c, u_s, u_0 = (a + b for a, b in zip(from_cos, from_sin))
+            terms = z_cos[:, cut] * u_c + z_sin[:, cut] * u_s + u_0
+            potential += [scale * column_sum(terms[:, :width]), scale * column_sum(terms[:, width:])]
         weighted = [everywhere(bond[j : j + 1, :]) * charge[j] for j in range(ranks)]
         relaxed = []
         total = blank
         for j in range(ranks):
-            potential = scale * column_sum(
-                z_cos[:, at(j)] * u_c[:, at(j)] + z_sin[:, at(j)] * u_s[:, at(j)] + u_0[:, at(j)]
-            )
             before = weighted[(j - 1) % ranks]
             after = weighted[(j + 1) % ranks]
             lower = jnp.where(lane < 3 * width // 4, weighted[j], before)
@@ -292,7 +309,7 @@
             )
             new = (1.0 - mixing) * charge[j] - everywhere(hard[j : j + 1, :]) * (
                 everywhere(chi[j : j + 1, :])
-                + potential
+                + potential[j]
                 + everywhere(bond[j : j + 1, :]) * column_sum(near)
             )
             relaxed.append(new)

time: 27.2 us -> 27.2 us (level)
  no operation moved by 1% of the time
where the time goes in v9:
time: 27.2 us; the launch traced here: 26.9 us
  starting transfers between devices  11 us (40%)
  Pallas kernels  8.32 us (31%)
  waiting for transfers between devices  6.18 us (23%)
  between operations  0.75 us (3%)
  local copies, waits for them, and re-layouts  0.65 us (2%)
    all_to_all x1, starting transfers between devices, body(): got = lax.all_to_all(packed, 'atoms', 0, 0, tiled=True)  7.5 us
    pallas_call x1, Pallas kernels, body(): pl.pallas_call(functools.partial(bead_kernel, scale, 1.0 / atoms, beads),...  5.35 us
    all_to_all x1, waiting for transfers between devices, body(): got = lax.all_to_all(packed, 'atoms', 0, 0, tiled=True)  4.39 us
    ppermute x3, starting transfers between devices, in_group(): return lax.ppermute(x, 'atoms', pairs)  1.93 us
    ppermute x3, waiting for transfers between devices, in_group(): return lax.ppermute(x, 'atoms', pairs)  1.79 us
    ppermute x1, starting transfers between devices, body(): low = high = lax.ppermute(edges, 'beads', [(0, 1), (1, 0)])  1.58 us
    pallas_call x1, Pallas kernels, body(): pl.pallas_call(functools.partial(pack_kernel, ranks), out_shape=pltpu.VME...  1.47 us
    pallas_call x1, Pallas kernels, body(): pl.pallas_call(weight_kernel, out_shape=(shape((24, MODES), F32), shape((...  0.89 us
  transfers between devices with their start and end apart: 5, of which 2 were waited for; matrix products, arithmetic and copies ran while one was open for 0% of the time, Pallas kernels for 23%

profile of v9, /device:TPU:0, one launch (start us, length us, event | category | flops | bytes accessed | tf_op | source)
XLA Modules:
  0.0 26.9 jit_solution(4657293491986395811)
XLA Ops:
  0.6 1.5 %pack.1.after = f32[16,13,1,128]{3,2,1,0:T(1,128)} custom-call(f32[3,4,128]{2,1,0:T(4,128)} %bitcast.7, f32[4,128]{1,0:T(4,128)} %charge_hbm.1, s32[1,128]{1,0:T(1,128)} %bitcast.11, s32[8,128]{1,0:T(8,128)} %neighbors_hbm.1), custom_call_target="tpu_custom_call" | custom-call | tf_op jit(solution)/shard_map/pack/pallas_call | solution.py:436
  2.1 0.0 copy-start
  2.1 0.0 copy-start.3
  2.1 0.0 copy-start.4
  2.1 7.5 %all-to-all-start = ((f32[16,13,1,128]{3,2,1,0:T(1,128)}), f32[16,13,1,128]{3,2,1,0:T(1,128)S(1)}, u32[]{:S(2)}, u32[]{:S(2)}) async-start(f32[16,13,1,128]{3,2,1,0:T(1,128)} %pack.1.after), calls=%async_computation | async-start | bytes 212992 | tf_op jit(solution)/shard_map/all_to_all | solution.py:451
  9.7 0.0 copy-start.2
  9.7 0.0 copy-start.5
  9.7 0.0 copy-done
  9.7 0.0 copy-done.3
  9.7 0.0 copy-done.4
  9.7 0.6 %copy-done.2 = s32[128]{0:T(128)S(1)} copy-done((s32[128]{0:T(128)S(1)}, s32[128]{0:T(128)}, u32[]{:S(2)}) %copy-start.2) | copy-done | bytes 536
  10.3 0.0 copy-done.5
  10.3 0.9 %weights.1 = (f32[24,160]{1,0:T(8,128)S(1)}, f32[6,128]{1,0:T(8,128)S(1)}, f32[1,128]{1,0:T(1,128)S(1)}) custom-call(s32[3,2048]{1,0:T(4,128)S(1)} %copy-done.3, f32[1,2048]{1,0:T(1,128)S(1)} %bitcast.13, f32[3,4,128]{2,1,0:T(4,128)S(1)} %bitcast.8, s32[1,128]{1,0:T(1,128)S(1)} %bitcast.12, f32[8]{0:T(128)S(1)} %copy-done.5, f32[16,13,1,128]{3,2,1,0:T(1,128)} %pack.1.after), custom_call_target="tpu_custom_call" | custom-call | flops 1000000000 | bytes 100000 | tf_op jit(solution)/shard_map/weights/pallas_call | solution.py:453
  11.2 1.6 %collective-permute-start = (f32[6,128]{1,0:T(8,128)S(1)}, f32[6,128]{1,0:T(8,128)S(1)}, u32[]{:S(2)}, u32[]{:S(2)}) collective-permute-start(f32[6,128]{1,0:T(8,128)S(1)} %get-tuple-element.13), channel_id=1, source_target_pairs={{0,1},{1,0},{2,3},{3,2},{4,5},{5,4},{6,7},{7,6},{8,9},{9,8},{10,11... | collective-permute-start | bytes 9224 | tf_op jit(solution)/shard_map/ppermute | solution.py:467
  12.8 4.4 %all-to-all-done.got = f32[16,13,1,128]{3,2,1,0:T(1,128)S(1)} async-done(((f32[16,13,1,128]{3,2,1,0:T(1,128)}), f32[16,13,1,128]{3,2,1,0:T(1,128)S(1)}, u32[]{:S(2)}, u32[]{:S(2)}) %all-to-all-start) | async-done | bytes 106528 | tf_op jit(solution)/shard_map/all_to_all | solution.py:451
  17.2 5.3 %bead.1 = (f32[4,128]{1,0:T(4,128)S(1)}, f32[4,128]{1,0:T(4,128)S(1)}, f32[4,128]{1,0:T(4,128)S(1)}, f32[4,128]{1,0:T(4,128)S(1)}) custom-call(s32[1]{0:T(128)} %bitcast.rank_ref, f32[24,160]{1,0:T(8,128)S(1)} %get-tuple-element.15.weights_hbm, f32[16,13,1,128]{3,2,1,0:T(1,128)S(1)} %all-to-all-done.got, f32[8]{0:T(128)} %chi_hbm.1, f32[8]{0:T(128)} %hard_hbm.1, ...), custom_call_target="tpu_custom_call" | custom-call | flops 10000000000 | bytes 1000000 | tf_op jit(solution)/shard_map/bead/pallas_call | solution.py:475
  22.5 0.0 copy-start.1
  22.6 0.1 collective-permute-start.1
  22.6 0.1 collective-permute-start.2
  22.7 1.8 %collective-permute-start.3 = (f32[4,128]{1,0:T(4,128)S(1)}, f32[4,128]{1,0:T(4,128)S(1)}, u32[]{:S(2)}, u32[]{:S(2)}) collective-permute-start(f32[4,128]{1,0:T(4,128)S(1)} %get-tuple-element.19), channel_id=1, source_target_pairs={{0,6},{2,4},{4,2},{6,0},{8,14},{10,12},{12,10},{14,8},{16,22},{18,... | collective-permute-start | bytes 6152 | tf_op jit(solution)/shard_map/ppermute | solution.py:433
  24.5 0.0 collective-permute-done.low.high
  24.5 0.0 collective-permute-done.1.refs_1_
  24.5 1.8 %collective-permute-done.2.refs_2_ = f32[4,128]{1,0:T(4,128)S(1)} collective-permute-done((f32[4,128]{1,0:T(4,128)S(1)}, f32[4,128]{1,0:T(4,128)S(1)}, u32[]{:S(2)}, u32[]{:S(2)}) %collective-permute-start.2) | collective-permute-done | bytes 2080 | tf_op jit(solution)/shard_map/ppermute | solution.py:433
  26.3 0.0 collective-permute-done.3.refs_3_
  26.3 0.0 copy-done.1
  26.3 0.6 %move.1 = (f32[3,4,128]{2,1,0:T(4,128)}, f32[3,4,128]{2,1,0:T(4,128)}, f32[4,128]{1,0:T(4,128)}) custom-call(s32[1]{0:T(128)} %bitcast.rank_ref, f32[3,4,128]{2,1,0:T(4,128)S(1)} %bitcast.9, f32[3,4,128]{2,1,0:T(4,128)S(1)} %bitcast.10, f32[6,128]{1,0:T(8,128)S(1)} %collective-permute-done.low.high, f32[6,128]{1,0:T(8,128)S(1)} %collective-permute-done.low.high, ...), custom_call_target="tpu_custom_call" | custom-call | tf_op jit(solution)/shard_map/move/pallas_call | solution.py:508
Async XLA Ops:
  2.1 7.6 %copy-start = (f32[4,3,128]{2,0,1:T(4,128)S(1)}, f32[4,3,128]{2,0,1:T(4,128)}, u32[]{:S(2)}) copy-start(f32[4,3,128]{2,0,1:T(4,128)} %param.11) | copy-start | bytes 18436
  2.1 7.6 %copy-start.3 = (s32[3,2048]{1,0:T(4,128)S(1)}, s32[3,2048]{1,0:T(4,128)}, u32[]{:S(2)}) copy-start(s32[3,2048]{1,0:T(4,128)} %k_index.1) | copy-start | bytes 73732
  2.1 7.6 %copy-start.4 = (f32[2048]{0:T(1024)S(1)}, f32[2048]{0:T(1024)}, u32[]{:S(2)}) copy-start(f32[2048]{0:T(1024)} %param.17) | copy-start | bytes 24580
  2.1 15.0 %all-to-all-start = ((f32[16,13,1,128]{3,2,1,0:T(1,128)}), f32[16,13,1,128]{3,2,1,0:T(1,128)S(1)}, u32[]{:S(2)}, u32[]{:S(2)}) async-start(f32[16,13,1,128]{3,2,1,0:T(1,128)} %pack.1.after), calls=%async_computation | async-start | bytes 212992 | tf_op jit(solution)/shard_map/all_to_all | solution.py:451
  9.7 0.7 %copy-start.2 = (s32[128]{0:T(128)S(1)}, s32[128]{0:T(128)}, u32[]{:S(2)}) copy-start(s32[128]{0:T(128)} %param.14) | copy-start | bytes 1540
  9.7 0.7 %copy-start.5 = (f32[8]{0:T(128)S(1)}, f32[8]{0:T(128)}, u32[]{:S(2)}) copy-start(f32[8]{0:T(128)} %mass_table.1) | copy-start | bytes 100
  11.2 13.3 %collective-permute-start = (f32[6,128]{1,0:T(8,128)S(1)}, f32[6,128]{1,0:T(8,128)S(1)}, u32[]{:S(2)}, u32[]{:S(2)}) collective-permute-start(f32[6,128]{1,0:T(8,128)S(1)} %get-tuple-element.13), channel_id=1, source_target_pairs={{0,1},{1,0},{2,3},{3,2},{4,5},{5,4},{6,7},{7,6},{8,9},{9,8},{10,11... | collective-permute-start | bytes 9224 | tf_op jit(solution)/shard_map/ppermute | solution.py:467
  22.5 3.7 %copy-start.1 = (f32[4,3,128]{2,0,1:T(4,128)S(1)}, f32[4,3,128]{2,0,1:T(4,128)}, u32[]{:S(2)}) copy-start(f32[4,3,128]{2,0,1:T(4,128)} %param.12) | copy-start | bytes 18436
  22.6 1.9 %collective-permute-start.1 = (f32[4,128]{1,0:T(4,128)S(1)}, f32[4,128]{1,0:T(4,128)S(1)}, u32[]{:S(2)}, u32[]{:S(2)}) collective-permute-start(f32[4,128]{1,0:T(4,128)S(1)} %get-tuple-element.17), channel_id=1, source_target_pairs={{0,2},{2,0},{4,6},{6,4},{8,10},{10,8},{12,14},{14,12},{16,18},{18,... | collective-permute-start | bytes 6152 | tf_op jit(solution)/shard_map/ppermute | solution.py:433
  22.6 3.7 %collective-permute-start.2 = (f32[4,128]{1,0:T(4,128)S(1)}, f32[4,128]{1,0:T(4,128)S(1)}, u32[]{:S(2)}, u32[]{:S(2)}) collective-permute-start(f32[4,128]{1,0:T(4,128)S(1)} %get-tuple-element.18), channel_id=1, source_target_pairs={{0,4},{2,6},{4,0},{6,2},{8,12},{10,14},{12,8},{14,10},{16,20},{18,... | collective-permute-start | bytes 6152 | tf_op jit(solution)/shard_map/ppermute | solution.py:433
  22.7 3.6 %collective-permute-start.3 = (f32[4,128]{1,0:T(4,128)S(1)}, f32[4,128]{1,0:T(4,128)S(1)}, u32[]{:S(2)}, u32[]{:S(2)}) collective-permute-start(f32[4,128]{1,0:T(4,128)S(1)} %get-tuple-element.19), channel_id=1, source_target_pairs={{0,6},{2,4},{4,2},{6,0},{8,14},{10,12},{12,10},{14,8},{16,22},{18,... | collective-permute-start | bytes 6152 | tf_op jit(solution)/shard_map/ppermute | solution.py:433

commit v10 on v5

--- a/solution.py
+++ b/solution.py
@@ -323,20 +323,22 @@
     ch, cl, sh, sl = (ref[:, own] for ref in (cos_high, cos_low, sin_high, sin_low))
     zc, zs, q = z_cos[:, own], z_sin[:, own], charges[:, own]
 
-    def field(for_cos, for_sin):
-        a = product(rows_of(*for_cos), ch, cl, NN)
-        b = product(rows_of(*for_sin), sh, sl, NN)
-        return (one + two for one, two in zip(a, b))
-
-    def force(wave):
-        u_c, u_s, u_0 = field(
-            (-wave * v_sc, -wave * v_ss, -wave * v_s0), (wave * v_cc, wave * v_cs, wave * v_c0)
-        )
-        return zc * u_c + zs * u_s + u_0
-
-    along_x = force(wave_x)
-    along_y = force(wave_y)
-    u_c, u_s, _ = field((v_cc, v_cs, v_c0), (v_sc, v_ss, v_s0))
+    v_cos, v_sin = (v_cc, v_cs, v_c0), (v_sc, v_ss, v_s0)
+    for_cos, for_sin = [rows_of(*v_cos)], [rows_of(*v_sin)]
+    for wave in (wave_x, wave_y):
+        for_cos.append(rows_of(*(-wave * v for v in v_sin)))
+        for_sin.append(rows_of(*(wave * v for v in v_cos)))
+    for_cos, for_sin = jnp.concatenate(for_cos, 0), jnp.concatenate(for_sin, 0)
+    fields = sum(
+        lax.dot_general(rows, part, NN, preferred_element_type=F32)
+        for rows, part in ((for_cos, ch), (for_cos, cl), (for_sin, sh), (for_sin, sl))
+    )
+    (u_c, u_s, _), (x_c, x_s, x_0), (y_c, y_s, y_0) = (
+        (f[0:8] + f[32:40], f[8:16] + f[40:48], f[16:24] + f[24:32])
+        for f in (fields[48 * i : 48 * i + 48] for i in range(3))
+    )
+    along_x = zc * x_c + zs * x_s + x_0
+    along_y = zc * y_c + zs * y_s + y_0
     wide_multiple = jnp.broadcast_to(multiple[:, 0:1], (8, span))
     along_z = wide_multiple * (zs * u_c - zc * u_s)
     factor = (two_pi * scale) * q
@@ -441,7 +443,14 @@
         compiler_params=params(4),
         name="pack",
     )(*map(stay, (places, charges_in, kinds, neighbors, chi_table, hard_table, bond_table)))
-    gathered = [packed] + [among_groups(packed, k) for k in range(1, groups)]
+    if groups & (groups - 1) == 0:
+        known, step = {0: packed}, groups // 2
+        while step:
+            known.update({k ^ step: among_groups(x, step) for k, x in known.items()})
+            step //= 2
+        gathered = [known[k] for k in range(groups)]
+    else:
+        gathered = [packed] + [among_groups(packed, k) for k in range(1, groups)]
     sorted_blocks = pl.pallas_call(
         functools.partial(sort_kernel, beads, groups),
         out_shape=[shape((groups, 16, width), F32)] * beads,

time: 28.2 us -> 26.9 us (0.954)
  waiting for transfers between devices: 8 us -> 4.51 us
  starting transfers between devices: 11.1 us -> 13.2 us
    ppermute x3, waiting for transfers between devices: 5.58 us -> 2.08 us  [among_groups(): return lax.ppermute(x, 'atoms', pairs)]
    ppermute x3, starting transfers between devices: 5.68 us -> 7.57 us  [among_groups(): return lax.ppermute(x, 'atoms', pairs)]
  transfers between devices with their start and end apart: 10 -> 10, of which waited for: 5 -> 6; matrix products, arithmetic and copies ran while one was open for 0% -> 0% of each run, Pallas kernels for 22% -> 23%
where the time goes in v10:
time: 26.9 us; the launch traced here: 26.7 us
  starting transfers between devices  13.2 us (49%)
  Pallas kernels  7.71 us (29%)
  waiting for transfers between devices  4.51 us (17%)
  between operations  0.7 us (3%)
  local copies, waits for them, and re-layouts  0.62 us (2%)
    ppermute x3, starting transfers between devices, among_groups(): return lax.ppermute(x, 'atoms', pairs)  7.57 us
    pallas_call x1, Pallas kernels, body(): pl.pallas_call(functools.partial(bead_kernel, scale, 1.0 / atoms, beads),...  5.28 us
    ppermute x6, starting transfers between devices, in_group(): return lax.ppermute(x, 'atoms', pairs)  4.03 us
    ppermute x6, waiting for transfers between devices, in_group(): return lax.ppermute(x, 'atoms', pairs)  2.42 us
    ppermute x3, waiting for transfers between devices, among_groups(): return lax.ppermute(x, 'atoms', pairs)  2.08 us
    ppermute x1, starting transfers between devices, body(): low = high = lax.ppermute(edges, 'beads', [(0, 1), (1, 0)])  1.58 us
    pallas_call x1, Pallas kernels, body(): pl.pallas_call(pack_kernel, out_shape=shape((beads + 1, 8, width), F32),...  0.9 us
    pallas_call x1, Pallas kernels, body(): pl.pallas_call(weight_kernel, out_shape=(shape((24, MODES), F32), shape((...  0.89 us
  transfers between devices with their start and end apart: 10, of which 6 were waited for; matrix products, arithmetic and copies ran while one was open for 0% of the time, Pallas kernels for 23%

profile of v10, /device:TPU:0, one launch (start us, length us, event | category | flops | bytes accessed | tf_op | source)
XLA Modules:
  0.0 26.7 jit_solution(12320914488368192546)
XLA Ops:
  0.6 0.9 %pack.1.after.refs_0_ = f32[5,8,128]{2,1,0:T(8,128)S(1)} custom-call(f32[3,4,128]{2,1,0:T(4,128)} %bitcast.7, f32[4,128]{1,0:T(4,128)} %charge_hbm.1, s32[1,128]{1,0:T(1,128)} %bitcast.11, s32[8,128]{1,0:T(8,128)} %neighbors_hbm.1, f32[8]{0:T(128)} %chi_hbm.1, f32[8]{0:T(128)} %hard_hbm.1, f32[8]{0:T(128)} %bond_hbm.1), custom_call_target="tpu_custom_call" | custom-call | tf_op jit(solution)/shard_map/pack/pallas_call | solution.py:428
  1.5 4.1 %collective-permute-start.2 = (f32[5,8,128]{2,1,0:T(8,128)S(1)}, f32[5,8,128]{2,1,0:T(8,128)S(1)}, u32[]{:S(2)}, u32[]{:S(2)}) collective-permute-start(f32[5,8,128]{2,1,0:T(8,128)S(1)} %pack.1.after.refs_0_), channel_id=1, source_target_pairs={{0,16},{2,18},{4,20},{6,22},{8,24},{10,26},{12,28},{14,30},{16,0},... | collective-permute-start | bytes 61448 | tf_op jit(solution)/shard_map/ppermute | solution.py:422
  5.6 1.6 %collective-permute-start.1 = (f32[5,8,128]{2,1,0:T(8,128)S(1)}, f32[5,8,128]{2,1,0:T(8,128)S(1)}, u32[]{:S(2)}, u32[]{:S(2)}) collective-permute-start(f32[5,8,128]{2,1,0:T(8,128)S(1)} %pack.1.after.refs_0_), channel_id=1, source_target_pairs={{0,8},{2,10},{4,12},{6,14},{8,0},{10,2},{12,4},{14,6},{16,24},{18,... | collective-permute-start | bytes 61448 | tf_op jit(solution)/shard_map/ppermute | solution.py:422
  7.2 0.2 collective-permute-done.2.refs_2_
  7.4 1.9 %collective-permute-start.3 = (f32[5,8,128]{2,1,0:T(8,128)S(1)}, f32[5,8,128]{2,1,0:T(8,128)S(1)}, u32[]{:S(2)}, u32[]{:S(2)}) collective-permute-start(f32[5,8,128]{2,1,0:T(8,128)S(1)} %collective-permute-done.2.refs_2_), channel_id=1, source_target_pairs={{0,8},{2,10},{4,12},{6,14},{8,0},{10,2},{12,4},{14,6},{16,24},{18,... | collective-permute-start | bytes 61448 | tf_op jit(solution)/shard_map/ppermute | solution.py:422
  9.3 0.2 collective-permute-done.1.refs_1_
  9.5 1.7 %collective-permute-done.3.refs_3_ = f32[5,8,128]{2,1,0:T(8,128)S(1)} collective-permute-done((f32[5,8,128]{2,1,0:T(8,128)S(1)}, f32[5,8,128]{2,1,0:T(8,128)S(1)}, u32[]{:S(2)}, u32[]{:S(2)}) %collective-permute-start.3) | collective-permute-done | bytes 20512 | tf_op jit(solution)/shard_map/ppermute | solution.py:422
  11.2 0.0 copy-start.3
  11.2 0.0 copy-start.4
  11.2 0.0 copy-start
  11.2 0.1 collective-permute-start.4
  11.3 2.0 %collective-permute-start.5 = (f32[4,16,128]{2,1,0:T(8,128)S(1)}, f32[4,16,128]{2,1,0:T(8,128)S(1)}, u32[]{:S(2)}, u32[]{:S(2)}) collective-permute-start(f32[4,16,128]{2,1,0:T(8,128)S(1)} %get-tuple-element.22), channel_id=1, source_target_pairs={{0,4},{2,6},{4,0},{6,2},{8,12},{10,14},{12,8},{14,10},{16,20},{18,... | collective-permute-start | bytes 98312 | tf_op jit(solution)/shard_map/ppermute | solution.py:426
  13.3 0.0 copy-start.2
  13.3 0.0 copy-start.5
  13.3 0.1 collective-permute-start.6
  13.4 0.0 copy-done.3
  13.4 0.0 copy-done.4
  13.4 0.0 copy-done
  13.4 0.6 %copy-done.2 = s32[128]{0:T(128)S(1)} copy-done((s32[128]{0:T(128)S(1)}, s32[128]{0:T(128)}, u32[]{:S(2)}) %copy-start.2) | copy-done | bytes 536
  13.9 0.0 copy-done.5
  14.0 0.9 %weights.1 = (f32[24,160]{1,0:T(8,128)S(1)}, f32[6,128]{1,0:T(8,128)S(1)}, f32[1,128]{1,0:T(1,128)S(1)}) custom-call(s32[3,2048]{1,0:T(4,128)S(1)} %copy-done.3, f32[1,2048]{1,0:T(1,128)S(1)} %bitcast.13, f32[3,4,128]{2,1,0:T(4,128)S(1)} %bitcast.8, s32[1,128]{1,0:T(1,128)S(1)} %bitcast.12, f32[8]{0:T(128)S(1)} %copy-done.5, f32[5,8,128]{2,1,0:T(8,128)S(1)} %pack.1.after.refs_0_), custom_call_target="tpu_custom_call" | custom-call | flops 1000000000 | bytes 100000 | tf_op jit(solution)/shard_map/weights/pallas_call | solution.py:464
  14.9 1.6 %collective-permute-start = (f32[6,128]{1,0:T(8,128)S(1)}, f32[6,128]{1,0:T(8,128)S(1)}, u32[]{:S(2)}, u32[]{:S(2)}) collective-permute-start(f32[6,128]{1,0:T(8,128)S(1)} %get-tuple-element.17), channel_id=1, source_target_pairs={{0,1},{1,0},{2,3},{3,2},{4,5},{5,4},{6,7},{7,6},{8,9},{9,8},{10,11... | collective-permute-start | bytes 9224 | tf_op jit(solution)/shard_map/ppermute | solution.py:478
  16.4 0.0 collective-permute-done.4.refs_1_
  16.4 0.0 collective-permute-done.5.refs_2_
  16.4 0.2 collective-permute-done.6.refs_3_
  16.6 5.3 %bead.1 = (f32[4,128]{1,0:T(4,128)S(1)}, f32[4,128]{1,0:T(4,128)S(1)}, f32[4,128]{1,0:T(4,128)S(1)}, f32[4,128]{1,0:T(4,128)S(1)}) custom-call(s32[1]{0:T(128)} %bitcast.rank_ref, f32[24,160]{1,0:T(8,128)S(1)} %get-tuple-element.19.weights_hbm, f32[4,16,128]{2,1,0:T(8,128)S(1)} %get-tuple-element.20.refs_0_, ...), custom_call_target="tpu_custom_call" | custom-call | flops 10000000000 | bytes 1000000 | tf_op jit(solution)/shard_map/bead/pallas_call | solution.py:486
  21.9 0.0 copy-start.1
  21.9 0.2 collective-permute-start.7
  22.2 0.9 %collective-permute-start.8 = (f32[4,128]{1,0:T(4,128)S(1)}, f32[4,128]{1,0:T(4,128)S(1)}, u32[]{:S(2)}, u32[]{:S(2)}) collective-permute-start(f32[4,128]{1,0:T(4,128)S(1)} %get-tuple-element.26), channel_id=1, source_target_pairs={{0,4},{2,6},{4,0},{6,2},{8,12},{10,14},{12,8},{14,10},{16,20},{18,... | collective-permute-start | bytes 6152 | tf_op jit(solution)/shard_map/ppermute | solution.py:426
  23.1 0.8 %collective-permute-start.9 = (f32[4,128]{1,0:T(4,128)S(1)}, f32[4,128]{1,0:T(4,128)S(1)}, u32[]{:S(2)}, u32[]{:S(2)}) collective-permute-start(f32[4,128]{1,0:T(4,128)S(1)} %get-tuple-element.27), channel_id=1, source_target_pairs={{0,6},{2,4},{4,2},{6,0},{8,14},{10,12},{12,10},{14,8},{16,22},{18,... | collective-permute-start | bytes 6152 | tf_op jit(solution)/shard_map/ppermute | solution.py:426
  23.9 0.0 collective-permute-done.low.high
  23.9 0.0 collective-permute-done.7.refs_1_
  23.9 1.9 %collective-permute-done.8.refs_2_ = f32[4,128]{1,0:T(4,128)S(1)} collective-permute-done((f32[4,128]{1,0:T(4,128)S(1)}, f32[4,128]{1,0:T(4,128)S(1)}, u32[]{:S(2)}, u32[]{:S(2)}) %collective-permute-start.8) | collective-permute-done | bytes 2080 | tf_op jit(solution)/shard_map/ppermute | solution.py:426
  25.8 0.3 %collective-permute-done.9.refs_3_ = f32[4,128]{1,0:T(4,128)S(1)} collective-permute-done((f32[4,128]{1,0:T(4,128)S(1)}, f32[4,128]{1,0:T(4,128)S(1)}, u32[]{:S(2)}, u32[]{:S(2)}) %collective-permute-start.9) | collective-permute-done | bytes 2080 | tf_op jit(solution)/shard_map/ppermute | solution.py:426
  26.1 0.0 copy-done.1
  26.1 0.6 %move.1 = (f32[3,4,128]{2,1,0:T(4,128)}, f32[3,4,128]{2,1,0:T(4,128)}, f32[4,128]{1,0:T(4,128)}) custom-call(s32[1]{0:T(128)} %bitcast.rank_ref, f32[3,4,128]{2,1,0:T(4,128)S(1)} %bitcast.9, f32[3,4,128]{2,1,0:T(4,128)S(1)} %bitcast.10, f32[6,128]{1,0:T(8,128)S(1)} %collective-permute-done.low.high, f32[6,128]{1,0:T(8,128)S(1)} %collective-permute-done.low.high, ...), custom_call_target="tpu_custom_call" | custom-call | tf_op jit(solution)/shard_map/move/pallas_call | solution.py:512
  (1 shorter events, 0.0 us)
Async XLA Ops:
  1.5 5.9 %collective-permute-start.2 = (f32[5,8,128]{2,1,0:T(8,128)S(1)}, f32[5,8,128]{2,1,0:T(8,128)S(1)}, u32[]{:S(2)}, u32[]{:S(2)}) collective-permute-start(f32[5,8,128]{2,1,0:T(8,128)S(1)} %pack.1.after.refs_0_), channel_id=1, source_target_pairs={{0,16},{2,18},{4,20},{6,22},{8,24},{10,26},{12,28},{14,30},{16,0},... | collective-permute-start | bytes 61448 | tf_op jit(solution)/shard_map/ppermute | solution.py:422
  5.6 3.9 %collective-permute-start.1 = (f32[5,8,128]{2,1,0:T(8,128)S(1)}, f32[5,8,128]{2,1,0:T(8,128)S(1)}, u32[]{:S(2)}, u32[]{:S(2)}) collective-permute-start(f32[5,8,128]{2,1,0:T(8,128)S(1)} %pack.1.after.refs_0_), channel_id=1, source_target_pairs={{0,8},{2,10},{4,12},{6,14},{8,0},{10,2},{12,4},{14,6},{16,24},{18,... | collective-permute-start | bytes 61448 | tf_op jit(solution)/shard_map/ppermute | solution.py:422
  7.4 3.8 %collective-permute-start.3 = (f32[5,8,128]{2,1,0:T(8,128)S(1)}, f32[5,8,128]{2,1,0:T(8,128)S(1)}, u32[]{:S(2)}, u32[]{:S(2)}) collective-permute-start(f32[5,8,128]{2,1,0:T(8,128)S(1)} %collective-permute-done.2.refs_2_), channel_id=1, source_target_pairs={{0,8},{2,10},{4,12},{6,14},{8,0},{10,2},{12,4},{14,6},{16,24},{18,... | collective-permute-start | bytes 61448 | tf_op jit(solution)/shard_map/ppermute | solution.py:422
  11.2 2.2 %copy-start.3 = (s32[3,2048]{1,0:T(4,128)S(1)}, s32[3,2048]{1,0:T(4,128)}, u32[]{:S(2)}) copy-start(s32[3,2048]{1,0:T(4,128)} %k_index.1) | copy-start | bytes 73732
  11.2 2.2 %copy-start.4 = (f32[2048]{0:T(1024)S(1)}, f32[2048]{0:T(1024)}, u32[]{:S(2)}) copy-start(f32[2048]{0:T(1024)} %param.17) | copy-start | bytes 24580
  11.2 2.1 %copy-start = (f32[4,3,128]{2,0,1:T(4,128)S(1)}, f32[4,3,128]{2,0,1:T(4,128)}, u32[]{:S(2)}) copy-start(f32[4,3,128]{2,0,1:T(4,128)} %param.11) | copy-start | bytes 18436
  11.2 5.2 %collective-permute-start.4 = (f32[4,16,128]{2,1,0:T(8,128)S(1)}, f32[4,16,128]{2,1,0:T(8,128)S(1)}, u32[]{:S(2)}, u32[]{:S(2)}) collective-permute-start(f32[4,16,128]{2,1,0:T(8,128)S(1)} %get-tuple-element.21), channel_id=1, source_target_pairs={{0,2},{2,0},{4,6},{6,4},{8,10},{10,8},{12,14},{14,12},{16,18},{18,... | collective-permute-start | bytes 98312 | tf_op jit(solution)/shard_map/ppermute | solution.py:426
  11.3 5.1 %collective-permute-start.5 = (f32[4,16,128]{2,1,0:T(8,128)S(1)}, f32[4,16,128]{2,1,0:T(8,128)S(1)}, u32[]{:S(2)}, u32[]{:S(2)}) collective-permute-start(f32[4,16,128]{2,1,0:T(8,128)S(1)} %get-tuple-element.22), channel_id=1, source_target_pairs={{0,4},{2,6},{4,0},{6,2},{8,12},{10,14},{12,8},{14,10},{16,20},{18,... | collective-permute-start | bytes 98312 | tf_op jit(solution)/shard_map/ppermute | solution.py:426
  13.3 0.7 %copy-start.2 = (s32[128]{0:T(128)S(1)}, s32[128]{0:T(128)}, u32[]{:S(2)}) copy-start(s32[128]{0:T(128)} %param.14) | copy-start | bytes 1540
  13.3 0.7 %copy-start.5 = (f32[8]{0:T(128)S(1)}, f32[8]{0:T(128)}, u32[]{:S(2)}) copy-start(f32[8]{0:T(128)} %mass_table.1) | copy-start | bytes 100
  13.3 3.3 %collective-permute-start.6 = (f32[4,16,128]{2,1,0:T(8,128)S(1)}, f32[4,16,128]{2,1,0:T(8,128)S(1)}, u32[]{:S(2)}, u32[]{:S(2)}) collective-permute-start(f32[4,16,128]{2,1,0:T(8,128)S(1)} %get-tuple-element.23), channel_id=1, source_target_pairs={{0,6},{2,4},{4,2},{6,0},{8,14},{10,12},{12,10},{14,8},{16,22},{18,... | collective-permute-start | bytes 98312 | tf_op jit(solution)/shard_map/ppermute | solution.py:426
  14.9 9.0 %collective-permute-start = (f32[6,128]{1,0:T(8,128)S(1)}, f32[6,128]{1,0:T(8,128)S(1)}, u32[]{:S(2)}, u32[]{:S(2)}) collective-permute-start(f32[6,128]{1,0:T(8,128)S(1)} %get-tuple-element.17), channel_id=1, source_target_pairs={{0,1},{1,0},{2,3},{3,2},{4,5},{5,4},{6,7},{7,6},{8,9},{9,8},{10,11... | collective-permute-start | bytes 9224 | tf_op jit(solution)/shard_map/ppermute | solution.py:478
  21.9 4.2 %copy-start.1 = (f32[4,3,128]{2,0,1:T(4,128)S(1)}, f32[4,3,128]{2,0,1:T(4,128)}, u32[]{:S(2)}) copy-start(f32[4,3,128]{2,0,1:T(4,128)} %param.12) | copy-start | bytes 18436
  21.9 1.9 %collective-permute-start.7 = (f32[4,128]{1,0:T(4,128)S(1)}, f32[4,128]{1,0:T(4,128)S(1)}, u32[]{:S(2)}, u32[]{:S(2)}) collective-permute-start(f32[4,128]{1,0:T(4,128)S(1)} %get-tuple-element.25), channel_id=1, source_target_pairs={{0,2},{2,0},{4,6},{6,4},{8,10},{10,8},{12,14},{14,12},{16,18},{18,... | collective-permute-start | bytes 6152 | tf_op jit(solution)/shard_map/ppermute | solution.py:426
  22.2 3.6 %collective-permute-start.8 = (f32[4,128]{1,0:T(4,128)S(1)}, f32[4,128]{1,0:T(4,128)S(1)}, u32[]{:S(2)}, u32[]{:S(2)}) collective-permute-start(f32[4,128]{1,0:T(4,128)S(1)} %get-tuple-element.26), channel_id=1, source_target_pairs={{0,4},{2,6},{4,0},{6,2},{8,12},{10,14},{12,8},{14,10},{16,20},{18,... | collective-permute-start | bytes 6152 | tf_op jit(solution)/shard_map/ppermute | solution.py:426
  23.1 3.0 %collective-permute-start.9 = (f32[4,128]{1,0:T(4,128)S(1)}, f32[4,128]{1,0:T(4,128)S(1)}, u32[]{:S(2)}, u32[]{:S(2)}) collective-permute-start(f32[4,128]{1,0:T(4,128)S(1)} %get-tuple-element.27), channel_id=1, source_target_pairs={{0,6},{2,4},{4,2},{6,0},{8,14},{10,12},{12,10},{14,8},{16,22},{18,... | collective-permute-start | bytes 6152 | tf_op jit(solution)/shard_map/ppermute | solution.py:426

commit v11 on v10

--- a/solution.py
+++ b/solution.py
@@ -100,6 +100,7 @@
 
 
 def pack_kernel(
+    rank_ref,
     pos_hbm,
     charge_hbm,
     species_hbm,
@@ -107,16 +108,10 @@
     chi_hbm,
     hard_hbm,
     bond_hbm,
-    out,
-    pos,
-    charge,
-    species,
-    neighbors,
-    chi_table,
-    hard_table,
-    bond_table,
-    arrived,
+    *refs,
 ):
+    outs = refs[:-8]
+    pos, charge, species, neighbors, chi_table, hard_table, bond_table, arrived = refs[-8:]
     sources = (pos_hbm, charge_hbm, species_hbm, neighbors_hbm, chi_hbm, hard_hbm, bond_hbm)
     targets = (pos, charge, species, neighbors, chi_table, hard_table, bond_table)
     copies = [
@@ -130,21 +125,20 @@
     dims, beads, width = pos.shape
     chi, hard, bond = lookup((chi_table, hard_table, bond_table), species[...])
     shared = [chi, mixing / hard, bond, jnp.zeros((1, width), F32)]
-    for b in range(beads):
-        own = [pos[d, b : b + 1, :] for d in range(dims)] + [charge[b : b + 1, :]]
-        out[b] = jnp.concatenate(own + shared, 0)
-    out[beads] = neighbors[...].astype(F32)
-
-
-def sort_kernel(beads, groups, rank_ref, *refs):
-    got, outs = refs[:groups], refs[groups:]
-    me, group = rank_ref[0] % beads, rank_ref[0] // beads
-    for k in range(groups):
-        source = partner(group, -k, groups)
-        near = got[k][beads]
-        for t in range(beads):
-            outs[t][source, 0:8, :] = near
-            outs[t][source, 8:16, :] = got[k][partner(me, t, beads)]
+    near = neighbors[...].astype(F32)
+    me = rank_ref[0] % beads
+    for t in range(beads):
+        bead = pl.ds(partner(me, t, beads), 1)
+        own = [pos[d, bead, :] for d in range(dims)] + [charge[bead, :]]
+        outs[t][0:8, :] = near
+        outs[t][8:16, :] = jnp.concatenate(own + shared, 0)
+
+
+def sort_kernel(beads, rank_ref, *refs):
+    out = refs[beads]
+    me = rank_ref[0] % beads
+    for t in range(beads):
+        out[partner(me, -t, beads)] = refs[t][...]
 
 
 def weight_kernel(k_index, kernel, pos, species, mass_table, after, out, edges, pull):
@@ -183,11 +177,12 @@
     scale,
     inverse_atoms,
     beads,
+    groups,
     rank_ref,
     weights_hbm,
     *refs,
 ):
-    blocks, outs = refs[:beads], refs[beads : 2 * beads]
+    blocks, outs = refs[:groups], refs[groups : groups + beads]
     (
         got,
         cos_high,
@@ -201,15 +196,15 @@
         weights,
         mine,
         arrived,
-    ) = refs[2 * beads :]
+    ) = refs[groups + beads :]
     bring = pltpu.make_async_copy(weights_hbm, weights, arrived)
     bring.start()
     ranks, _, width = got.shape
     me = rank_ref[0] % beads
-    for t in range(beads):
-        source = partner(me, -t, beads)
-        for group in range(ranks // beads):
-            got[group * beads + source] = blocks[t][group]
+    for k in range(groups):
+        source = partner(rank_ref[0] // beads, -k, groups) * beads
+        for member in range(beads):
+            got[source + member] = blocks[k][member]
     lane = lax.broadcasted_iota(jnp.int32, (8, width), 1)
     row = lax.broadcasted_iota(jnp.int32, (8, width), 0)
     multiple = (row + 1).astype(F32)
@@ -427,9 +422,9 @@
 
     packed = pl.pallas_call(
         pack_kernel,
-        out_shape=shape((beads + 1, 8, width), F32),
-        in_specs=[HBM] * 7,
-        out_specs=VMEM,
+        out_shape=[shape((16, width), F32)] * beads,
+        in_specs=[SMEM] + [HBM] * 7,
+        out_specs=[VMEM] * beads,
         scratch_shapes=[
             pltpu.VMEM(places.shape, F32),
             pltpu.VMEM(charges_in.shape, F32),
@@ -442,24 +437,24 @@
         ],
         compiler_params=params(4),
         name="pack",
-    )(*map(stay, (places, charges_in, kinds, neighbors, chi_table, hard_table, bond_table)))
+    )(rank, *map(stay, (places, charges_in, kinds, neighbors, chi_table, hard_table, bond_table)))
+    gathered = [packed[0]] + [in_group(packed[t], t) for t in range(1, beads)]
+    together = pl.pallas_call(
+        functools.partial(sort_kernel, beads),
+        out_shape=shape((beads, 16, width), F32),
+        in_specs=[SMEM] + [VMEM] * beads,
+        out_specs=VMEM,
+        compiler_params=params(4),
+        name="sort",
+    )(rank, *gathered)
     if groups & (groups - 1) == 0:
-        known, step = {0: packed}, groups // 2
+        known, step = {0: together}, groups // 2
         while step:
             known.update({k ^ step: among_groups(x, step) for k, x in known.items()})
             step //= 2
-        gathered = [known[k] for k in range(groups)]
+        blocks = [known[k] for k in range(groups)]
     else:
-        gathered = [packed] + [among_groups(packed, k) for k in range(1, groups)]
-    sorted_blocks = pl.pallas_call(
-        functools.partial(sort_kernel, beads, groups),
-        out_shape=[shape((groups, 16, width), F32)] * beads,
-        in_specs=[SMEM] + [VMEM] * groups,
-        out_specs=[VMEM] * beads,
-        compiler_params=params(4),
-        name="sort",
-    )(rank, *gathered)
-    blocks = [sorted_blocks[0]] + [in_group(sorted_blocks[t], t) for t in range(1, beads)]
+        blocks = [together] + [among_groups(together, k) for k in range(1, groups)]
 
     weights, edges, pull = pl.pallas_call(
         weight_kernel,
@@ -473,7 +468,7 @@
         compiler_params=params(8),
         name="weights",
         cost_estimate=pl.CostEstimate(flops=10**9, bytes_accessed=10**5, transcendentals=0),
-    )(k_index, kernel[None, :], places, kinds, mass_table, packed)
+    )(k_index, kernel[None, :], places, kinds, mass_table, packed[0])
     if chain == 2:
         low = high = lax.ppermute(edges, "beads", [(0, 1), (1, 0)])
         low_at, high_at = dims, 0
@@ -484,9 +479,9 @@
         low_at, high_at = 0, 0
 
     results = pl.pallas_call(
-        functools.partial(bead_kernel, scale, 1.0 / atoms, beads),
+        functools.partial(bead_kernel, scale, 1.0 / atoms, beads, groups),
         out_shape=[shape((4, width), F32)] * beads,
-        in_specs=[SMEM, ANY] + [VMEM] * beads,
+        in_specs=[SMEM, ANY] + [VMEM] * groups,
         out_specs=[VMEM] * beads,
         scratch_shapes=[
             pltpu.VMEM((ranks, 16, width), F32),

time: 26.9 us -> 26.9 us (level)
  waiting for transfers between devices: 4.51 us -> 6.2 us
  starting transfers between devices: 13.2 us -> 12 us
  local copies, waits for them, and re-layouts: 0.62 us -> 0.03 us
    ppermute x6, waiting for transfers between devices: 2.42 us -> 4.81 us  [in_group(): return lax.ppermute(x, 'atoms', pairs)]
    ppermute x3, starting transfers between devices: 7.57 us -> 5.35 us  [among_groups(): return lax.ppermute(x, 'atoms', pairs)]
    ppermute x6, starting transfers between devices: 4.03 us -> 5.08 us  [in_group(): return lax.ppermute(x, 'atoms', pairs)]
    ppermute x3, waiting for transfers between devices: 2.08 us -> 1.38 us  [among_groups(): return lax.ppermute(x, 'atoms', pairs)]
    unnamed x12, local copies, waits for them, and re-layouts: 0.62 us -> 0.03 us
  transfers between devices with their start and end apart: 10 -> 10, of which waited for: 6 -> 5; matrix products, arithmetic and copies ran while one was open for 0% -> 0% of each run, Pallas kernels for 23% -> 23%
where the time goes in v11:
time: 26.9 us; the launch traced here: 26.7 us
  starting transfers between devices  12 us (45%)
  Pallas kernels  7.7 us (29%)
  waiting for transfers between devices  6.2 us (23%)
  between operations  0.72 us (3%)
    ppermute x3, starting transfers between devices, among_groups(): return lax.ppermute(x, 'atoms', pairs)  5.35 us
    pallas_call x1, Pallas kernels, body(): pl.pallas_call(functools.partial(bead_kernel, scale, 1.0 / atoms, beads,...  5.28 us
    ppermute x6, starting transfers between devices, in_group(): return lax.ppermute(x, 'atoms', pairs)  5.08 us
    ppermute x6, waiting for transfers between devices, in_group(): return lax.ppermute(x, 'atoms', pairs)  4.81 us
    ppermute x1, starting transfers between devices, body(): low = high = lax.ppermute(edges, 'beads', [(0, 1), (1, 0)])  1.58 us
    ppermute x3, waiting for transfers between devices, among_groups(): return lax.ppermute(x, 'atoms', pairs)  1.38 us
    pallas_call x1, Pallas kernels, body(): pl.pallas_call(pack_kernel, out_shape=[shape((16, width), F32)] * beads,...  0.9 us
    pallas_call x1, Pallas kernels, body(): pl.pallas_call(weight_kernel, out_shape=(shape((24, MODES), F32), shape((...  0.89 us
  transfers between devices with their start and end apart: 10, of which 5 were waited for; matrix products, arithmetic and copies ran while one was open for 0% of the time, Pallas kernels for 23%

profile of v11, /device:TPU:0, one launch (start us, length us, event | category | flops | bytes accessed | tf_op | source)
XLA Modules:
  0.0 26.7 jit_solution(4249455939163864049)
XLA Ops:
  0.6 0.9 %pack.1 = (f32[16,128]{1,0:T(8,128)S(1)}, f32[16,128]{1,0:T(8,128)S(1)}, f32[16,128]{1,0:T(8,128)S(1)}, f32[16,128]{1,0:T(8,128)S(1)}) custom-call(s32[1]{0:T(128)} %bitcast.rank_ref, f32[3,4,128]{2,1,0:T(4,128)} %bitcast.7, f32[4,128]{1,0:T(4,128)} %charge_hbm.1, s32[1,128]{1,0:T(1,128)} %bitcast.11, s32[8,128]{1,0:T(8,128)} %neighbors_hbm.1, f32[8]{0:T(128)} %chi_hbm.1, ...), custom_call_target="tpu_custom_call" | custom-call | tf_op jit(solution)/shard_map/pack/pallas_call | solution.py:423
  1.5 0.5 %collective-permute-start.1 = (f32[16,128]{1,0:T(8,128)S(1)}, f32[16,128]{1,0:T(8,128)S(1)}, u32[]{:S(2)}, u32[]{:S(2)}) collective-permute-start(f32[16,128]{1,0:T(8,128)S(1)} %get-tuple-element.21), channel_id=1, source_target_pairs={{0,2},{2,0},{4,6},{6,4},{8,10},{10,8},{12,14},{14,12},{16,18},{18,... | collective-permute-start | bytes 24584 | tf_op jit(solution)/shard_map/ppermute | solution.py:421
  2.1 2.6 %collective-permute-start.2 = (f32[16,128]{1,0:T(8,128)S(1)}, f32[16,128]{1,0:T(8,128)S(1)}, u32[]{:S(2)}, u32[]{:S(2)}) collective-permute-start(f32[16,128]{1,0:T(8,128)S(1)} %get-tuple-element.22), channel_id=1, source_target_pairs={{0,4},{2,6},{4,0},{6,2},{8,12},{10,14},{12,8},{14,10},{16,20},{18,... | collective-permute-start | bytes 24584 | tf_op jit(solution)/shard_map/ppermute | solution.py:421
  4.6 0.1 collective-permute-start.3
  4.7 0.0 collective-permute-done.1.refs_1_
  4.7 1.6 %collective-permute-done.2.refs_2_ = f32[16,128]{1,0:T(8,128)S(1)} collective-permute-done((f32[16,128]{1,0:T(8,128)S(1)}, f32[16,128]{1,0:T(8,128)S(1)}, u32[]{:S(2)}, u32[]{:S(2)}) %collective-permute-start.2) | collective-permute-done | bytes 8224 | tf_op jit(solution)/shard_map/ppermute | solution.py:421
  6.3 1.4 %collective-permute-done.3.refs_3_ = f32[16,128]{1,0:T(8,128)S(1)} collective-permute-done((f32[16,128]{1,0:T(8,128)S(1)}, f32[16,128]{1,0:T(8,128)S(1)}, u32[]{:S(2)}, u32[]{:S(2)}) %collective-permute-start.3) | collective-permute-done | bytes 8224 | tf_op jit(solution)/shard_map/ppermute | solution.py:421
  7.7 0.0 copy-start
  7.7 0.0 copy-start.3
  7.7 0.0 copy-start.4
  7.7 0.0 copy-start.2
  7.7 0.0 copy-start.5
  7.7 2.7 %collective-permute-start.5 = (f32[4,16,128]{2,1,0:T(8,128)S(1)}, f32[4,16,128]{2,1,0:T(8,128)S(1)}, u32[]{:S(2)}, u32[]{:S(2)}) collective-permute-start(f32[4,16,128]{2,1,0:T(8,128)S(1)} %sort.1.refs_0_), channel_id=1, source_target_pairs={{0,16},{2,18},{4,20},{6,22},{8,24},{10,26},{12,28},{14,30},{16,0},... | collective-permute-start | bytes 98312 | tf_op jit(solution)/shard_map/ppermute | solution.py:417
  10.4 1.6 %collective-permute-start.4 = (f32[4,16,128]{2,1,0:T(8,128)S(1)}, f32[4,16,128]{2,1,0:T(8,128)S(1)}, u32[]{:S(2)}, u32[]{:S(2)}) collective-permute-start(f32[4,16,128]{2,1,0:T(8,128)S(1)} %sort.1.refs_0_), channel_id=1, source_target_pairs={{0,8},{2,10},{4,12},{6,14},{8,0},{10,2},{12,4},{14,6},{16,24},{18,... | collective-permute-start | bytes 98312 | tf_op jit(solution)/shard_map/ppermute | solution.py:417
  12.0 1.1 %collective-permute-done.5.refs_2_ = f32[4,16,128]{2,1,0:T(8,128)S(1)} collective-permute-done((f32[4,16,128]{2,1,0:T(8,128)S(1)}, f32[4,16,128]{2,1,0:T(8,128)S(1)}, u32[]{:S(2)}, u32[]{:S(2)}) %collective-permute-start.5) | collective-permute-done | bytes 32800 | tf_op jit(solution)/shard_map/ppermute | solution.py:417
  13.1 1.1 %collective-permute-start.6 = (f32[4,16,128]{2,1,0:T(8,128)S(1)}, f32[4,16,128]{2,1,0:T(8,128)S(1)}, u32[]{:S(2)}, u32[]{:S(2)}) collective-permute-start(f32[4,16,128]{2,1,0:T(8,128)S(1)} %collective-permute-done.5.refs_2_), channel_id=1, source_target_pairs={{0,8},{2,10},{4,12},{6,14},{8,0},{10,2},{12,4},{14,6},{16,24},{18,... | collective-permute-start | bytes 98312 | tf_op jit(solution)/shard_map/ppermute | solution.py:417
  14.2 0.0 copy-done
  14.2 0.0 copy-done.3
  14.2 0.0 copy-done.4
  14.2 0.0 copy-done.2
  14.2 0.0 copy-done.5
  14.2 0.9 %weights.1 = (f32[24,160]{1,0:T(8,128)S(1)}, f32[6,128]{1,0:T(8,128)S(1)}, f32[1,128]{1,0:T(1,128)S(1)}) custom-call(s32[3,2048]{1,0:T(4,128)S(1)} %copy-done.3, f32[1,2048]{1,0:T(1,128)S(1)} %bitcast.13, f32[3,4,128]{2,1,0:T(4,128)S(1)} %bitcast.8, s32[1,128]{1,0:T(1,128)S(1)} %bitcast.12, f32[8]{0:T(128)S(1)} %copy-done.5, ...), custom_call_target="tpu_custom_call" | custom-call | flops 1000000000 | bytes 100000 | tf_op jit(solution)/shard_map/weights/pallas_call | solution.py:459
  15.1 1.6 %collective-permute-start = (f32[6,128]{1,0:T(8,128)S(1)}, f32[6,128]{1,0:T(8,128)S(1)}, u32[]{:S(2)}, u32[]{:S(2)}) collective-permute-start(f32[6,128]{1,0:T(8,128)S(1)} %get-tuple-element.18), channel_id=1, source_target_pairs={{0,1},{1,0},{2,3},{3,2},{4,5},{5,4},{6,7},{7,6},{8,9},{9,8},{10,11... | collective-permute-start | bytes 9224 | tf_op jit(solution)/shard_map/ppermute | solution.py:473
  16.7 0.0 collective-permute-done.4.refs_1_
  16.7 0.3 %collective-permute-done.6.refs_3_ = f32[4,16,128]{2,1,0:T(8,128)S(1)} collective-permute-done((f32[4,16,128]{2,1,0:T(8,128)S(1)}, f32[4,16,128]{2,1,0:T(8,128)S(1)}, u32[]{:S(2)}, u32[]{:S(2)}) %collective-permute-start.6) | collective-permute-done | bytes 32800 | tf_op jit(solution)/shard_map/ppermute | solution.py:417
  17.0 5.3 %bead.1 = (f32[4,128]{1,0:T(4,128)S(1)}, f32[4,128]{1,0:T(4,128)S(1)}, f32[4,128]{1,0:T(4,128)S(1)}, f32[4,128]{1,0:T(4,128)S(1)}) custom-call(s32[1]{0:T(128)} %bitcast.rank_ref, f32[24,160]{1,0:T(8,128)S(1)} %get-tuple-element.20.weights_hbm, f32[4,16,128]{2,1,0:T(8,128)S(1)} %sort.1.refs_0_, f32[4,16,128]{2,1,0:T(8,128)S(1)} %collective-permute-done.4.refs_1_, ...), custom_call_target="tpu_custom_call" | custom-call | flops 10000000000 | bytes 1000000 | tf_op jit(solution)/shard_map/bead/pallas_call | solution.py:481
  22.3 0.0 copy-start.1
  22.3 0.1 collective-permute-start.7
  22.4 0.7 %collective-permute-start.8 = (f32[4,128]{1,0:T(4,128)S(1)}, f32[4,128]{1,0:T(4,128)S(1)}, u32[]{:S(2)}, u32[]{:S(2)}) collective-permute-start(f32[4,128]{1,0:T(4,128)S(1)} %get-tuple-element.26), channel_id=1, source_target_pairs={{0,4},{2,6},{4,0},{6,2},{8,12},{10,14},{12,8},{14,10},{16,20},{18,... | collective-permute-start | bytes 6152 | tf_op jit(solution)/shard_map/ppermute | solution.py:421
  23.0 1.2 %collective-permute-start.9 = (f32[4,128]{1,0:T(4,128)S(1)}, f32[4,128]{1,0:T(4,128)S(1)}, u32[]{:S(2)}, u32[]{:S(2)}) collective-permute-start(f32[4,128]{1,0:T(4,128)S(1)} %get-tuple-element.27), channel_id=1, source_target_pairs={{0,6},{2,4},{4,2},{6,0},{8,14},{10,12},{12,10},{14,8},{16,22},{18,... | collective-permute-start | bytes 6152 | tf_op jit(solution)/shard_map/ppermute | solution.py:421
  24.2 0.0 collective-permute-done.low.high
  24.2 0.0 collective-permute-done.7.refs_1_
  24.2 1.8 %collective-permute-done.8.refs_2_ = f32[4,128]{1,0:T(4,128)S(1)} collective-permute-done((f32[4,128]{1,0:T(4,128)S(1)}, f32[4,128]{1,0:T(4,128)S(1)}, u32[]{:S(2)}, u32[]{:S(2)}) %collective-permute-start.8) | collective-permute-done | bytes 2080 | tf_op jit(solution)/shard_map/ppermute | solution.py:421
  26.0 0.0 collective-permute-done.9.refs_3_
  26.0 0.0 copy-done.1
  26.0 0.6 %move.1 = (f32[3,4,128]{2,1,0:T(4,128)}, f32[3,4,128]{2,1,0:T(4,128)}, f32[4,128]{1,0:T(4,128)}) custom-call(s32[1]{0:T(128)} %bitcast.rank_ref, f32[3,4,128]{2,1,0:T(4,128)S(1)} %bitcast.9, f32[3,4,128]{2,1,0:T(4,128)S(1)} %bitcast.10, f32[6,128]{1,0:T(8,128)S(1)} %collective-permute-done.low.high, f32[6,128]{1,0:T(8,128)S(1)} %collective-permute-done.low.high, ...), custom_call_target="tpu_custom_call" | custom-call | tf_op jit(solution)/shard_map/move/pallas_call | solution.py:507
  (1 shorter events, 0.0 us)
Async XLA Ops:
  1.5 3.2 %collective-permute-start.1 = (f32[16,128]{1,0:T(8,128)S(1)}, f32[16,128]{1,0:T(8,128)S(1)}, u32[]{:S(2)}, u32[]{:S(2)}) collective-permute-start(f32[16,128]{1,0:T(8,128)S(1)} %get-tuple-element.21), channel_id=1, source_target_pairs={{0,2},{2,0},{4,6},{6,4},{8,10},{10,8},{12,14},{14,12},{16,18},{18,... | collective-permute-start | bytes 24584 | tf_op jit(solution)/shard_map/ppermute | solution.py:421
  2.1 4.2 %collective-permute-start.2 = (f32[16,128]{1,0:T(8,128)S(1)}, f32[16,128]{1,0:T(8,128)S(1)}, u32[]{:S(2)}, u32[]{:S(2)}) collective-permute-start(f32[16,128]{1,0:T(8,128)S(1)} %get-tuple-element.22), channel_id=1, source_target_pairs={{0,4},{2,6},{4,0},{6,2},{8,12},{10,14},{12,8},{14,10},{16,20},{18,... | collective-permute-start | bytes 24584 | tf_op jit(solution)/shard_map/ppermute | solution.py:421
  4.6 3.1 %collective-permute-start.3 = (f32[16,128]{1,0:T(8,128)S(1)}, f32[16,128]{1,0:T(8,128)S(1)}, u32[]{:S(2)}, u32[]{:S(2)}) collective-permute-start(f32[16,128]{1,0:T(8,128)S(1)} %get-tuple-element.23), channel_id=1, source_target_pairs={{0,6},{2,4},{4,2},{6,0},{8,14},{10,12},{12,10},{14,8},{16,22},{18,... | collective-permute-start | bytes 24584 | tf_op jit(solution)/shard_map/ppermute | solution.py:421
  7.7 6.5 %copy-start = (f32[4,3,128]{2,0,1:T(4,128)S(1)}, f32[4,3,128]{2,0,1:T(4,128)}, u32[]{:S(2)}) copy-start(f32[4,3,128]{2,0,1:T(4,128)} %param.11) | copy-start | bytes 18436
  7.7 6.5 %copy-start.3 = (s32[3,2048]{1,0:T(4,128)S(1)}, s32[3,2048]{1,0:T(4,128)}, u32[]{:S(2)}) copy-start(s32[3,2048]{1,0:T(4,128)} %k_index.1) | copy-start | bytes 73732
  7.7 6.5 %copy-start.4 = (f32[2048]{0:T(1024)S(1)}, f32[2048]{0:T(1024)}, u32[]{:S(2)}) copy-start(f32[2048]{0:T(1024)} %param.17) | copy-start | bytes 24580
  7.7 6.5 %copy-start.2 = (s32[128]{0:T(128)S(1)}, s32[128]{0:T(128)}, u32[]{:S(2)}) copy-start(s32[128]{0:T(128)} %param.14) | copy-start | bytes 1540
  7.7 6.5 %copy-start.5 = (f32[8]{0:T(128)S(1)}, f32[8]{0:T(128)}, u32[]{:S(2)}) copy-start(f32[8]{0:T(128)} %mass_table.1) | copy-start | bytes 100
  7.7 5.3 %collective-permute-start.5 = (f32[4,16,128]{2,1,0:T(8,128)S(1)}, f32[4,16,128]{2,1,0:T(8,128)S(1)}, u32[]{:S(2)}, u32[]{:S(2)}) collective-permute-start(f32[4,16,128]{2,1,0:T(8,128)S(1)} %sort.1.refs_0_), channel_id=1, source_target_pairs={{0,16},{2,18},{4,20},{6,22},{8,24},{10,26},{12,28},{14,30},{16,0},... | collective-permute-start | bytes 98312 | tf_op jit(solution)/shard_map/ppermute | solution.py:417
  10.4 6.3 %collective-permute-start.4 = (f32[4,16,128]{2,1,0:T(8,128)S(1)}, f32[4,16,128]{2,1,0:T(8,128)S(1)}, u32[]{:S(2)}, u32[]{:S(2)}) collective-permute-start(f32[4,16,128]{2,1,0:T(8,128)S(1)} %sort.1.refs_0_), channel_id=1, source_target_pairs={{0,8},{2,10},{4,12},{6,14},{8,0},{10,2},{12,4},{14,6},{16,24},{18,... | collective-permute-start | bytes 98312 | tf_op jit(solution)/shard_map/ppermute | solution.py:417
  13.1 3.9 %collective-permute-start.6 = (f32[4,16,128]{2,1,0:T(8,128)S(1)}, f32[4,16,128]{2,1,0:T(8,128)S(1)}, u32[]{:S(2)}, u32[]{:S(2)}) collective-permute-start(f32[4,16,128]{2,1,0:T(8,128)S(1)} %collective-permute-done.5.refs_2_), channel_id=1, source_target_pairs={{0,8},{2,10},{4,12},{6,14},{8,0},{10,2},{12,4},{14,6},{16,24},{18,... | collective-permute-start | bytes 98312 | tf_op jit(solution)/shard_map/ppermute | solution.py:417
  15.1 9.1 %collective-permute-start = (f32[6,128]{1,0:T(8,128)S(1)}, f32[6,128]{1,0:T(8,128)S(1)}, u32[]{:S(2)}, u32[]{:S(2)}) collective-permute-start(f32[6,128]{1,0:T(8,128)S(1)} %get-tuple-element.18), channel_id=1, source_target_pairs={{0,1},{1,0},{2,3},{3,2},{4,5},{5,4},{6,7},{7,6},{8,9},{9,8},{10,11... | collective-permute-start | bytes 9224 | tf_op jit(solution)/shard_map/ppermute | solution.py:473
  22.3 3.8 %copy-start.1 = (f32[4,3,128]{2,0,1:T(4,128)S(1)}, f32[4,3,128]{2,0,1:T(4,128)}, u32[]{:S(2)}) copy-start(f32[4,3,128]{2,0,1:T(4,128)} %param.12) | copy-start | bytes 18436
  22.3 1.9 %collective-permute-start.7 = (f32[4,128]{1,0:T(4,128)S(1)}, f32[4,128]{1,0:T(4,128)S(1)}, u32[]{:S(2)}, u32[]{:S(2)}) collective-permute-start(f32[4,128]{1,0:T(4,128)S(1)} %get-tuple-element.25), channel_id=1, source_target_pairs={{0,2},{2,0},{4,6},{6,4},{8,10},{10,8},{12,14},{14,12},{16,18},{18,... | collective-permute-start | bytes 6152 | tf_op jit(solution)/shard_map/ppermute | solution.py:421
  22.4 3.7 %collective-permute-start.8 = (f32[4,128]{1,0:T(4,128)S(1)}, f32[4,128]{1,0:T(4,128)S(1)}, u32[]{:S(2)}, u32[]{:S(2)}) collective-permute-start(f32[4,128]{1,0:T(4,128)S(1)} %get-tuple-element.26), channel_id=1, source_target_pairs={{0,4},{2,6},{4,0},{6,2},{8,12},{10,14},{12,8},{14,10},{16,20},{18,... | collective-permute-start | bytes 6152 | tf_op jit(solution)/shard_map/ppermute | solution.py:421
  23.0 3.0 %collective-permute-start.9 = (f32[4,128]{1,0:T(4,128)S(1)}, f32[4,128]{1,0:T(4,128)S(1)}, u32[]{:S(2)}, u32[]{:S(2)}) collective-permute-start(f32[4,128]{1,0:T(4,128)S(1)} %get-tuple-element.27), channel_id=1, source_target_pairs={{0,6},{2,4},{4,2},{6,0},{8,14},{10,12},{12,10},{14,8},{16,22},{18,... | collective-permute-start | bytes 6152 | tf_op jit(solution)/shard_map/ppermute | solution.py:421
